TPU v7x, 128 devices: a whole 4x4x4 slice. The times are simulated.
128 devices in a mesh: dp: 32 (over z, x, core), tensor: 4 (over y).
Axes of the slice: x: 4, y: 4, z: 4, core: 2. Of those that a mesh axis runs over, the one named last changes fastest.
Arguments:
- acts: bfloat16 [8192, 8192], P('dp', 'tensor'), may hold values from -6 to 6
- out_grad: bfloat16 [8192, 8192], P('dp'), may hold values from -0.19921875 to 0.19921875
- basis: float32 [8192, 256], replicated, may hold values from -0.0625 to 0.0625
- moment1: float32 [4, 2048, 256], P('tensor', 'dp'), may hold values from -2 to 2
- moment2: float32 [4, 2048, 256], P('tensor', 'dp'), may hold values from 0.002 to 0.05
- weight: bfloat16 [4, 2048, 8192], P('tensor', 'dp'), may hold values from -0.0625 to 0.0625
- next_acts: bfloat16 [8192, 8192], P('dp', 'tensor'), may hold values from -6 to 6
Outputs:
- output: bfloat16 [8192, 8192], P('dp', 'tensor')
- new_weight: bfloat16 [4, 2048, 8192], P('tensor', 'dp')
- first: float32 [4, 2048, 256], P('tensor', 'dp')
- second: float32 [4, 2048, 256], P('tensor', 'dp')
All inputs are finite; a program needn't handle non-finite values.
Results may differ from a plain program's by a relative error of at most 0.018.
Values may be sent and summed in bfloat16 or wider, within the bound.
No kernel may reach another device: no remote copies, remote signals or barrier semaphores. Data moves between devices by JAX's collectives and lax.ppermute only.
A program may use at most 192 MiB of HBM per device.

v0:
```python
import jax
import jax.numpy as jnp
from jax import lax
from jax.sharding import PartitionSpec as P

beta_one = 0.9
beta_two = 0.999
adam_step = 10.0
learning_rate = 0.02
epsilon = 1e-08


def back_project(direction, basis):
    return lax.dot_general(
        direction,
        basis,
        (((1,), (1,)), ((), ())),
        precision=lax.Precision.HIGHEST,
        preferred_element_type=jnp.float32,
    )


def on_device(acts, out_grad, basis, moment1, moment2, weight, next_acts):
    columns = acts
    grad = lax.dot_general(
        columns, out_grad, (((0,), (0,)), ((), ())), preferred_element_type=jnp.float32
    )
    projected = lax.psum_scatter(
        jnp.dot(
            grad, basis, precision=lax.Precision.HIGHEST, preferred_element_type=jnp.float32
        ).astype(jnp.bfloat16),
        "dp",
        scatter_dimension=0,
        tiled=True,
    ).astype(jnp.float32)
    first = beta_one * moment1[0] + (1.0 - beta_one) * projected
    second = beta_two * moment2[0] + (1.0 - beta_two) * projected * projected
    direction = (
        first
        / (1.0 - beta_one**adam_step)
        / (jnp.sqrt(second / (1.0 - beta_two**adam_step)) + epsilon)
    )
    fresh = (weight[0].astype(jnp.float32) - learning_rate * back_project(direction, basis)).astype(
        jnp.bfloat16
    )
    columns = next_acts
    partial_sum = jnp.dot(
        columns, lax.all_gather(fresh, "dp", axis=0, tiled=True), preferred_element_type=jnp.float32
    )
    output = lax.psum_scatter(
        partial_sum.astype(jnp.bfloat16), "tensor", scatter_dimension=1, tiled=True
    )
    return (output, fresh[None], first[None], second[None])


def solution(mesh):
    placed = (
        P("dp", "tensor"),
        P("dp", None),
        P(),
        P("tensor", "dp", None),
        P("tensor", "dp", None),
        P("tensor", "dp", None),
        P("dp", "tensor"),
    )
    return jax.shard_map(
        on_device,
        mesh=mesh,
        in_specs=placed,
        out_specs=(
            P("dp", "tensor"),
            P("tensor", "dp", None),
            P("tensor", "dp", None),
            P("tensor", "dp", None),
        ),
        check_vma=False,
    )
```

profile of v0, /device:TPU:1, one launch (start us, length us, event | category | flops | bytes accessed | tf_op | source)
XLA Modules:
  0.0 371.1 jit_solution(4118389554679964805)
XLA Ops:
  7.2 0.0 copy-start
  7.2 0.0 reduce-scatter.3.cloned.1.call-start
  7.2 1.2 copy-done
  8.4 25.3 %fusion.28 = f32[2048,8192]{1,0:T(8,128)} fusion(bf16[256,2048]{1,0:T(8,128)(2,1)S(1)} %copy-done, bf16[256,8192]{1,0:T(8,128)(2,1)} %param.8), kind=kOutput, calls=%fused_computation.31 | convolution fusion | flops 8589934592 | bytes 72351744 | tf_op jit(solution)/shard_map/dot_general | solution.py:25
  33.7 0.0 copy-start.1
  33.7 0.0 copy-start.2
  33.7 0.0 copy-start.3
  33.7 58.4 %convolution_convert_fusion.1 = bf16[2048,256]{1,0:T(8,128)(2,1)} fusion(f32[2048,8192]{1,0:T(8,128)} %fusion.28, f32[8192,256]{1,0:T(8,128)} %param.9), kind=kOutput, calls=%fused_computation.5 | convolution fusion | flops 51540131840 | bytes 76546048 | tf_op jit(solution)/shard_map/dot_general | solution.py:29
  92.1 0.0 copy-start.5
  92.1 0.0 reduce-scatter.3.cloned.1.call-update
  92.1 0.2 all-gather.2.cloned.1.call-start
  92.3 79.2 %reduce-scatter.3.cloned.1.call-done = bf16[64,256]{1,0:T(8,128)(2,1)} async-done(((bf16[2048,256]{1,0:T(8,128)(2,1)}), bf16[64,256]{1,0:T(8,128)(2,1)}) %reduce-scatter.3.cloned.1.call-update) | async-done | bytes 32784 | tf_op jit(solution)/shard_map/reduce_scatter | solution.py:28
  171.5 0.0 copy-done.1
  171.5 0.0 copy-done.2
  171.5 0.0 copy-done.3
  171.5 12.3 %fusion.2 = bf16[64,8192]{1,0:T(8,128)(2,1)} fusion(f32[8192,256]{1,0:T(8,128)} %param.9, bf16[1,64,8192]{2,1,0:T(8,128)(2,1)S(1)} %copy-done.1, bf16[64,256]{1,0:T(8,128)(2,1)} %reduce-scatter.3.cloned.1.call-done, f32[1,64,256]{2,1,0:T(8,128)S(1)} %copy-done.2, f32[1,64,256]{2,1,0:T(8,128)S(1)} %copy-done.3), kind=kOutput, calls=%fused_computation.4 | convolution fusion | flops 1612906496 | bytes 10649600 | tf_op jit(solution)/shard_map/dot_general | solution.py:14
  183.8 0.0 all-gather.2.cloned.1.call-update
  183.8 0.0 copy-start.4
  183.8 0.0 reduce-scatter.5.cloned.1.call-start
  183.9 115.3 %all-gather.2.cloned.1.call-done = bf16[2048,8192]{1,0:T(8,128)(2,1)} async-done(((bf16[64,8192]{1,0:T(8,128)(2,1)}), bf16[2048,8192]{1,0:T(8,128)(2,1)}) %all-gather.2.cloned.1.call-update) | async-done | bytes 33554448 | tf_op jit(solution)/shard_map/all_gather | solution.py:48
  299.2 0.0 copy-done.5
  299.2 17.2 %fusion = bf16[256,8192]{0,1:T(8,128)(2,1)} fusion(bf16[2048,8192]{1,0:T(8,128)(2,1)} %all-gather.2.cloned.1.call-done, bf16[256,2048]{1,0:T(8,128)(2,1)S(1)} %copy-done.5), kind=kOutput, calls=%fused_computation.1 | convolution fusion | flops 8592031744 | bytes 38797312 | tf_op jit(solution)/shard_map/dot_general | solution.py:47
  316.5 0.0 reduce-scatter.5.cloned.1.call-update
  316.5 0.0 copy-done.4
  316.5 0.7 fusion.12
  317.2 45.1 %reduce-scatter.5.cloned.1.call-done = bf16[256,2048]{0,1:T(8,128)(2,1)} async-done(((bf16[256,8192]{0,1:T(8,128)(2,1)}), bf16[256,2048]{0,1:T(8,128)(2,1)}) %reduce-scatter.5.cloned.1.call-update) | async-done | bytes 1048592 | tf_op jit(solution)/shard_map/reduce_scatter | solution.py:50
  362.3 2.3 copy.11
Async XLA Ops:
  7.2 1.2 copy-start
  7.2 164.3 %reduce-scatter.3.cloned.1.call-start = ((), (), s32[]{:S(2)}) async-start(), calls=%async_computation.2 | async-start | bytes 1081344 | tf_op jit(solution)/shard_map/reduce_scatter | solution.py:28
  33.7 137.8 %copy-start.1 = (bf16[1,64,8192]{2,1,0:T(8,128)(2,1)S(1)}, bf16[1,64,8192]{2,1,0:T(8,128)(2,1)}, u32[]{:S(2)}) copy-start(bf16[1,64,8192]{2,1,0:T(8,128)(2,1)} %param.12) | copy-start | bytes 3145732
  33.7 137.8 %copy-start.2 = (f32[1,64,256]{2,1,0:T(8,128)S(1)}, f32[1,64,256]{2,1,0:T(8,128)}, u32[]{:S(2)}) copy-start(f32[1,64,256]{2,1,0:T(8,128)} %param.10) | copy-start | bytes 196612
  33.7 137.8 %copy-start.3 = (f32[1,64,256]{2,1,0:T(8,128)S(1)}, f32[1,64,256]{2,1,0:T(8,128)}, u32[]{:S(2)}) copy-start(f32[1,64,256]{2,1,0:T(8,128)} %param.11) | copy-start | bytes 196612
  92.1 207.2 %copy-start.5 = (bf16[256,2048]{1,0:T(8,128)(2,1)S(1)}, bf16[256,2048]{1,0:T(8,128)(2,1)}, u32[]{:S(2)}) copy-start(bf16[256,2048]{1,0:T(8,128)(2,1)} %param.13) | copy-start | bytes 3145732
  92.1 207.1 %all-gather.2.cloned.1.call-start = ((), (), s32[]{:S(2)}) async-start(), calls=%async_computation.3 | async-start | bytes 34603008 | tf_op jit(solution)/shard_map/all_gather | solution.py:48
  183.8 132.6 %copy-start.4 = (bf16[64,256]{1,0:T(8,128)(2,1)S(1)}, bf16[64,256]{1,0:T(8,128)(2,1)}, u32[]{:S(2)}) copy-start(bf16[64,256]{1,0:T(8,128)(2,1)} %reduce-scatter.3.cloned.1.call-done) | copy-start | bytes 98308
  183.8 178.5 %reduce-scatter.5.cloned.1.call-start = ((), (), s32[]{:S(2)}) async-start(), calls=%async_computation.4 | async-start | bytes 5242880 | tf_op jit(solution)/shard_map/reduce_scatter | solution.py:50
Sparse Core Ops, SparseCore 0:
  92.2 79.2 reduce-scatter.2
  184.0 115.2 all-gather.1
  316.6 45.6 reduce-scatter.4
where the time goes:
time: 371 us
  waiting for transfers between devices  240 us (65%)
  matrix products  113 us (30%)
  between operations  13.8 us (4%)
    all_gather x1, waiting for transfers between devices, on_device(): lax.all_gather(fresh, 'dp', axis=0, tiled=True)  115 us
    reduce_scatter x1, waiting for transfers between devices, on_device(): lax.psum_scatter(jnp.dot(grad, basis, precision=lax.Precision.HIGHEST, pr...  79.2 us
    dot_general x1, matrix products, on_device(): jnp.dot(grad, basis, precision=lax.Precision.HIGHEST, preferred_element_t...  58.4 us
    reduce_scatter x1, waiting for transfers between devices, on_device(): lax.psum_scatter(partial_sum.astype(jnp.bfloat16), 'tensor', scatter_dime...  45.1 us
    dot_general x1, matrix products, on_device(): lax.dot_general(columns, out_grad, (((0,), (0,)), ((), ())), preferred_el...  25.3 us
    dot_general x1, matrix products, on_device(): jnp.dot(columns, lax.all_gather(fresh, 'dp', axis=0, tiled=True), preferr...  17.2 us
    dot_general x1, matrix products, back_project(): lax.dot_general(direction, basis, (((1,), (1,)), ((), ())), precision=lax...  12.3 us
  transfers between devices with their start and end apart: 3, of which 3 were waited for; matrix products, arithmetic and copies ran while one was open for 0% of the time, Pallas kernels for 0%

commit v1 on v0

v1 whole, which is shorter than its diff:
```python
import functools

import jax
import jax.numpy as jnp
from jax import lax
from jax.experimental import pallas as pl
from jax.experimental.pallas import tpu as pltpu
from jax.sharding import Mesh
from jax.sharding import PartitionSpec as P

beta_one = 0.9
beta_two = 0.999
adam_step = 10.0
learning_rate = 0.02
epsilon = 1e-08

F32 = jnp.float32
BF16 = jnp.bfloat16
DP = ("z", "x", "c")
MIB = 1 << 20


def two_terms(value):
    high = value.astype(BF16)
    low = (value - high.astype(F32)).astype(BF16)
    return high, low


def dot(a, b):
    return jnp.dot(a, b, preferred_element_type=F32)


def dot_t(a, b, dims):
    return lax.dot_general(a, b, (dims, ((), ())), preferred_element_type=F32)


def project_kernel(grad_ref, basis_ref, acts_ref, out_ref, total):
    step = pl.program_id(0)
    high, low = two_terms(basis_ref[...])
    grad = grad_ref[...]
    term = dot(grad, high) + dot(grad, low)

    @pl.when(step == 0)
    def _():
        total[...] = term

    @pl.when(step > 0)
    def _():
        total[...] += term

    @pl.when(step == pl.num_programs(0) - 1)
    def _():
        high, low = two_terms(total[...])
        acts = acts_ref[...]
        out_ref[...] = (
            dot_t(acts, high, ((0,), (0,))) + dot_t(acts, low, ((0,), (0,)))
        ).astype(BF16)


def project(acts, out_grad, basis):
    steps = 8
    tokens, width = out_grad.shape
    rank = basis.shape[1]
    depth = width // steps
    return pl.pallas_call(
        project_kernel,
        grid=(steps,),
        in_specs=[
            pl.BlockSpec((tokens, depth), lambda i: (0, i)),
            pl.BlockSpec((depth, rank), lambda i: (i, 0)),
            pl.BlockSpec(acts.shape, lambda i: (0, 0)),
        ],
        out_specs=pl.BlockSpec((acts.shape[1], rank), lambda i: (0, 0)),
        out_shape=jax.ShapeDtypeStruct((acts.shape[1], rank), BF16),
        scratch_shapes=[pltpu.VMEM((tokens, rank), F32)],
        compiler_params=pltpu.CompilerParams(vmem_limit_bytes=48 * MIB),
        name="project",
    )(out_grad, basis, acts)


def fresh_kernel(direction_ref, basis_ref, weight_ref, out_ref):
    dh, dl = two_terms(direction_ref[...])
    bh, bl = two_terms(basis_ref[...])
    last = ((1,), (1,))
    change = dot_t(dh, bh, last) + dot_t(dh, bl, last) + dot_t(dl, bh, last)
    out_ref[...] = (weight_ref[...].astype(F32) - learning_rate * change).astype(BF16)


def fresh_rows(direction, basis, weight):
    rows, width = weight.shape
    block = 1024
    return pl.pallas_call(
        fresh_kernel,
        grid=(width // block,),
        in_specs=[
            pl.BlockSpec(direction.shape, lambda i: (0, 0)),
            pl.BlockSpec((block, basis.shape[1]), lambda i: (i, 0)),
            pl.BlockSpec((rows, block), lambda i: (0, i)),
        ],
        out_specs=pl.BlockSpec((rows, block), lambda i: (0, i)),
        out_shape=jax.ShapeDtypeStruct((rows, width), BF16),
        compiler_params=pltpu.CompilerParams(vmem_limit_bytes=48 * MIB),
        name="fresh_rows",
    )(direction, basis, weight)


def parts_kernel(place_ref, acts_ref, own, right, left, far_a, far_b, dir_ref, basis_ref, out_ref, rows):
    step = pl.program_id(0)
    depth = own.shape[0]
    half = depth // 2

    @pl.when(step == 0)
    def _():
        basis = basis_ref[...].astype(BF16)
        for piece, index, shift, size in (
            (own, 0, 0, depth),
            (right, 1, 0, depth),
            (left, 2, 0, depth),
            (far_a, 3, 0, half),
            (far_b, 3, half, half),
        ):
            at = pl.ds(pl.multiple_of(place_ref[index] * depth + shift, half), size)
            change = dot_t(dir_ref[at, :], basis, ((1,), (1,)))
            rows[at, :] = (piece[...].astype(F32) - learning_rate * change).astype(BF16)

    part = dot(acts_ref[...], rows[...]).astype(BF16)
    count, _, width = out_ref.shape
    for j in range(count):
        out_ref[j] = part[:, j * width : (j + 1) * width]


def parts(place, acts, pieces, direction, basis):
    blocks, tokens, depth = acts.shape
    columns = pieces[0].shape[1]
    whole = lambda a: pl.BlockSpec(a.shape, lambda i, place: (0,) * len(a.shape))
    return pl.pallas_call(
        parts_kernel,
        grid_spec=pltpu.PrefetchScalarGridSpec(
            num_scalar_prefetch=1,
            grid=(blocks,),
            in_specs=[
                pl.BlockSpec((None, tokens, depth), lambda i, place: (i, 0, 0)),
                *[whole(p) for p in pieces],
                whole(direction),
                whole(basis),
            ],
            out_specs=pl.BlockSpec((None, 4, tokens, columns // 4), lambda i, place: (i, 0, 0, 0)),
            scratch_shapes=[pltpu.VMEM((depth, columns), BF16)],
        ),
        out_shape=jax.ShapeDtypeStruct((blocks, 4, tokens, columns // 4), BF16),
        compiler_params=pltpu.CompilerParams(vmem_limit_bytes=56 * MIB),
        name="parts",
    )(place, acts, *pieces, direction, basis)


def shift(value, axis, by):
    return lax.ppermute(value, axis, [(i, (i + by) % 4) for i in range(4)])


def on_device(acts, out_grad, basis, moment1, moment2, weight, next_acts):
    z, x, c = lax.axis_index("z"), lax.axis_index("x"), lax.axis_index("c")
    old = weight[0]
    own = old.reshape(64, 4, 8, 256).transpose(2, 0, 1, 3).reshape(8, 64, 1024)
    own = lax.all_to_all(own, ("x", "c"), 0, 0).reshape(512, 1024)
    right = shift(own, "z", 1)
    left = shift(own, "z", -1)
    far_a = shift(right[:256], "z", 1)
    far_b = shift(left[256:], "z", -1)
    place = jnp.stack([z, (z + 3) % 4, (z + 1) % 4, (z + 2) % 4]).astype(jnp.int32)

    columns = lax.all_gather(next_acts, ("x", "c"), axis=0, tiled=False)

    projected = project(acts, out_grad, basis)
    projected = lax.all_to_all(projected.reshape(32, 64, 256), DP, 0, 0)
    projected = jnp.sum(projected.astype(F32), axis=0)
    first = beta_one * moment1[0] + (1.0 - beta_one) * projected
    second = beta_two * moment2[0] + (1.0 - beta_two) * projected * projected
    direction = (
        first
        / (1.0 - beta_one**adam_step)
        / (jnp.sqrt(second / (1.0 - beta_two**adam_step)) + epsilon)
    )
    sent = jnp.broadcast_to(direction.astype(BF16)[None], (32, 64, 256))
    directions = lax.all_to_all(sent, DP, 0, 0).reshape(2048, 256)
    fresh = fresh_rows(direction, basis, old)

    basis_rows = lax.dynamic_index_in_dim(
        basis.reshape(4, 8, 256, 256), 2 * x + c, axis=1, keepdims=False
    ).reshape(1024, 256)
    part = parts(place, columns, (own, right, left, far_a, far_b), directions, basis_rows)
    part = lax.all_to_all(part.reshape(32, 256, 256), ("x", "c", "y"), 0, 0)
    total = jnp.sum(part.reshape(8, 4, 256, 256).astype(F32), axis=1).astype(BF16)
    output = total.transpose(1, 0, 2).reshape(256, 2048)
    return (output, fresh[None], first[None], second[None])


def solution(mesh):
    cube = Mesh(mesh.devices.reshape(4, 4, 2, 4), ("z", "x", "c", "y"))
    placed = (
        P(DP, "y"),
        P(DP, None),
        P(),
        P("y", DP, None),
        P("y", DP, None),
        P("y", DP, None),
        P(DP, "y"),
    )
    return jax.shard_map(
        on_device,
        mesh=cube,
        in_specs=placed,
        out_specs=(
            P(DP, "y"),
            P("y", DP, None),
            P("y", DP, None),
            P("y", DP, None),
        ),
        check_vma=False,
    )
```

time: 371 us -> 195 us (0.53)
  waiting for transfers between devices: 240 us -> 93.2 us
  matrix products: 113 us -> 0 us
  Pallas kernels: 0 us -> 35.9 us
  starting transfers between devices: 0.3 us -> 33.8 us
  local copies, waits for them, and re-layouts: 3.46 us -> 11.7 us
    reduce_scatter x2 -> x0, waiting for transfers between devices: 124 us -> none  [the longest x1 79.2 us: on_device(): lax.psum_scatter(jnp.dot(grad, basis, precision=lax.Precision.HIGHEST, pr...]
    all_gather x1, waiting for transfers between devices: 115 us -> 0.01 us  [on_device(): columns = lax.all_gather(next_acts, ('x', 'c'), axis=0, tiled=False)]
    dot_general x4 -> x0, matrix products: 113 us -> none  [the longest x1 58.4 us: on_device(): jnp.dot(grad, basis, precision=lax.Precision.HIGHEST, preferred_element_t...]
    all_to_all x0 -> x4, waiting for transfers between devices: none -> 80.6 us  [the longest x1 41.5 us: on_device(): part = lax.all_to_all(part.reshape(32, 256, 256), ('x', 'c', 'y'), 0, 0)]
    pallas_call x0 -> x3, Pallas kernels: none -> 35.9 us  [the longest x1 16.6 us: parts(): pl.pallas_call(parts_kernel, grid_spec=pltpu.PrefetchScalarGridSpec(num_s...]
    all_to_all x0 -> x4, starting transfers between devices: none -> 28.3 us  [the longest x1 8.42 us: on_device(): projected = lax.all_to_all(projected.reshape(32, 64, 256), DP, 0, 0)]
    ppermute x0 -> x4, waiting for transfers between devices: none -> 11.9 us  [shift(): return lax.ppermute(value, axis, [(i, (i + by) % 4) for i in range(4)])]
    ppermute x0 -> x4, starting transfers between devices: none -> 5.47 us  [shift(): return lax.ppermute(value, axis, [(i, (i + by) % 4) for i in range(4)])]
  transfers between devices with their start and end apart: 3 -> 9, of which waited for: 3 -> 6; matrix products, arithmetic and copies ran while one was open for 0% -> 6% of each run, Pallas kernels for 0% -> 10%
where the time goes in v1:
time: 195 us; the launch traced here: 193 us
  waiting for transfers between devices  93.2 us (48%)
  Pallas kernels  35.9 us (18%)
  starting transfers between devices  33.8 us (17%)
  between operations  14.1 us (7%)
  local copies, waits for them, and re-layouts  11.7 us (6%)
  other arithmetic  4.33 us (2%)
    all_to_all x1, waiting for transfers between devices, on_device(): part = lax.all_to_all(part.reshape(32, 256, 256), ('x', 'c', 'y'), 0, 0)  41.5 us
    all_to_all x1, waiting for transfers between devices, on_device(): projected = lax.all_to_all(projected.reshape(32, 64, 256), DP, 0, 0)  23.6 us
    pallas_call x1, Pallas kernels, parts(): pl.pallas_call(parts_kernel, grid_spec=pltpu.PrefetchScalarGridSpec(num_s...  16.6 us
    ppermute x4, waiting for transfers between devices, shift(): return lax.ppermute(value, axis, [(i, (i + by) % 4) for i in range(4)])  11.9 us
    pallas_call x1, Pallas kernels, project(): pl.pallas_call(project_kernel, grid=(steps,), in_specs=[pl.BlockSpec((tok...  10.3 us
    all_to_all x1, waiting for transfers between devices, on_device(): own = lax.all_to_all(own, ('x', 'c'), 0, 0).reshape(512, 1024)  9.18 us
    pallas_call x1, Pallas kernels, fresh_rows(): pl.pallas_call(fresh_kernel, grid=(width // block,), in_specs=[pl.BlockSp...  8.97 us
    all_to_all x1, starting transfers between devices, on_device(): projected = lax.all_to_all(projected.reshape(32, 64, 256), DP, 0, 0)  8.42 us
  transfers between devices with their start and end apart: 9, of which 6 were waited for; matrix products, arithmetic and copies ran while one was open for 6% of the time, Pallas kernels for 10%

profile of v1, /device:TPU:1, one launch (start us, length us, event | category | flops | bytes accessed | tf_op | source)
XLA Modules:
  0.0 193.1 jit_solution(11600241407266304099)
XLA Ops:
  7.2 0.0 all-gather.3.cloned.1.call-start
  7.2 0.7 all-gather.3.cloned.1.call-update
  7.9 0.0 copy-start.1
  7.9 1.6 copy.20
  9.5 0.4 copy.15
  9.9 1.5 reshape.58
  11.4 5.8 %all-to-all-start = ((bf16[8,64,1024]{2,1,0:T(8,128)(2,1)}), bf16[8,64,1024]{2,1,0:T(8,128)(2,1)S(1)}, u32[]{:S(2)}, u32[]{:S(2)}) async-start(bf16[8,64,1024]{2,1,0:T(8,128)(2,1)} %reshape.58), calls=%async_computation | async-start | bytes 2097152 | tf_op jit(solution)/shard_map/all_to_all | solution.py:164
  17.2 0.0 copy-done.1
  17.3 0.0 copy-start.5
  17.3 0.0 copy-start.6
  17.3 10.3 %project.1 = bf16[2048,256]{1,0:T(8,128)(2,1)} custom-call(bf16[256,8192]{1,0:T(8,128)(2,1)} %grad_ref.1, f32[8192,256]{1,0:T(8,128)} %basis_ref.3, bf16[256,2048]{1,0:T(8,128)(2,1)S(1)} %copy-done.1), custom_call_target="tpu_custom_call" | custom-call | tf_op jit(solution)/shard_map/project/pallas_call | solution.py:65
  27.6 9.2 %all-to-all-done = bf16[8,64,1024]{2,1,0:T(8,128)(2,1)S(1)} async-done(((bf16[8,64,1024]{2,1,0:T(8,128)(2,1)}), bf16[8,64,1024]{2,1,0:T(8,128)(2,1)S(1)}, u32[]{:S(2)}, u32[]{:S(2)}) %all-to-all-start) | async-done | bytes 1048608 | tf_op jit(solution)/shard_map/all_to_all | solution.py:164
  36.8 0.0 copy-start.2
  36.8 8.4 %all-to-all-start.1 = ((bf16[32,64,256]{2,1,0:T(8,128)(2,1)}), bf16[32,64,256]{2,1,0:T(8,128)(2,1)S(1)}, u32[]{:S(2)}, u32[]{:S(2)}) async-start(bf16[32,64,256]{2,1,0:T(8,128)(2,1)} %bitcast.7), calls=%async_computation.1 | async-start | bytes 2097152 | tf_op jit(solution)/shard_map/all_to_all | solution.py:174
  45.2 1.5 collective-permute-start
  46.7 1.3 collective-permute-start.1
  48.0 23.6 %all-to-all-done.1 = bf16[32,64,256]{2,1,0:T(8,128)(2,1)S(1)} async-done(((bf16[32,64,256]{2,1,0:T(8,128)(2,1)}), bf16[32,64,256]{2,1,0:T(8,128)(2,1)S(1)}, u32[]{:S(2)}, u32[]{:S(2)}) %all-to-all-start.1) | async-done | bytes 1048608 | tf_op jit(solution)/shard_map/all_to_all | solution.py:174
  71.6 0.2 convert_reduce_fusion
  71.8 0.0 copy-done.5
  71.8 0.0 copy-done.6
  71.8 0.7 fusion.8
  72.5 1.2 broadcast_in_dim.14
  73.6 6.2 %all-to-all-start.2 = ((bf16[32,64,256]{2,1,0:T(8,128)(2,1)}), bf16[32,64,256]{2,1,0:T(8,128)(2,1)S(1)}, u32[]{:S(2)}, u32[]{:S(2)}) async-start(bf16[32,64,256]{2,1,0:T(8,128)(2,1)} %broadcast_in_dim.14), calls=%async_computation.2 | async-start | bytes 2097152 | tf_op jit(solution)/shard_map/all_to_all | solution.py:184
  79.9 2.5 %collective-permute-done.right = bf16[512,1024]{1,0:T(8,128)(2,1)S(1)} collective-permute-done((bf16[512,1024]{1,0:T(8,128)(2,1)S(1)}, bf16[512,1024]{1,0:T(8,128)(2,1)S(1)}, u32[]{:S(2)}, u32[]{:S(2)}) %collective-permute-start) | collective-permute-done | bytes 1048608 | tf_op jit(solution)/shard_map/ppermute | solution.py:157
  82.4 0.0 copy-start.4
  82.4 0.9 slice.8
  83.3 0.0 collective-permute-start.2
  83.3 0.0 collective-permute-done.1.left
  83.3 1.9 slice.9
  85.2 0.0 copy-done.2
  85.2 2.7 %collective-permute-start.3 = (bf16[256,1024]{1,0:T(8,128)(2,1)}, bf16[256,1024]{1,0:T(8,128)(2,1)}, u32[]{:S(2)}, u32[]{:S(2)}) collective-permute-start(bf16[256,1024]{1,0:T(8,128)(2,1)} %slice.9), channel_id=1, source_target_pairs={{0,96},{32,0},{64,32},{96,64},{1,97},{33,1},{65,33},{97,65},{2,98}... | collective-permute-start | bytes 1572872 | tf_op jit(solution)/shard_map/ppermute | solution.py:157
  87.9 0.7 pad_add_fusion.place_ref
  88.5 2.3 %constant_dynamic-slice_fusion = f32[4,1,256,256]{3,2,1,0:T(8,128)} fusion(f32[4,8,256,256]{3,2,1,0:T(8,128)} %bitcast.44, s32[]{:T(128)S(6)} %select_n.22), kind=kLoop, calls=%fused_computation.17 | loop fusion | bytes 2097156 | tf_op jit(solution)/shard_map/jit(dynamic_index_in_dim)/dynamic_slice | solution.py:187
  90.8 6.3 %all-to-all-done.2 = bf16[32,64,256]{2,1,0:T(8,128)(2,1)S(1)} async-done(((bf16[32,64,256]{2,1,0:T(8,128)(2,1)}), bf16[32,64,256]{2,1,0:T(8,128)(2,1)S(1)}, u32[]{:S(2)}, u32[]{:S(2)}) %all-to-all-start.2) | async-done | bytes 1048608 | tf_op jit(solution)/shard_map/all_to_all | solution.py:184
  97.2 0.0 copy-start.3
  97.2 9.4 %collective-permute-done.2.far_a = bf16[256,1024]{1,0:T(8,128)(2,1)} collective-permute-done((bf16[256,1024]{1,0:T(8,128)(2,1)}, bf16[256,1024]{1,0:T(8,128)(2,1)}, u32[]{:S(2)}, u32[]{:S(2)}) %collective-permute-start.2) | collective-permute-done | bytes 524320 | tf_op jit(solution)/shard_map/ppermute | solution.py:157
  106.5 0.0 collective-permute-done.3.far_b
  106.5 0.0 copy-done.4
  106.5 0.0 copy-done.3
  106.5 16.6 %parts.1 = bf16[8,4,256,256]{3,2,1,0:T(8,128)(2,1)} custom-call(s32[4]{0:T(128)} %pad_add_fusion.place_ref, bf16[8,256,2048]{2,1,0:T(8,128)(2,1)} %bitcast.46, bf16[512,1024]{1,0:T(8,128)(2,1)} %bitcast.53, bf16[512,1024]{1,0:T(8,128)(2,1)} %copy-done.4, bf16[512,1024]{1,0:T(8,128)(2,1)} %collective-permute-done.1.left, ...), custom_call_target="tpu_custom_call" | custom-call | tf_op jit(solution)/shard_map/parts/pallas_call | solution.py:136
  123.1 7.8 %all-to-all-start.3 = ((bf16[32,256,256]{2,1,0:T(8,128)(2,1)}), bf16[32,256,256]{2,1,0:T(8,128)(2,1)}, u32[]{:S(2)}, u32[]{:S(2)}) async-start(bf16[32,256,256]{2,1,0:T(8,128)(2,1)} %bitcast.45), calls=%async_computation.3 | async-start | bytes 8388608 | tf_op jit(solution)/shard_map/all_to_all | solution.py:191
  130.9 0.1 fusion.5.direction_ref
  131.0 0.0 copy-done
  131.0 9.0 %fresh_rows.1 = bf16[64,8192]{1,0:T(8,128)(2,1)} custom-call(f32[64,256]{1,0:T(8,128)S(1)} %fusion.5.direction_ref, f32[8192,256]{1,0:T(8,128)} %basis_ref.3, bf16[64,8192]{1,0:T(8,128)(2,1)S(1)} %bitcast.43), custom_call_target="tpu_custom_call" | custom-call | tf_op jit(solution)/shard_map/fresh_rows/pallas_call | solution.py:92
  140.0 41.5 %all-to-all-done.3 = bf16[32,256,256]{2,1,0:T(8,128)(2,1)} async-done(((bf16[32,256,256]{2,1,0:T(8,128)(2,1)}), bf16[32,256,256]{2,1,0:T(8,128)(2,1)}, u32[]{:S(2)}, u32[]{:S(2)}) %all-to-all-start.3) | async-done | bytes 4194336 | tf_op jit(solution)/shard_map/all_to_all | solution.py:191
  181.5 2.8 %bitcast_reduce_fusion = bf16[8,256,256]{2,1,0:T(8,128)(2,1)S(1)} fusion(bf16[32,256,256]{2,1,0:T(8,128)(2,1)} %all-to-all-done.3), kind=kLoop, calls=%fused_computation | loop fusion | flops 1572864 | bytes 5242880 | tf_op jit(solution)/shard_map/reduce_sum | solution.py:192
  184.3 0.5 copy.17
  184.8 1.4 copy.18
  (2 shorter events, 0.0 us)
Async XLA Ops:
  7.2 99.4 %all-gather.3.cloned.1.call-start = ((), (), s32[]{:S(2)}) async-start(), calls=%async_computation.4 | async-start | bytes 9437184 | tf_op jit(solution)/shard_map/all_gather | solution.py:171
  7.9 9.4 %copy-start.1 = (bf16[256,2048]{1,0:T(8,128)(2,1)S(1)}, bf16[256,2048]{1,0:T(8,128)(2,1)}, u32[]{:S(2)}) copy-start(bf16[256,2048]{1,0:T(8,128)(2,1)} %acts_ref.1) | copy-start | bytes 3145732
  11.4 25.3 %all-to-all-start = ((bf16[8,64,1024]{2,1,0:T(8,128)(2,1)}), bf16[8,64,1024]{2,1,0:T(8,128)(2,1)S(1)}, u32[]{:S(2)}, u32[]{:S(2)}) async-start(bf16[8,64,1024]{2,1,0:T(8,128)(2,1)} %reshape.58), calls=%async_computation | async-start | bytes 2097152 | tf_op jit(solution)/shard_map/all_to_all | solution.py:164
  17.3 54.5 %copy-start.5 = (f32[1,64,256]{2,1,0:T(8,128)S(1)}, f32[1,64,256]{2,1,0:T(8,128)}, u32[]{:S(2)}) copy-start(f32[1,64,256]{2,1,0:T(8,128)} %param.10) | copy-start | bytes 196612
  17.3 54.5 %copy-start.6 = (f32[1,64,256]{2,1,0:T(8,128)S(1)}, f32[1,64,256]{2,1,0:T(8,128)}, u32[]{:S(2)}) copy-start(f32[1,64,256]{2,1,0:T(8,128)} %param.11) | copy-start | bytes 196612
  36.8 48.4 %copy-start.2 = (bf16[8,64,1024]{2,1,0:T(8,128)(2,1)}, bf16[8,64,1024]{2,1,0:T(8,128)(2,1)S(1)}, u32[]{:S(2)}) copy-start(bf16[8,64,1024]{2,1,0:T(8,128)(2,1)S(1)} %all-to-all-done) | copy-start | bytes 3145732
  36.8 34.8 %all-to-all-start.1 = ((bf16[32,64,256]{2,1,0:T(8,128)(2,1)}), bf16[32,64,256]{2,1,0:T(8,128)(2,1)S(1)}, u32[]{:S(2)}, u32[]{:S(2)}) async-start(bf16[32,64,256]{2,1,0:T(8,128)(2,1)} %bitcast.7), calls=%async_computation.1 | async-start | bytes 2097152 | tf_op jit(solution)/shard_map/all_to_all | solution.py:174
  45.2 37.2 %collective-permute-start = (bf16[512,1024]{1,0:T(8,128)(2,1)S(1)}, bf16[512,1024]{1,0:T(8,128)(2,1)S(1)}, u32[]{:S(2)}, u32[]{:S(2)}) collective-permute-start(bf16[512,1024]{1,0:T(8,128)(2,1)S(1)} %bitcast.51), channel_id=1, source_target_pairs={{0,32},{32,64},{64,96},{96,0},{1,33},{33,65},{65,97},{97,1},{2,34}... | collective-permute-start | bytes 3145736 | tf_op jit(solution)/shard_map/ppermute | solution.py:157
  46.7 36.7 %collective-permute-start.1 = (bf16[512,1024]{1,0:T(8,128)(2,1)S(1)}, bf16[512,1024]{1,0:T(8,128)(2,1)}, u32[]{:S(2)}, u32[]{:S(2)}) collective-permute-start(bf16[512,1024]{1,0:T(8,128)(2,1)S(1)} %bitcast.52), channel_id=1, source_target_pairs={{0,96},{32,0},{64,32},{96,64},{1,97},{33,1},{65,33},{97,65},{2,98}... | collective-permute-start | bytes 3145736 | tf_op jit(solution)/shard_map/ppermute | solution.py:157
  73.6 23.5 %all-to-all-start.2 = ((bf16[32,64,256]{2,1,0:T(8,128)(2,1)}), bf16[32,64,256]{2,1,0:T(8,128)(2,1)S(1)}, u32[]{:S(2)}, u32[]{:S(2)}) async-start(bf16[32,64,256]{2,1,0:T(8,128)(2,1)} %broadcast_in_dim.14), calls=%async_computation.2 | async-start | bytes 2097152 | tf_op jit(solution)/shard_map/all_to_all | solution.py:184
  82.4 24.1 %copy-start.4 = (bf16[512,1024]{1,0:T(8,128)(2,1)}, bf16[512,1024]{1,0:T(8,128)(2,1)S(1)}, u32[]{:S(2)}) copy-start(bf16[512,1024]{1,0:T(8,128)(2,1)S(1)} %collective-permute-done.right) | copy-start | bytes 3145732
  83.3 23.2 %collective-permute-start.2 = (bf16[256,1024]{1,0:T(8,128)(2,1)}, bf16[256,1024]{1,0:T(8,128)(2,1)}, u32[]{:S(2)}, u32[]{:S(2)}) collective-permute-start(bf16[256,1024]{1,0:T(8,128)(2,1)} %slice.8), channel_id=1, source_target_pairs={{0,32},{32,64},{64,96},{96,0},{1,33},{33,65},{65,97},{97,1},{2,34}... | collective-permute-start | bytes 1572872 | tf_op jit(solution)/shard_map/ppermute | solution.py:157
  85.2 21.3 %collective-permute-start.3 = (bf16[256,1024]{1,0:T(8,128)(2,1)}, bf16[256,1024]{1,0:T(8,128)(2,1)}, u32[]{:S(2)}, u32[]{:S(2)}) collective-permute-start(bf16[256,1024]{1,0:T(8,128)(2,1)} %slice.9), channel_id=1, source_target_pairs={{0,96},{32,0},{64,32},{96,64},{1,97},{33,1},{65,33},{97,65},{2,98}... | collective-permute-start | bytes 1572872 | tf_op jit(solution)/shard_map/ppermute | solution.py:157
  97.2 9.4 %copy-start.3 = (bf16[32,64,256]{2,1,0:T(8,128)(2,1)}, bf16[32,64,256]{2,1,0:T(8,128)(2,1)S(1)}, u32[]{:S(2)}) copy-start(bf16[32,64,256]{2,1,0:T(8,128)(2,1)S(1)} %all-to-all-done.2) | copy-start | bytes 3145732
  123.1 7.9 %copy-start = (bf16[1,64,8192]{2,1,0:T(8,128)(2,1)S(1)}, bf16[1,64,8192]{2,1,0:T(8,128)(2,1)}, u32[]{:S(2)}) copy-start(bf16[1,64,8192]{2,1,0:T(8,128)(2,1)} %param.12) | copy-start | bytes 3145732
  123.1 58.4 %all-to-all-start.3 = ((bf16[32,256,256]{2,1,0:T(8,128)(2,1)}), bf16[32,256,256]{2,1,0:T(8,128)(2,1)}, u32[]{:S(2)}, u32[]{:S(2)}) async-start(bf16[32,256,256]{2,1,0:T(8,128)(2,1)} %bitcast.45), calls=%async_computation.3 | async-start | bytes 8388608 | tf_op jit(solution)/shard_map/all_to_all | solution.py:191
Sparse Core Ops, SparseCore 0:
  9.7 69.6 all-gather.2

commit v2 on v1

v2 whole, which is shorter than its diff:
```python
import functools

import jax
import jax.numpy as jnp
from jax import lax
from jax.experimental import pallas as pl
from jax.experimental.pallas import tpu as pltpu
from jax.sharding import Mesh
from jax.sharding import PartitionSpec as P

beta_one = 0.9
beta_two = 0.999
adam_step = 10.0
learning_rate = 0.02
epsilon = 1e-08

F32 = jnp.float32
BF16 = jnp.bfloat16
DP = ("z", "x", "c")
MIB = 1 << 20


def two_terms(value):
    high = value.astype(BF16)
    low = (value - high.astype(F32)).astype(BF16)
    return high, low


def dot(a, b):
    return jnp.dot(a, b, preferred_element_type=F32)


def dot_t(a, b, dims):
    return lax.dot_general(a, b, (dims, ((), ())), preferred_element_type=F32)


def project_kernel(core_ref, grad_ref, basis_ref, acts_ref, keep_ref, give_ref, total):
    step = pl.program_id(0)
    high, low = two_terms(basis_ref[...])
    grad = grad_ref[...]
    term = dot(grad, high) + dot(grad, low)

    @pl.when(step == 0)
    def _():
        total[...] = term

    @pl.when(step > 0)
    def _():
        total[...] += term

    @pl.when(step == pl.num_programs(0) - 1)
    def _():
        high, low = two_terms(total[...])
        acts = acts_ref[...]
        term = dot_t(acts, high, ((0,), (0,))) + dot_t(acts, low, ((0,), (0,)))
        term = term.reshape(16, 2, 64, term.shape[-1])
        mine = core_ref[0] == 0
        keep_ref[...] = jnp.where(mine, term[:, 0], term[:, 1])
        give_ref[...] = jnp.where(mine, term[:, 1], term[:, 0]).astype(BF16)


def project(core, acts, out_grad, basis):
    steps = 8
    tokens, width = out_grad.shape
    rank = basis.shape[1]
    depth = width // steps
    return pl.pallas_call(
        project_kernel,
        grid_spec=pltpu.PrefetchScalarGridSpec(
            num_scalar_prefetch=1,
            grid=(steps,),
            in_specs=[
                pl.BlockSpec((tokens, depth), lambda i, core: (0, i)),
                pl.BlockSpec((depth, rank), lambda i, core: (i, 0)),
                pl.BlockSpec(acts.shape, lambda i, core: (0, 0)),
            ],
            out_specs=[pl.BlockSpec((16, 64, rank), lambda i, core: (0, 0, 0))] * 2,
            scratch_shapes=[pltpu.VMEM((tokens, rank), F32)],
        ),
        out_shape=[
            jax.ShapeDtypeStruct((16, 64, rank), F32),
            jax.ShapeDtypeStruct((16, 64, rank), BF16),
        ],
        compiler_params=pltpu.CompilerParams(vmem_limit_bytes=48 * MIB),
        name="project",
    )(core, out_grad, basis, acts)


ORDER = (2, 1, 3, 0)


def exchange_order_kernel(order, y_ref, weight_ref, out_ref):
    for i, d in enumerate(order):
        j = lax.rem(y_ref[0] + d, 4)
        for k in range(8):
            column = pl.multiple_of((j * 8 + k) * 256, 256)
            out_ref[k, :, i * 256 : (i + 1) * 256] = weight_ref[:, pl.ds(column, 256)]


def exchange_order(order, y, weight):
    rows = weight.shape[0]
    return pl.pallas_call(
        functools.partial(exchange_order_kernel, order),
        in_specs=[pl.BlockSpec(memory_space=pltpu.SMEM), pl.BlockSpec(memory_space=pltpu.VMEM)],
        out_shape=jax.ShapeDtypeStruct((8, rows, 256 * len(order)), BF16),
        compiler_params=pltpu.CompilerParams(vmem_limit_bytes=16 * MIB),
        name="exchange_order",
    )(y, weight)


def fresh_kernel(direction_ref, basis_ref, weight_ref, out_ref):
    dh, dl = two_terms(direction_ref[...])
    both = dot_t(jnp.concatenate([dh, dl], axis=0), basis_ref[...].astype(BF16), ((1,), (1,)))
    change = both[: dh.shape[0]] + both[dh.shape[0] :]
    out_ref[...] = (weight_ref[...].astype(F32) - learning_rate * change).astype(BF16)


def fresh_rows(direction, basis, weight):
    rows, width = weight.shape
    block = 2048
    return pl.pallas_call(
        fresh_kernel,
        grid=(width // block,),
        in_specs=[
            pl.BlockSpec(direction.shape, lambda i: (0, 0)),
            pl.BlockSpec((block, basis.shape[1]), lambda i: (i, 0)),
            pl.BlockSpec((rows, block), lambda i: (0, i)),
        ],
        out_specs=pl.BlockSpec((rows, block), lambda i: (0, i)),
        out_shape=jax.ShapeDtypeStruct((rows, width), BF16),
        compiler_params=pltpu.CompilerParams(vmem_limit_bytes=48 * MIB),
        name="fresh_rows",
    )(direction, basis, weight)


def parts_kernel(place_ref, *refs):
    pieces, acts, outs = refs[:5], refs[5:15], refs[15:23]
    rows, tokens, made, row_sems, token_sems, made_sems = refs[23:]
    depth, size = pieces[0].shape[0], tokens.shape[1]
    half = size // 2

    loads = []
    for n, (index, shift) in enumerate(((0, 0), (1, 0), (2, 0), (3, 0), (3, depth // 2))):
        count = pieces[n].shape[0]
        at = pl.ds(pl.multiple_of(place_ref[index] * depth + shift, count), count)
        loads.append(pltpu.make_async_copy(pieces[n], rows.at[at, :], row_sems.at[n]))
    token_loads = []
    for n in range(8):
        h, k = n // 4, n % 4
        copies = []
        for m in range(2):
            source = acts[5 * h + k].at[m * half : (m + 1) * half, :] if k < 3 else acts[5 * h + 3 + m]
            target = tokens.at[n, m * half : (m + 1) * half, :]
            copies.append(pltpu.make_async_copy(source, target, token_sems.at[n, m]))
        token_loads.append(copies)

    for copy in loads + token_loads[0]:
        copy.start()
    for copy in loads:
        copy.wait()

    def store(n, i, h):
        return pltpu.make_async_copy(made.at[n, i], outs[2 * i + h].at[lax.rem(n, 4)], made_sems.at[n, i])

    def body(n, carry):
        for k in range(1, 8):

            @pl.when(n == k - 1)
            def _(k=k):
                for copy in token_loads[k]:
                    copy.start()

        for m in range(2):
            held = tokens.at[n, m * half : (m + 1) * half, :]
            pltpu.make_async_copy(held, held, token_sems.at[n, m]).wait()
        part = dot(tokens[n], rows[...]).astype(BF16)
        for i in range(4):
            made[n, i] = part[:, i * 256 : (i + 1) * 256]
        for h in range(2):

            @pl.when(n // 4 == h)
            def _(h=h):
                for i in range(4):
                    store(n, i, h).start()

        return carry

    lax.fori_loop(0, 8, body, 0)
    for n in range(8):
        for i in range(4):
            store(n, i, n // 4).wait()


def parts(place, pieces, acts):
    tokens, depth = acts[0].shape
    columns = pieces[0].shape[1]
    whole = pl.BlockSpec(memory_space=pl.ANY)
    return pl.pallas_call(
        parts_kernel,
        in_specs=[pl.BlockSpec(memory_space=pltpu.SMEM)] + [whole] * 15,
        out_specs=[whole] * 8,
        scratch_shapes=[
            pltpu.VMEM((depth, columns), BF16),
            pltpu.VMEM((8, tokens, depth), BF16),
            pltpu.VMEM((8, 4, tokens, columns // 4), BF16),
            pltpu.SemaphoreType.DMA((5,)),
            pltpu.SemaphoreType.DMA((8, 2)),
            pltpu.SemaphoreType.DMA((8, 4)),
        ],
        out_shape=[jax.ShapeDtypeStruct((4, tokens, columns // 4), BF16)] * 8,
        compiler_params=pltpu.CompilerParams(vmem_limit_bytes=58 * MIB),
        name="parts",
    )(place, *pieces, *acts)


def sums_kernel(groups, terms, placed, *refs):
    place_ref, refs = (refs[0], refs[1:]) if placed else (None, refs)
    ins, outs = refs[: groups * terms], refs[groups * terms : -4]
    held, made, in_sems, out_sems = refs[-4:]
    loads = [pltpu.make_async_copy(ins[k], held.at[k], in_sems.at[k]) for k in range(groups * terms)]
    for copy in loads:
        copy.start()
    stores = []
    for g in range(groups):
        for k in range(terms):
            loads[g * terms + k].wait()
        for n in range(4):
            total = held[g * terms, n].astype(F32)
            for k in range(1, terms):
                total += held[g * terms + k, n].astype(F32)
            made[g, n] = total.astype(BF16)
            target = outs[0].at[place_ref[4 + 4 * g + n]] if placed else outs[g].at[n]
            stores.append(pltpu.make_async_copy(made.at[g, n], target, out_sems.at[g, n]))
            stores[-1].start()
    for copy in stores:
        copy.wait()


def sums(groups, place=None):
    count, terms, block = len(groups), len(groups[0]), groups[0][0].shape
    whole = pl.BlockSpec(memory_space=pl.ANY)
    placed = place is not None
    shape = jax.ShapeDtypeStruct((4 * count, *block[1:]) if placed else block, BF16)
    return pl.pallas_call(
        functools.partial(sums_kernel, count, terms, placed),
        in_specs=[pl.BlockSpec(memory_space=pltpu.SMEM)] * placed + [whole] * (count * terms),
        out_specs=whole if placed else [whole] * count,
        out_shape=shape if placed else [shape] * count,
        scratch_shapes=[
            pltpu.VMEM((count * terms, *block), BF16),
            pltpu.VMEM((count, *block), BF16),
            pltpu.SemaphoreType.DMA((count * terms,)),
            pltpu.SemaphoreType.DMA((count, 4)),
        ],
        compiler_params=pltpu.CompilerParams(vmem_limit_bytes=58 * MIB),
        name="sums",
    )(*[place] * placed, *[v for g in groups for v in g])


def inner_kernel(core_ref, acts_ref, mine_ref, other_ref, out_ref, rows):
    for k in range(16):
        for ref, core in ((mine_ref, core_ref[0]), (other_ref, 1 - core_ref[0])):
            at = pl.ds(pl.multiple_of(k * 128 + core * 64, 64), 64)
            rows[at, :] = ref[k]
    out_ref[...] = dot(acts_ref[...], rows[...])


def inner(core, acts, mine, other):
    rank = mine.shape[-1]
    whole = lambda a: pl.BlockSpec(a.shape, lambda i, core: (0,) * len(a.shape))
    return pl.pallas_call(
        inner_kernel,
        grid_spec=pltpu.PrefetchScalarGridSpec(
            num_scalar_prefetch=1,
            grid=(1,),
            in_specs=[whole(acts), whole(mine), whole(other)],
            out_specs=pl.BlockSpec((acts.shape[0], rank), lambda i, core: (0, 0)),
            scratch_shapes=[pltpu.VMEM((acts.shape[1], rank), BF16)],
        ),
        out_shape=jax.ShapeDtypeStruct((acts.shape[0], rank), F32),
        compiler_params=pltpu.CompilerParams(vmem_limit_bytes=40 * MIB),
        name="inner",
    )(core, acts, mine, other)


def change_kernel(y_ref, *refs):
    shares, basis_ref, out_ref = refs[:4], refs[4], refs[5]
    total = shares[0][...].astype(F32)
    for ref in shares[1:]:
        total += ref[...].astype(F32)
    zh, zl = two_terms(total)
    both = dot_t(jnp.concatenate([zh, zl], axis=0), basis_ref[...].astype(BF16), ((1,), (1,)))
    out_ref[...] = (learning_rate * (both[: zh.shape[0]] + both[zh.shape[0] :])).astype(BF16)


def change_of(y, shares, basis):
    columns = 1024
    tokens, rank = shares[0].shape
    return pl.pallas_call(
        change_kernel,
        grid_spec=pltpu.PrefetchScalarGridSpec(
            num_scalar_prefetch=1,
            grid=(2,),
            in_specs=[pl.BlockSpec((tokens, rank), lambda i, y: (0, 0))] * 4
            + [pl.BlockSpec((columns, rank), lambda i, y: (y[0] * 2 + i, 0))],
            out_specs=pl.BlockSpec((tokens, columns), lambda i, y: (0, i)),
        ),
        out_shape=jax.ShapeDtypeStruct((tokens, 2 * columns), BF16),
        compiler_params=pltpu.CompilerParams(vmem_limit_bytes=24 * MIB),
        name="change",
    )(y, *shares, basis)


def halves_kernel(first_ref, last_ref, *out_refs):
    out_refs[0][...] = first_ref[...]
    out_refs[1][...] = last_ref[...]


def halves(first, last):
    rows, width = first.shape
    shape = (rows // 2, width)
    return pl.pallas_call(
        halves_kernel,
        grid=(1,),
        in_specs=[pl.BlockSpec(shape, lambda i: (0, 0)), pl.BlockSpec(shape, lambda i: (1, 0))],
        out_specs=[pl.BlockSpec(shape, lambda i: (0, 0))] * 2,
        out_shape=[jax.ShapeDtypeStruct(shape, BF16)] * 2,
        compiler_params=pltpu.CompilerParams(vmem_limit_bytes=16 * MIB),
        name="halves",
    )(first, last)


def output_kernel(part_ref, change_ref, out_ref):
    for n in range(part_ref.shape[0]):
        columns = slice(n * 256, (n + 1) * 256)
        total = part_ref[n].astype(F32) - change_ref[:, columns].astype(F32)
        out_ref[:, columns] = total.astype(BF16)


def output_rows(part, change):
    blocks, tokens, columns = part.shape
    return pl.pallas_call(
        output_kernel,
        grid=(2,),
        in_specs=[
            pl.BlockSpec((blocks // 2, tokens, columns), lambda i: (i, 0, 0)),
            pl.BlockSpec((tokens, blocks // 2 * columns), lambda i: (0, i)),
        ],
        out_specs=pl.BlockSpec((tokens, blocks // 2 * columns), lambda i: (0, i)),
        out_shape=jax.ShapeDtypeStruct((tokens, blocks * columns), BF16),
        name="output_rows",
    )(part, change)


def swap(value):
    return lax.ppermute(value, "c", [(0, 1), (1, 0)])


def shift(value, axis, by):
    return lax.ppermute(value, axis, [(i, (i + by) % 4) for i in range(4)])


def on_device(acts, out_grad, basis, moment1, moment2, weight, next_acts):
    z, x, c, y = (lax.axis_index(a).astype(jnp.int32) for a in ("z", "x", "c", "y"))
    core, tensor = c[None], y[None]
    old = weight[0]
    keep, give = project(core, acts, out_grad, basis)
    own = lax.all_to_all(exchange_order(ORDER, tensor, old), ("x", "c"), 0, 0)
    got, beside = swap(give), swap(next_acts)
    own, keep, got, tokens, beside = lax.optimization_barrier((own, keep, got, next_acts, beside))
    own = own.reshape(512, 1024)
    near = (shift(own, "z", 1), shift(own, "z", -1), shift(tokens, "x", 1), shift(tokens, "x", -1))
    right, left, tr, tl = lax.optimization_barrier(near)
    ta, tb = halves(tr, tl)
    ta, tb, right, left = lax.optimization_barrier((ta, tb, right, left))
    near_a, near_b = halves(right, left)
    ta, tb = shift(ta, "x", 1), shift(tb, "x", -1)
    far_a, far_b = shift(near_a, "z", 1), shift(near_b, "z", -1)
    ta, tb, tr, tl, far_a, far_b = lax.optimization_barrier((ta, tb, tr, tl, far_a, far_b))
    pieces = (own, right, left, far_a, far_b)
    blocks = (tokens, tr, tl, ta, tb)
    others = (beside, *(swap(v) for v in blocks[1:]))
    place = [(v + d) % 4 for v in (z, x) for d in (0, 3, 1, 2)]
    place = jnp.stack(place[:4] + [2 * v + c for v in place[4:]] + [2 * v + 1 - c for v in place[4:]])
    up2, down2, up1, down1, up3, down3, up0, down0 = parts(place, pieces, blocks + others)
    got_up2, got_down2 = shift(up2, "y", 1), shift(down2, "y", -1)
    keep, got, up2 = lax.optimization_barrier((keep, got, up2))
    projected = (keep + got.astype(F32)).astype(BF16)
    projected = lax.all_to_all(projected, ("z", "x"), 0, 0)
    got_down1, got_up3 = shift(down1, "y", 1), shift(up3, "y", -1)
    up1, down3 = sums(((up1, got_up2), (down3, got_down2)))
    got_up1, got_down3 = shift(up1, "y", 1), shift(down3, "y", -1)
    projected, up1 = lax.optimization_barrier((projected, up1))
    projected = jnp.sum(projected.astype(F32), axis=0)
    first = beta_one * moment1[0] + (1.0 - beta_one) * projected
    second = beta_two * moment2[0] + (1.0 - beta_two) * projected * projected
    direction = (
        first
        / (1.0 - beta_one**adam_step)
        / (jnp.sqrt(second / (1.0 - beta_two**adam_step)) + epsilon)
    )
    sent = jnp.broadcast_to(direction.astype(BF16)[None], (16, 64, 256))
    mine = lax.all_to_all(sent, ("z", "x"), 0, 0)
    fresh = fresh_rows(direction, basis, old)
    up0, down0, fresh, mine = lax.optimization_barrier((up0, down0, fresh, mine))
    part = sums(((up0, got_up1, got_up3), (down0, got_down1, got_down3)), place)
    part, mine = lax.optimization_barrier((part, mine))
    share = inner(core, next_acts, mine, swap(mine)).astype(BF16)
    shares = [share] + [shift(share, "y", d) for d in (1, -1, 2)]
    change = change_of(tensor, shares, basis)
    part = lax.all_to_all(part, ("x", "c"), 0, 0)
    output = output_rows(part, change)
    return (output, fresh[None], first[None], second[None])


def solution(mesh):
    cube = Mesh(mesh.devices.reshape(4, 4, 2, 4), ("z", "x", "c", "y"))
    placed = (
        P(DP, "y"),
        P(DP, None),
        P(),
        P("y", DP, None),
        P("y", DP, None),
        P("y", DP, None),
        P(DP, "y"),
    )
    return jax.shard_map(
        on_device,
        mesh=cube,
        in_specs=placed,
        out_specs=(
            P(DP, "y"),
            P("y", DP, None),
            P("y", DP, None),
            P("y", DP, None),
        ),
        check_vma=False,
    )
```

time: 195 us -> 163 us (0.84)
  waiting for transfers between devices: 93.2 us -> 60.4 us
  between operations: 14.1 us -> 0.81 us
  starting transfers between devices: 33.8 us -> 45.4 us
  Pallas kernels: 35.9 us -> 42.2 us
  other arithmetic: 4.33 us -> 1.77 us
    all_to_all x4, waiting for transfers between devices: 80.6 us -> 5.92 us  [the longest x1 2.98 us: on_device(): mine = lax.all_to_all(sent, ('z', 'x'), 0, 0)]
    ppermute x4 -> x17, waiting for transfers between devices: 11.9 us -> 47.2 us  [shift(): return lax.ppermute(value, axis, [(i, (i + by) % 4) for i in range(4)])]
    ppermute x4 -> x17, starting transfers between devices: 5.47 us -> 21.3 us  [shift(): return lax.ppermute(value, axis, [(i, (i + by) % 4) for i in range(4)])]
    all_to_all x4, starting transfers between devices: 28.3 us -> 17.3 us  [the longest x1 5.49 us: on_device(): part = lax.all_to_all(part, ('x', 'c'), 0, 0)]
    pallas_call x2 -> x10, Pallas kernels: 26.9 us -> 36.3 us  [the longest x1 15 us: parts(): pl.pallas_call(parts_kernel, in_specs=[pl.BlockSpec(memory_space=pltpu.SM...]
    ppermute x0 -> x7, waiting for transfers between devices: none -> 7.27 us  [swap(): return lax.ppermute(value, 'c', [(0, 1), (1, 0)])]
    ppermute x0 -> x7, starting transfers between devices: none -> 6.85 us  [swap(): return lax.ppermute(value, 'c', [(0, 1), (1, 0)])]
    unnamed x16 -> x36, local copies, waits for them, and re-layouts: 3.02 us -> 9.43 us
  transfers between devices with their start and end apart: 9 -> 28, of which waited for: 6 -> 18; matrix products, arithmetic and copies ran while one was open for 6% -> 2% of each run, Pallas kernels for 10% -> 12%
where the time goes in v2:
time: 163 us; the launch traced here: 161 us
  waiting for transfers between devices  60.4 us (37%)
  starting transfers between devices  45.4 us (28%)
  Pallas kernels  42.2 us (26%)
  local copies, waits for them, and re-layouts  10.9 us (7%)
  other arithmetic  1.77 us (1%)
    ppermute x17, waiting for transfers between devices, shift(): return lax.ppermute(value, axis, [(i, (i + by) % 4) for i in range(4)])  47.2 us
    ppermute x17, starting transfers between devices, shift(): return lax.ppermute(value, axis, [(i, (i + by) % 4) for i in range(4)])  21.3 us
    pallas_call x1, Pallas kernels, parts(): pl.pallas_call(parts_kernel, in_specs=[pl.BlockSpec(memory_space=pltpu.SM...  15 us
    unnamed x36, local copies, waits for them, and re-layouts  9.43 us
    pallas_call x1, Pallas kernels, project(): pl.pallas_call(project_kernel, grid_spec=pltpu.PrefetchScalarGridSpec(num...  9.05 us
    ppermute x7, waiting for transfers between devices, swap(): return lax.ppermute(value, 'c', [(0, 1), (1, 0)])  7.27 us
    ppermute x7, starting transfers between devices, swap(): return lax.ppermute(value, 'c', [(0, 1), (1, 0)])  6.85 us
    pallas_call x2, Pallas kernels, sums(): pl.pallas_call(functools.partial(sums_kernel, count, terms, placed), in_s...  5.89 us
  transfers between devices with their start and end apart: 28, of which 18 were waited for; matrix products, arithmetic and copies ran while one was open for 2% of the time, Pallas kernels for 12%

profile of v2, /device:TPU:1, one launch (start us, length us, event | category | flops | bytes accessed | tf_op | source)
XLA Modules:
  0.0 161.5 jit_solution(12625255058330042761)
XLA Ops:
  0.6 1.5 collective-permute-start.1
  2.1 1.2 copy-done.2
  3.4 1.1 exchange_order.1
  4.5 4.6 %all-to-all-start = ((bf16[8,64,1024]{2,1,0:T(8,128)(2,1)}), bf16[8,64,1024]{2,1,0:T(8,128)(2,1)}, u32[]{:S(2)}, u32[]{:S(2)}) async-start(bf16[8,64,1024]{2,1,0:T(8,128)(2,1)} %exchange_order.1), calls=%async_computation | async-start | bytes 2097152 | tf_op jit(solution)/shard_map/all_to_all | solution.py:368
  9.1 1.2 copy-done.8
  10.3 9.0 %project.1 = (f32[16,64,256]{2,1,0:T(8,128)S(1)}, bf16[16,64,256]{2,1,0:T(8,128)(2,1)S(1)}) custom-call(s32[1]{0:T(128)} %bitcast.14.core_ref, bf16[256,8192]{1,0:T(8,128)(2,1)} %grad_ref.1, f32[8192,256]{1,0:T(8,128)} %refs_4_.1, bf16[256,2048]{1,0:T(8,128)(2,1)S(1)} %copy-done.8), custom_call_target="tpu_custom_call" | custom-call | tf_op jit(solution)/shard_map/project/pallas_call | solution.py:67
  19.5 1.9 %collective-permute-done = bf16[16,64,256]{2,1,0:T(8,128)(2,1)S(1)} collective-permute-done((bf16[16,64,256]{2,1,0:T(8,128)(2,1)S(1)}, bf16[16,64,256]{2,1,0:T(8,128)(2,1)S(1)}, u32[]{:S(2)}, u32[]{:S(2)}) %collective-permute-start) | collective-permute-done | bytes 524320 | tf_op jit(solution)/shard_map/ppermute | solution.py:356
  21.4 2.9 %all-to-all-done = bf16[8,64,1024]{2,1,0:T(8,128)(2,1)} async-done(((bf16[8,64,1024]{2,1,0:T(8,128)(2,1)}), bf16[8,64,1024]{2,1,0:T(8,128)(2,1)}, u32[]{:S(2)}, u32[]{:S(2)}) %all-to-all-start) | async-done | bytes 1048608 | tf_op jit(solution)/shard_map/all_to_all | solution.py:368
  24.3 3.8 %collective-permute-start.3 = (bf16[512,1024]{1,0:T(8,128)(2,1)}, bf16[512,1024]{1,0:T(8,128)(2,1)S(1)}, u32[]{:S(2)}, u32[]{:S(2)}) collective-permute-start(bf16[512,1024]{1,0:T(8,128)(2,1)} %bitcast.15.refs_0_), channel_id=1, source_target_pairs={{0,96},{32,0},{64,32},{96,64},{1,97},{33,1},{65,33},{97,65},{2,98}... | collective-permute-start | bytes 3145736 | tf_op jit(solution)/shard_map/ppermute | solution.py:360
  28.1 0.9 collective-permute-start.5
  29.5 20.4 %collective-permute-done.3.last_ref.refs_2_ = bf16[512,1024]{1,0:T(8,128)(2,1)S(1)} collective-permute-done((bf16[512,1024]{1,0:T(8,128)(2,1)}, bf16[512,1024]{1,0:T(8,128)(2,1)S(1)}, u32[]{:S(2)}, u32[]{:S(2)}) %collective-permute-start.3) | collective-permute-done | bytes 1048608 | tf_op jit(solution)/shard_map/ppermute | solution.py:360
  50.0 3.1 %collective-permute-done.2.first_ref.refs_1_ = bf16[512,1024]{1,0:T(8,128)(2,1)S(1)} collective-permute-done((bf16[512,1024]{1,0:T(8,128)(2,1)}, bf16[512,1024]{1,0:T(8,128)(2,1)S(1)}, u32[]{:S(2)}, u32[]{:S(2)}) %collective-permute-start.2) | collective-permute-done | bytes 1048608 | tf_op jit(solution)/shard_map/ppermute | solution.py:360
  53.5 1.3 halves.2
  55.0 2.5 %collective-permute-start.7 = (bf16[128,2048]{1,0:T(8,128)(2,1)S(1)}, bf16[128,2048]{1,0:T(8,128)(2,1)}, u32[]{:S(2)}, u32[]{:S(2)}) collective-permute-start(bf16[128,2048]{1,0:T(8,128)(2,1)S(1)} %get-tuple-element.61), channel_id=1, source_target_pairs={{0,24},{8,0},{16,8},{24,16},{1,25},{9,1},{17,9},{25,17},{2,26},{10... | collective-permute-start | bytes 1572872 | tf_op jit(solution)/shard_map/ppermute | solution.py:360
  57.7 2.7 %collective-permute-start.9 = (bf16[256,1024]{1,0:T(8,128)(2,1)S(1)}, bf16[256,1024]{1,0:T(8,128)(2,1)S(1)}, u32[]{:S(2)}, u32[]{:S(2)}) collective-permute-start(bf16[256,1024]{1,0:T(8,128)(2,1)S(1)} %get-tuple-element.63), channel_id=1, source_target_pairs={{0,96},{32,0},{64,32},{96,64},{1,97},{33,1},{65,33},{97,65},{2,98}... | collective-permute-start | bytes 1572872 | tf_op jit(solution)/shard_map/ppermute | solution.py:360
  60.3 6.9 %collective-permute-done.6.refs_8_ = bf16[128,2048]{1,0:T(8,128)(2,1)} collective-permute-done((bf16[128,2048]{1,0:T(8,128)(2,1)S(1)}, bf16[128,2048]{1,0:T(8,128)(2,1)}, u32[]{:S(2)}, u32[]{:S(2)}) %collective-permute-start.6) | collective-permute-done | bytes 524320 | tf_op jit(solution)/shard_map/ppermute | solution.py:360
  67.2 2.3 %collective-permute-done.8.refs_3_ = bf16[256,1024]{1,0:T(8,128)(2,1)S(1)} collective-permute-done((bf16[256,1024]{1,0:T(8,128)(2,1)S(1)}, bf16[256,1024]{1,0:T(8,128)(2,1)S(1)}, u32[]{:S(2)}, u32[]{:S(2)}) %collective-permute-start.8) | collective-permute-done | bytes 524320 | tf_op jit(solution)/shard_map/ppermute | solution.py:360
  69.5 0.8 copy-done.10
  70.3 3.7 %collective-permute-start.10 = (bf16[256,2048]{1,0:T(8,128)(2,1)}, bf16[256,2048]{1,0:T(8,128)(2,1)}, u32[]{:S(2)}, u32[]{:S(2)}) collective-permute-start(bf16[256,2048]{1,0:T(8,128)(2,1)} %collective-permute-done.4.first_ref.refs_6_), channel_id=1, source_target_pairs={{0,4},{4,0},{1,5},{5,1},{2,6},{6,2},{3,7},{7,3},{8,12},{12,8},{9,1... | collective-permute-start | bytes 3145736 | tf_op jit(solution)/shard_map/ppermute | solution.py:356
  74.0 0.8 collective-permute-start.11
  76.0 2.9 %collective-permute-done.12.refs_13_ = bf16[128,2048]{1,0:T(8,128)(2,1)} collective-permute-done((bf16[128,2048]{1,0:T(8,128)(2,1)}, bf16[128,2048]{1,0:T(8,128)(2,1)}, u32[]{:S(2)}, u32[]{:S(2)}) %collective-permute-start.12) | collective-permute-done | bytes 524320 | tf_op jit(solution)/shard_map/ppermute | solution.py:356
  79.7 15.0 %parts.1 = (bf16[4,256,256]{2,1,0:T(8,128)(2,1)}, bf16[4,256,256]{2,1,0:T(8,128)(2,1)}, bf16[4,256,256]{2,1,0:T(8,128)(2,1)}, bf16[4,256,256]{2,1,0:T(8,128)(2,1...) custom-call(s32[12]{0:T(128)} %stack.51.place_ref.refs_0_, ...), custom_call_target="tpu_custom_call" | custom-call | tf_op jit(solution)/shard_map/parts/pallas_call | solution.py:198
  94.6 1.4 collective-permute-start.14
  96.0 1.5 collective-permute-start.15
  97.5 0.9 add_convert_fusion
  98.4 3.6 %all-to-all-start.1 = ((bf16[16,64,256]{2,1,0:T(8,128)(2,1)}), bf16[16,64,256]{2,1,0:T(8,128)(2,1)S(1)}, u32[]{:S(2)}, u32[]{:S(2)}) async-start(bf16[16,64,256]{2,1,0:T(8,128)(2,1)} %add_convert_fusion), calls=%async_computation.1 | async-start | bytes 1048576 | tf_op jit(solution)/shard_map/all_to_all | solution.py:389
  102.0 1.5 collective-permute-start.17
  103.6 5.5 %collective-permute-done.15.refs_3_ = bf16[4,256,256]{2,1,0:T(8,128)(2,1)S(1)} collective-permute-done((bf16[4,256,256]{2,1,0:T(8,128)(2,1)}, bf16[4,256,256]{2,1,0:T(8,128)(2,1)S(1)}, u32[]{:S(2)}, u32[]{:S(2)}) %collective-permute-start.15) | collective-permute-done | bytes 524320 | tf_op jit(solution)/shard_map/ppermute | solution.py:360
  110.2 2.4 %sums.2 = (bf16[4,256,256]{2,1,0:T(8,128)(2,1)}, bf16[4,256,256]{2,1,0:T(8,128)(2,1)}) custom-call(bf16[4,256,256]{2,1,0:T(8,128)(2,1)} %get-tuple-element.78.refs_0_, bf16[4,256,256]{2,1,0:T(8,128)(2,1)} %copy-done.14, bf16[4,256,256]{2,1,0:T(8,128)(2,1)} %get-tuple-element.79.refs_2_, bf16[4,256,256]{2,1,0:T(8,128)(2,1)} %copy-done.15), custom_call_target="tpu_custom_call" | custom-call | tf_op jit(solution)/shard_map/sums/pallas_call | solution.py:244
  112.6 1.2 collective-permute-start.16
  113.9 1.7 %collective-permute-start.19 = (bf16[4,256,256]{2,1,0:T(8,128)(2,1)}, bf16[4,256,256]{2,1,0:T(8,128)(2,1)}, u32[]{:S(2)}, u32[]{:S(2)}) collective-permute-start(bf16[4,256,256]{2,1,0:T(8,128)(2,1)} %get-tuple-element.87), channel_id=1, source_target_pairs={{0,3},{1,0},{2,1},{3,2},{4,7},{5,4},{6,5},{7,6},{8,11},{9,8},{10,9... | collective-permute-start | bytes 1572872 | tf_op jit(solution)/shard_map/ppermute | solution.py:360
  116.2 0.8 broadcast_in_dim.22
  117.1 3.6 %all-to-all-start.2 = ((bf16[16,64,256]{2,1,0:T(8,128)(2,1)}), bf16[16,64,256]{2,1,0:T(8,128)(2,1)S(1)}, u32[]{:S(2)}, u32[]{:S(2)}) async-start(bf16[16,64,256]{2,1,0:T(8,128)(2,1)} %broadcast_in_dim.22), calls=%async_computation.2 | async-start | bytes 1048576 | tf_op jit(solution)/shard_map/all_to_all | solution.py:403
  120.8 5.9 %fresh_rows.1 = bf16[64,8192]{1,0:T(8,128)(2,1)} custom-call(f32[64,256]{1,0:T(8,128)S(1)} %fusion.4.direction_ref, f32[8192,256]{1,0:T(8,128)} %refs_4_.1, bf16[64,8192]{1,0:T(8,128)(2,1)S(1)} %bitcast.35), custom_call_target="tpu_custom_call" | custom-call | tf_op jit(solution)/shard_map/fresh_rows/pallas_call | solution.py:121
  126.6 3.0 %all-to-all-done.2.mine_ref = bf16[16,64,256]{2,1,0:T(8,128)(2,1)S(1)} async-done(((bf16[16,64,256]{2,1,0:T(8,128)(2,1)}), bf16[16,64,256]{2,1,0:T(8,128)(2,1)S(1)}, u32[]{:S(2)}, u32[]{:S(2)}) %all-to-all-start.2) | async-done | bytes 524320 | tf_op jit(solution)/shard_map/all_to_all | solution.py:403
  129.6 2.0 %collective-permute-done.19.refs_6_ = bf16[4,256,256]{2,1,0:T(8,128)(2,1)} collective-permute-done((bf16[4,256,256]{2,1,0:T(8,128)(2,1)}, bf16[4,256,256]{2,1,0:T(8,128)(2,1)}, u32[]{:S(2)}, u32[]{:S(2)}) %collective-permute-start.19) | collective-permute-done | bytes 524320 | tf_op jit(solution)/shard_map/ppermute | solution.py:360
  132.0 3.5 %sums.3 = bf16[8,256,256]{2,1,0:T(8,128)(2,1)} custom-call(s32[12]{0:T(128)} %stack.51.place_ref.refs_0_, bf16[4,256,256]{2,1,0:T(8,128)(2,1)} %get-tuple-element.83.refs_1_, bf16[4,256,256]{2,1,0:T(8,128)(2,1)} %collective-permute-done.16.refs_2_, bf16[4,256,256]{2,1,0:T(8,128)(2,1)} %collective-permute-done.17.refs_3_, ...), custom_call_target="tpu_custom_call" | custom-call | tf_op jit(solution)/shard_map/sums/pallas_call | solution.py:244
  135.4 5.5 %all-to-all-start.3 = ((bf16[8,256,256]{2,1,0:T(8,128)(2,1)}), bf16[8,256,256]{2,1,0:T(8,128)(2,1)S(1)}, u32[]{:S(2)}, u32[]{:S(2)}) async-start(bf16[8,256,256]{2,1,0:T(8,128)(2,1)} %sums.3), calls=%async_computation.3 | async-start | bytes 2097152 | tf_op jit(solution)/shard_map/all_to_all | solution.py:411
  141.1 1.7 %collective-permute-done.20.other_ref = bf16[16,64,256]{2,1,0:T(8,128)(2,1)S(1)} collective-permute-done((bf16[16,64,256]{2,1,0:T(8,128)(2,1)S(1)}, bf16[16,64,256]{2,1,0:T(8,128)(2,1)S(1)}, u32[]{:S(2)}, u32[]{:S(2)}) %collective-permute-start.20) | collective-permute-done | bytes 524320 | tf_op jit(solution)/shard_map/ppermute | solution.py:356
  143.4 1.9 %collective-permute-start.23 = (bf16[256,256]{1,0:T(8,128)(2,1)S(1)}, bf16[256,256]{1,0:T(8,128)(2,1)S(1)}, u32[]{:S(2)}, u32[]{:S(2)}) collective-permute-start(bf16[256,256]{1,0:T(8,128)(2,1)S(1)} %convert_element_type.20.refs_0_), channel_id=1, source_target_pairs={{0,2},{1,3},{2,0},{3,1},{4,6},{5,7},{6,4},{7,5},{8,10},{9,11},{10,... | collective-permute-start | bytes 393224 | tf_op jit(solution)/shard_map/ppermute | solution.py:360
  145.2 1.1 collective-permute-start.22
  146.7 3.2 %collective-permute-done.23.refs_3_ = bf16[256,256]{1,0:T(8,128)(2,1)S(1)} collective-permute-done((bf16[256,256]{1,0:T(8,128)(2,1)S(1)}, bf16[256,256]{1,0:T(8,128)(2,1)S(1)}, u32[]{:S(2)}, u32[]{:S(2)}) %collective-permute-start.23) | collective-permute-done | bytes 131104 | tf_op jit(solution)/shard_map/ppermute | solution.py:360
  149.9 2.3 %collective-permute-done.22.refs_2_ = bf16[256,256]{1,0:T(8,128)(2,1)S(1)} collective-permute-done((bf16[256,256]{1,0:T(8,128)(2,1)S(1)}, bf16[256,256]{1,0:T(8,128)(2,1)S(1)}, u32[]{:S(2)}, u32[]{:S(2)}) %collective-permute-start.22) | collective-permute-done | bytes 131104 | tf_op jit(solution)/shard_map/ppermute | solution.py:360
  152.6 3.4 %copy-done = f32[8192,256]{1,0:T(8,128)S(1)} copy-done((f32[8192,256]{1,0:T(8,128)S(1)}, f32[8192,256]{1,0:T(8,128)}, u32[]{:S(2)}) %copy-start) | copy-done | bytes 8388632
  156.0 1.1 change.1.change_ref
  157.1 1.0 copy-done.1
  158.1 1.0 copy-done.9
  159.1 2.4 %output_rows.1 = bf16[256,2048]{1,0:T(8,128)(2,1)} custom-call(bf16[8,256,256]{2,1,0:T(8,128)(2,1)} %copy-done.9, bf16[256,2048]{1,0:T(8,128)(2,1)} %copy-done.1), custom_call_target="tpu_custom_call" | custom-call | tf_op jit(solution)/shard_map/output_rows/pallas_call | solution.py:342
  (62 shorter events, 7.4 us)
Async XLA Ops:
  0.6 23.7 %collective-permute-start.1 = (bf16[256,2048]{1,0:T(8,128)(2,1)}, bf16[256,2048]{1,0:T(8,128)(2,1)}, u32[]{:S(2)}, u32[]{:S(2)}) collective-permute-start(bf16[256,2048]{1,0:T(8,128)(2,1)} %acts_ref.3), channel_id=1, source_target_pairs={{0,4},{4,0},{1,5},{5,1},{2,6},{6,2},{3,7},{7,3},{8,12},{12,8},{9,1... | collective-permute-start | bytes 3145736 | tf_op jit(solution)/shard_map/ppermute | solution.py:356
  2.1 1.2 copy-start.2
  4.5 23.6 %copy-start.4 = (bf16[256,2048]{1,0:T(8,128)(2,1)S(1)}, bf16[256,2048]{1,0:T(8,128)(2,1)}, u32[]{:S(2)}) copy-start(bf16[256,2048]{1,0:T(8,128)(2,1)} %acts_ref.3) | copy-start | bytes 3145732
  4.5 19.8 %all-to-all-start = ((bf16[8,64,1024]{2,1,0:T(8,128)(2,1)}), bf16[8,64,1024]{2,1,0:T(8,128)(2,1)}, u32[]{:S(2)}, u32[]{:S(2)}) async-start(bf16[8,64,1024]{2,1,0:T(8,128)(2,1)} %exchange_order.1), calls=%async_computation | async-start | bytes 2097152 | tf_op jit(solution)/shard_map/all_to_all | solution.py:368
  9.1 1.2 copy-start.8
  19.4 2.0 %collective-permute-start = (bf16[16,64,256]{2,1,0:T(8,128)(2,1)S(1)}, bf16[16,64,256]{2,1,0:T(8,128)(2,1)S(1)}, u32[]{:S(2)}, u32[]{:S(2)}) collective-permute-start(bf16[16,64,256]{2,1,0:T(8,128)(2,1)S(1)} %get-tuple-element.49), channel_id=1, source_target_pairs={{0,4},{4,0},{1,5},{5,1},{2,6},{6,2},{3,7},{7,3},{8,12},{12,8},{9,1... | collective-permute-start | bytes 1572872 | tf_op jit(solution)/shard_map/ppermute | solution.py:356
  21.4 2.9 %copy-start.12 = (bf16[16,64,256]{2,1,0:T(8,128)(2,1)}, bf16[16,64,256]{2,1,0:T(8,128)(2,1)S(1)}, u32[]{:S(2)}) copy-start(bf16[16,64,256]{2,1,0:T(8,128)(2,1)S(1)} %collective-permute-done) | copy-start | bytes 1572868
  24.3 25.7 %collective-permute-start.3 = (bf16[512,1024]{1,0:T(8,128)(2,1)}, bf16[512,1024]{1,0:T(8,128)(2,1)S(1)}, u32[]{:S(2)}, u32[]{:S(2)}) collective-permute-start(bf16[512,1024]{1,0:T(8,128)(2,1)} %bitcast.15.refs_0_), channel_id=1, source_target_pairs={{0,96},{32,0},{64,32},{96,64},{1,97},{33,1},{65,33},{97,65},{2,98}... | collective-permute-start | bytes 3145736 | tf_op jit(solution)/shard_map/ppermute | solution.py:360
  28.1 25.0 %collective-permute-start.2 = (bf16[512,1024]{1,0:T(8,128)(2,1)}, bf16[512,1024]{1,0:T(8,128)(2,1)S(1)}, u32[]{:S(2)}, u32[]{:S(2)}) collective-permute-start(bf16[512,1024]{1,0:T(8,128)(2,1)} %bitcast.15.refs_0_), channel_id=1, source_target_pairs={{0,32},{32,64},{64,96},{96,0},{1,33},{33,65},{65,97},{97,1},{2,34}... | collective-permute-start | bytes 3145736 | tf_op jit(solution)/shard_map/ppermute | solution.py:360
  28.1 25.0 %collective-permute-start.5 = (bf16[256,2048]{1,0:T(8,128)(2,1)S(1)}, bf16[256,2048]{1,0:T(8,128)(2,1)}, u32[]{:S(2)}, u32[]{:S(2)}) collective-permute-start(bf16[256,2048]{1,0:T(8,128)(2,1)S(1)} %copy-done.4), channel_id=1, source_target_pairs={{0,24},{8,0},{16,8},{24,16},{1,25},{9,1},{17,9},{25,17},{2,26},{10... | collective-permute-start | bytes 3145736 | tf_op jit(solution)/shard_map/ppermute | solution.py:360
  29.0 24.5 %collective-permute-start.4 = (bf16[256,2048]{1,0:T(8,128)(2,1)S(1)}, bf16[256,2048]{1,0:T(8,128)(2,1)}, u32[]{:S(2)}, u32[]{:S(2)}) collective-permute-start(bf16[256,2048]{1,0:T(8,128)(2,1)S(1)} %copy-done.4), channel_id=1, source_target_pairs={{0,8},{8,16},{16,24},{24,0},{1,9},{9,17},{17,25},{25,1},{2,10},{10... | collective-permute-start | bytes 3145736 | tf_op jit(solution)/shard_map/ppermute | solution.py:360
  50.0 29.7 %copy-start.6 = (bf16[512,1024]{1,0:T(8,128)(2,1)}, bf16[512,1024]{1,0:T(8,128)(2,1)S(1)}, u32[]{:S(2)}) copy-start(bf16[512,1024]{1,0:T(8,128)(2,1)S(1)} %collective-permute-done.3.last_ref.refs_2_) | copy-start | bytes 3145732
  53.1 4.4 %copy-start.7 = (bf16[512,1024]{1,0:T(8,128)(2,1)}, bf16[512,1024]{1,0:T(8,128)(2,1)S(1)}, u32[]{:S(2)}) copy-start(bf16[512,1024]{1,0:T(8,128)(2,1)S(1)} %collective-permute-done.2.first_ref.refs_1_) | copy-start | bytes 3145732
  54.8 12.4 %collective-permute-start.6 = (bf16[128,2048]{1,0:T(8,128)(2,1)S(1)}, bf16[128,2048]{1,0:T(8,128)(2,1)}, u32[]{:S(2)}, u32[]{:S(2)}) collective-permute-start(bf16[128,2048]{1,0:T(8,128)(2,1)S(1)} %get-tuple-element.60), channel_id=1, source_target_pairs={{0,8},{8,16},{16,24},{24,0},{1,9},{9,17},{17,25},{25,1},{2,10},{10... | collective-permute-start | bytes 1572872 | tf_op jit(solution)/shard_map/ppermute | solution.py:360
  55.0 12.2 %collective-permute-start.7 = (bf16[128,2048]{1,0:T(8,128)(2,1)S(1)}, bf16[128,2048]{1,0:T(8,128)(2,1)}, u32[]{:S(2)}, u32[]{:S(2)}) collective-permute-start(bf16[128,2048]{1,0:T(8,128)(2,1)S(1)} %get-tuple-element.61), channel_id=1, source_target_pairs={{0,24},{8,0},{16,8},{24,16},{1,25},{9,1},{17,9},{25,17},{2,26},{10... | collective-permute-start | bytes 1572872 | tf_op jit(solution)/shard_map/ppermute | solution.py:360
  57.6 11.9 %collective-permute-start.8 = (bf16[256,1024]{1,0:T(8,128)(2,1)S(1)}, bf16[256,1024]{1,0:T(8,128)(2,1)S(1)}, u32[]{:S(2)}, u32[]{:S(2)}) collective-permute-start(bf16[256,1024]{1,0:T(8,128)(2,1)S(1)} %get-tuple-element.62), channel_id=1, source_target_pairs={{0,32},{32,64},{64,96},{96,0},{1,33},{33,65},{65,97},{97,1},{2,34}... | collective-permute-start | bytes 1572872 | tf_op jit(solution)/shard_map/ppermute | solution.py:360
  57.7 11.8 %collective-permute-start.9 = (bf16[256,1024]{1,0:T(8,128)(2,1)S(1)}, bf16[256,1024]{1,0:T(8,128)(2,1)S(1)}, u32[]{:S(2)}, u32[]{:S(2)}) collective-permute-start(bf16[256,1024]{1,0:T(8,128)(2,1)S(1)} %get-tuple-element.63), channel_id=1, source_target_pairs={{0,96},{32,0},{64,32},{96,64},{1,97},{33,1},{65,33},{97,65},{2,98}... | collective-permute-start | bytes 1572872 | tf_op jit(solution)/shard_map/ppermute | solution.py:360
  69.5 0.8 copy-start.10
  70.3 3.7 %copy-start.11 = (bf16[256,1024]{1,0:T(8,128)(2,1)}, bf16[256,1024]{1,0:T(8,128)(2,1)S(1)}, u32[]{:S(2)}) copy-start(bf16[256,1024]{1,0:T(8,128)(2,1)S(1)} %collective-permute-done.9.refs_4_) | copy-start | bytes 1572868
  70.3 9.4 %collective-permute-start.10 = (bf16[256,2048]{1,0:T(8,128)(2,1)}, bf16[256,2048]{1,0:T(8,128)(2,1)}, u32[]{:S(2)}, u32[]{:S(2)}) collective-permute-start(bf16[256,2048]{1,0:T(8,128)(2,1)} %collective-permute-done.4.first_ref.refs_6_), channel_id=1, source_target_pairs={{0,4},{4,0},{1,5},{5,1},{2,6},{6,2},{3,7},{7,3},{8,12},{12,8},{9,1... | collective-permute-start | bytes 3145736 | tf_op jit(solution)/shard_map/ppermute | solution.py:356
  74.0 5.6 %collective-permute-start.11 = (bf16[256,2048]{1,0:T(8,128)(2,1)}, bf16[256,2048]{1,0:T(8,128)(2,1)}, u32[]{:S(2)}, u32[]{:S(2)}) collective-permute-start(bf16[256,2048]{1,0:T(8,128)(2,1)} %collective-permute-done.5.last_ref.refs_7_), channel_id=1, source_target_pairs={{0,4},{4,0},{1,5},{5,1},{2,6},{6,2},{3,7},{7,3},{8,12},{12,8},{9,1... | collective-permute-start | bytes 3145736 | tf_op jit(solution)/shard_map/ppermute | solution.py:356
  74.9 4.0 %collective-permute-start.12 = (bf16[128,2048]{1,0:T(8,128)(2,1)}, bf16[128,2048]{1,0:T(8,128)(2,1)}, u32[]{:S(2)}, u32[]{:S(2)}) collective-permute-start(bf16[128,2048]{1,0:T(8,128)(2,1)} %collective-permute-done.6.refs_8_), channel_id=1, source_target_pairs={{0,4},{4,0},{1,5},{5,1},{2,6},{6,2},{3,7},{7,3},{8,12},{12,8},{9,1... | collective-permute-start | bytes 1572872 | tf_op jit(solution)/shard_map/ppermute | solution.py:356
  74.9 4.8 %collective-permute-start.13 = (bf16[128,2048]{1,0:T(8,128)(2,1)}, bf16[128,2048]{1,0:T(8,128)(2,1)}, u32[]{:S(2)}, u32[]{:S(2)}) collective-permute-start(bf16[128,2048]{1,0:T(8,128)(2,1)} %collective-permute-done.7.refs_9_), channel_id=1, source_target_pairs={{0,4},{4,0},{1,5},{5,1},{2,6},{6,2},{3,7},{7,3},{8,12},{12,8},{9,1... | collective-permute-start | bytes 1572872 | tf_op jit(solution)/shard_map/ppermute | solution.py:356
  76.0 21.5 %copy-start.13 = (bf16[16,64,256]{2,1,0:T(8,128)(2,1)S(1)}, bf16[16,64,256]{2,1,0:T(8,128)(2,1)}, u32[]{:S(2)}) copy-start(bf16[16,64,256]{2,1,0:T(8,128)(2,1)} %copy-done.12) | copy-start | bytes 1572868
  76.0 39.6 %copy-start.16 = (f32[1,64,256]{2,1,0:T(8,128)S(1)}, f32[1,64,256]{2,1,0:T(8,128)}, u32[]{:S(2)}) copy-start(f32[1,64,256]{2,1,0:T(8,128)} %param.10) | copy-start | bytes 196612
  76.0 39.6 %copy-start.17 = (f32[1,64,256]{2,1,0:T(8,128)S(1)}, f32[1,64,256]{2,1,0:T(8,128)}, u32[]{:S(2)}) copy-start(f32[1,64,256]{2,1,0:T(8,128)} %param.11) | copy-start | bytes 196612
  76.0 44.7 %copy-start.3 = (bf16[1,64,8192]{2,1,0:T(8,128)(2,1)S(1)}, bf16[1,64,8192]{2,1,0:T(8,128)(2,1)}, u32[]{:S(2)}) copy-start(bf16[1,64,8192]{2,1,0:T(8,128)(2,1)} %param.12) | copy-start | bytes 3145732
  94.6 14.8 %collective-permute-start.14 = (bf16[4,256,256]{2,1,0:T(8,128)(2,1)}, bf16[4,256,256]{2,1,0:T(8,128)(2,1)S(1)}, u32[]{:S(2)}, u32[]{:S(2)}) collective-permute-start(bf16[4,256,256]{2,1,0:T(8,128)(2,1)} %get-tuple-element.75), channel_id=1, source_target_pairs={{0,1},{1,2},{2,3},{3,0},{4,5},{5,6},{6,7},{7,4},{8,9},{9,10},{10,1... | collective-permute-start | bytes 1572872 | tf_op jit(solution)/shard_map/ppermute | solution.py:360
  96.0 13.0 %collective-permute-start.15 = (bf16[4,256,256]{2,1,0:T(8,128)(2,1)}, bf16[4,256,256]{2,1,0:T(8,128)(2,1)S(1)}, u32[]{:S(2)}, u32[]{:S(2)}) collective-permute-start(bf16[4,256,256]{2,1,0:T(8,128)(2,1)} %get-tuple-element.80), channel_id=1, source_target_pairs={{0,3},{1,0},{2,1},{3,2},{4,7},{5,4},{6,5},{7,6},{8,11},{9,8},{10,9... | collective-permute-start | bytes 1572872 | tf_op jit(solution)/shard_map/ppermute | solution.py:360
  98.4 15.3 %all-to-all-start.1 = ((bf16[16,64,256]{2,1,0:T(8,128)(2,1)}), bf16[16,64,256]{2,1,0:T(8,128)(2,1)S(1)}, u32[]{:S(2)}, u32[]{:S(2)}) async-start(bf16[16,64,256]{2,1,0:T(8,128)(2,1)} %add_convert_fusion), calls=%async_computation.1 | async-start | bytes 1048576 | tf_op jit(solution)/shard_map/all_to_all | solution.py:389
  102.0 27.6 %collective-permute-start.17 = (bf16[4,256,256]{2,1,0:T(8,128)(2,1)}, bf16[4,256,256]{2,1,0:T(8,128)(2,1)}, u32[]{:S(2)}, u32[]{:S(2)}) collective-permute-start(bf16[4,256,256]{2,1,0:T(8,128)(2,1)} %get-tuple-element.84), channel_id=1, source_target_pairs={{0,3},{1,0},{2,1},{3,2},{4,7},{5,4},{6,5},{7,6},{8,11},{9,8},{10,9... | collective-permute-start | bytes 1572872 | tf_op jit(solution)/shard_map/ppermute | solution.py:360
  103.5 26.2 %collective-permute-start.18 = (bf16[4,256,256]{2,1,0:T(8,128)(2,1)}, bf16[4,256,256]{2,1,0:T(8,128)(2,1)}, u32[]{:S(2)}, u32[]{:S(2)}) collective-permute-start(bf16[4,256,256]{2,1,0:T(8,128)(2,1)} %get-tuple-element.86), channel_id=1, source_target_pairs={{0,1},{1,2},{2,3},{3,0},{4,5},{5,6},{6,7},{7,4},{8,9},{9,10},{10,1... | collective-permute-start | bytes 1572872 | tf_op jit(solution)/shard_map/ppermute | solution.py:360
  109.0 0.8 copy-start.15
  109.4 0.8 copy-start.14
  112.6 19.3 %collective-permute-start.16 = (bf16[4,256,256]{2,1,0:T(8,128)(2,1)}, bf16[4,256,256]{2,1,0:T(8,128)(2,1)}, u32[]{:S(2)}, u32[]{:S(2)}) collective-permute-start(bf16[4,256,256]{2,1,0:T(8,128)(2,1)} %get-tuple-element.81), channel_id=1, source_target_pairs={{0,1},{1,2},{2,3},{3,0},{4,5},{5,6},{6,7},{7,4},{8,9},{9,10},{10,1... | collective-permute-start | bytes 1572872 | tf_op jit(solution)/shard_map/ppermute | solution.py:360
  113.9 17.7 %collective-permute-start.19 = (bf16[4,256,256]{2,1,0:T(8,128)(2,1)}, bf16[4,256,256]{2,1,0:T(8,128)(2,1)}, u32[]{:S(2)}, u32[]{:S(2)}) collective-permute-start(bf16[4,256,256]{2,1,0:T(8,128)(2,1)} %get-tuple-element.87), channel_id=1, source_target_pairs={{0,3},{1,0},{2,1},{3,2},{4,7},{5,4},{6,5},{7,6},{8,11},{9,8},{10,9... | collective-permute-start | bytes 1572872 | tf_op jit(solution)/shard_map/ppermute | solution.py:360
  117.1 12.5 %all-to-all-start.2 = ((bf16[16,64,256]{2,1,0:T(8,128)(2,1)}), bf16[16,64,256]{2,1,0:T(8,128)(2,1)S(1)}, u32[]{:S(2)}, u32[]{:S(2)}) async-start(bf16[16,64,256]{2,1,0:T(8,128)(2,1)} %broadcast_in_dim.22), calls=%async_computation.2 | async-start | bytes 1048576 | tf_op jit(solution)/shard_map/all_to_all | solution.py:403
  120.7 22.1 %copy-start.5 = (bf16[256,2048]{1,0:T(8,128)(2,1)S(1)}, bf16[256,2048]{1,0:T(8,128)(2,1)}, u32[]{:S(2)}) copy-start(bf16[256,2048]{1,0:T(8,128)(2,1)} %acts_ref.3) | copy-start | bytes 3145732
  135.4 22.6 %all-to-all-start.3 = ((bf16[8,256,256]{2,1,0:T(8,128)(2,1)}), bf16[8,256,256]{2,1,0:T(8,128)(2,1)S(1)}, u32[]{:S(2)}, u32[]{:S(2)}) async-start(bf16[8,256,256]{2,1,0:T(8,128)(2,1)} %sums.3), calls=%async_computation.3 | async-start | bytes 2097152 | tf_op jit(solution)/shard_map/all_to_all | solution.py:411
  140.9 1.9 %collective-permute-start.20 = (bf16[16,64,256]{2,1,0:T(8,128)(2,1)S(1)}, bf16[16,64,256]{2,1,0:T(8,128)(2,1)S(1)}, u32[]{:S(2)}, u32[]{:S(2)}) collective-permute-start(bf16[16,64,256]{2,1,0:T(8,128)(2,1)S(1)} %all-to-all-done.2.mine_ref), channel_id=1, source_target_pairs={{0,4},{4,0},{1,5},{5,1},{2,6},{6,2},{3,7},{7,3},{8,12},{12,8},{9,1... | collective-permute-start | bytes 1572872 | tf_op jit(solution)/shard_map/ppermute | solution.py:356
  143.4 6.5 %collective-permute-start.23 = (bf16[256,256]{1,0:T(8,128)(2,1)S(1)}, bf16[256,256]{1,0:T(8,128)(2,1)S(1)}, u32[]{:S(2)}, u32[]{:S(2)}) collective-permute-start(bf16[256,256]{1,0:T(8,128)(2,1)S(1)} %convert_element_type.20.refs_0_), channel_id=1, source_target_pairs={{0,2},{1,3},{2,0},{3,1},{4,6},{5,7},{6,4},{7,5},{8,10},{9,11},{10,... | collective-permute-start | bytes 393224 | tf_op jit(solution)/shard_map/ppermute | solution.py:360
  145.2 7.0 %collective-permute-start.22 = (bf16[256,256]{1,0:T(8,128)(2,1)S(1)}, bf16[256,256]{1,0:T(8,128)(2,1)S(1)}, u32[]{:S(2)}, u32[]{:S(2)}) collective-permute-start(bf16[256,256]{1,0:T(8,128)(2,1)S(1)} %convert_element_type.20.refs_0_), channel_id=1, source_target_pairs={{0,3},{1,0},{2,1},{3,2},{4,7},{5,4},{6,5},{7,6},{8,11},{9,8},{10,9... | collective-permute-start | bytes 393224 | tf_op jit(solution)/shard_map/ppermute | solution.py:360
  146.3 6.3 %collective-permute-start.21 = (bf16[256,256]{1,0:T(8,128)(2,1)S(1)}, bf16[256,256]{1,0:T(8,128)(2,1)S(1)}, u32[]{:S(2)}, u32[]{:S(2)}) collective-permute-start(bf16[256,256]{1,0:T(8,128)(2,1)S(1)} %convert_element_type.20.refs_0_), channel_id=1, source_target_pairs={{0,1},{1,2},{2,3},{3,0},{4,5},{5,6},{6,7},{7,4},{8,9},{9,10},{10,1... | collective-permute-start | bytes 393224 | tf_op jit(solution)/shard_map/ppermute | solution.py:360
  152.6 3.4 %copy-start = (f32[8192,256]{1,0:T(8,128)S(1)}, f32[8192,256]{1,0:T(8,128)}, u32[]{:S(2)}) copy-start(f32[8192,256]{1,0:T(8,128)} %refs_4_.1) | copy-start | bytes 25165828
  157.1 1.0 copy-start.1
  158.1 1.0 copy-start.9

commit v3 on v2

--- a/solution.py
+++ b/solution.py
@@ -89,21 +89,28 @@
 ORDER = (2, 1, 3, 0)
 
 
-def exchange_order_kernel(order, y_ref, weight_ref, out_ref):
+def exchange_order_kernel(order, y_ref, weight_ref, out_ref, held, sems):
+    loads = []
     for i, d in enumerate(order):
-        j = lax.rem(y_ref[0] + d, 4)
+        column = pl.multiple_of(lax.rem(y_ref[0] + d, 4) * 2048, 2048)
+        loads.append(pltpu.make_async_copy(weight_ref.at[:, pl.ds(column, 2048)], held.at[i], sems.at[i]))
+    for copy in loads:
+        copy.start()
+    for i, copy in enumerate(loads):
+        copy.wait()
         for k in range(8):
-            column = pl.multiple_of((j * 8 + k) * 256, 256)
-            out_ref[k, :, i * 256 : (i + 1) * 256] = weight_ref[:, pl.ds(column, 256)]
+            out_ref[k, :, i * 256 : (i + 1) * 256] = held[i, :, k * 256 : (k + 1) * 256]
 
 
 def exchange_order(order, y, weight):
     rows = weight.shape[0]
+    count = len(order)
     return pl.pallas_call(
         functools.partial(exchange_order_kernel, order),
-        in_specs=[pl.BlockSpec(memory_space=pltpu.SMEM), pl.BlockSpec(memory_space=pltpu.VMEM)],
-        out_shape=jax.ShapeDtypeStruct((8, rows, 256 * len(order)), BF16),
-        compiler_params=pltpu.CompilerParams(vmem_limit_bytes=16 * MIB),
+        in_specs=[pl.BlockSpec(memory_space=pltpu.SMEM), pl.BlockSpec(memory_space=pl.ANY)],
+        out_shape=jax.ShapeDtypeStruct((8, rows, 256 * count), BF16),
+        scratch_shapes=[pltpu.VMEM((count, rows, 2048), BF16), pltpu.SemaphoreType.DMA((count,))],
+        compiler_params=pltpu.CompilerParams(vmem_limit_bytes=58 * MIB),
         name="exchange_order",
     )(y, weight)
 
@@ -283,32 +290,29 @@
     )(core, acts, mine, other)
 
 
-def change_kernel(y_ref, *refs):
+def change_kernel(*refs):
     shares, basis_ref, out_ref = refs[:4], refs[4], refs[5]
     total = shares[0][...].astype(F32)
     for ref in shares[1:]:
         total += ref[...].astype(F32)
     zh, zl = two_terms(total)
-    both = dot_t(jnp.concatenate([zh, zl], axis=0), basis_ref[...].astype(BF16), ((1,), (1,)))
+    both = dot_t(jnp.concatenate([zh, zl], axis=0), basis_ref[...], ((1,), (1,)))
     out_ref[...] = (learning_rate * (both[: zh.shape[0]] + both[zh.shape[0] :])).astype(BF16)
 
 
-def change_of(y, shares, basis):
+def change_of(shares, basis):
     columns = 1024
     tokens, rank = shares[0].shape
     return pl.pallas_call(
         change_kernel,
-        grid_spec=pltpu.PrefetchScalarGridSpec(
-            num_scalar_prefetch=1,
-            grid=(2,),
-            in_specs=[pl.BlockSpec((tokens, rank), lambda i, y: (0, 0))] * 4
-            + [pl.BlockSpec((columns, rank), lambda i, y: (y[0] * 2 + i, 0))],
-            out_specs=pl.BlockSpec((tokens, columns), lambda i, y: (0, i)),
-        ),
+        grid=(2,),
+        in_specs=[pl.BlockSpec((tokens, rank), lambda i: (0, 0))] * 4
+        + [pl.BlockSpec((columns, rank), lambda i: (i, 0))],
+        out_specs=pl.BlockSpec((tokens, columns), lambda i: (0, i)),
         out_shape=jax.ShapeDtypeStruct((tokens, 2 * columns), BF16),
         compiler_params=pltpu.CompilerParams(vmem_limit_bytes=24 * MIB),
         name="change",
-    )(y, *shares, basis)
+    )(*shares, basis)
 
 
 def halves_kernel(first_ref, last_ref, *out_refs):
@@ -348,6 +352,7 @@
         ],
         out_specs=pl.BlockSpec((tokens, blocks // 2 * columns), lambda i: (0, i)),
         out_shape=jax.ShapeDtypeStruct((tokens, blocks * columns), BF16),
+        compiler_params=pltpu.CompilerParams(vmem_limit_bytes=24 * MIB),
         name="output_rows",
     )(part, change)
 
@@ -367,7 +372,8 @@
     keep, give = project(core, acts, out_grad, basis)
     own = lax.all_to_all(exchange_order(ORDER, tensor, old), ("x", "c"), 0, 0)
     got, beside = swap(give), swap(next_acts)
-    own, keep, got, tokens, beside = lax.optimization_barrier((own, keep, got, next_acts, beside))
+    rows = lax.dynamic_slice_in_dim(basis, y * 2048, 2048, axis=0).astype(BF16)
+    own, keep, got, tokens, beside, rows = lax.optimization_barrier((own, keep, got, next_acts, beside, rows))
     own = own.reshape(512, 1024)
     near = (shift(own, "z", 1), shift(own, "z", -1), shift(tokens, "x", 1), shift(tokens, "x", -1))
     right, left, tr, tl = lax.optimization_barrier(near)
@@ -402,12 +408,12 @@
     sent = jnp.broadcast_to(direction.astype(BF16)[None], (16, 64, 256))
     mine = lax.all_to_all(sent, ("z", "x"), 0, 0)
     fresh = fresh_rows(direction, basis, old)
-    up0, down0, fresh, mine = lax.optimization_barrier((up0, down0, fresh, mine))
+    up0, down0, fresh = lax.optimization_barrier((up0, down0, fresh))
     part = sums(((up0, got_up1, got_up3), (down0, got_down1, got_down3)), place)
     part, mine = lax.optimization_barrier((part, mine))
     share = inner(core, next_acts, mine, swap(mine)).astype(BF16)
     shares = [share] + [shift(share, "y", d) for d in (1, -1, 2)]
-    change = change_of(tensor, shares, basis)
+    change = change_of(shares, rows)
     part = lax.all_to_all(part, ("x", "c"), 0, 0)
     output = output_rows(part, change)
     return (output, fresh[None], first[None], second[None])

time: 163 us -> 160 us (0.982)
  local copies, waits for them, and re-layouts: 10.9 us -> 7.2 us
  Pallas kernels: 42.2 us -> 44 us
  waiting for transfers between devices: 60.4 us -> 58.7 us
    unnamed x36 -> x28, local copies, waits for them, and re-layouts: 9.43 us -> 2.99 us
    ppermute x17, waiting for transfers between devices: 47.2 us -> 51 us  [shift(): return lax.ppermute(value, axis, [(i, (i + by) % 4) for i in range(4)])]
    all_to_all x1, waiting for transfers between devices: 2.98 us -> 0.01 us  [on_device(): mine = lax.all_to_all(sent, ('z', 'x'), 0, 0)]
    convert_element_type x0 -> x1, local copies, waits for them, and re-layouts: none -> 2.69 us  [on_device(): rows = lax.dynamic_slice_in_dim(basis, y * 2048, 2048, axis=0).astype(BF16)]
    ppermute x17, starting transfers between devices: 21.3 us -> 23 us  [shift(): return lax.ppermute(value, axis, [(i, (i + by) % 4) for i in range(4)])]
    ppermute x7, waiting for transfers between devices: 7.27 us -> 5.57 us  [swap(): return lax.ppermute(value, 'c', [(0, 1), (1, 0)])]
  transfers between devices with their start and end apart: 28 -> 28, of which waited for: 18 -> 16; matrix products, arithmetic and copies ran while one was open for 2% -> 4% of each run, Pallas kernels for 12% -> 17%
where the time goes in v3:
time: 160 us; the launch traced here: 159 us
  waiting for transfers between devices  58.7 us (37%)
  starting transfers between devices  46.3 us (29%)
  Pallas kernels  44 us (28%)
  local copies, waits for them, and re-layouts  7.2 us (4%)
  other arithmetic  1.78 us (1%)
    ppermute x17, waiting for transfers between devices, shift(): return lax.ppermute(value, axis, [(i, (i + by) % 4) for i in range(4)])  51 us
    ppermute x17, starting transfers between devices, shift(): return lax.ppermute(value, axis, [(i, (i + by) % 4) for i in range(4)])  23 us
    pallas_call x1, Pallas kernels, parts(): pl.pallas_call(parts_kernel, in_specs=[pl.BlockSpec(memory_space=pltpu.SM...  15 us
    pallas_call x1, Pallas kernels, project(): pl.pallas_call(project_kernel, grid_spec=pltpu.PrefetchScalarGridSpec(num...  9.83 us
    ppermute x7, starting transfers between devices, swap(): return lax.ppermute(value, 'c', [(0, 1), (1, 0)])  6.09 us
    pallas_call x1, Pallas kernels, fresh_rows(): pl.pallas_call(fresh_kernel, grid=(width // block,), in_specs=[pl.BlockSp...  5.95 us
    pallas_call x2, Pallas kernels, sums(): pl.pallas_call(functools.partial(sums_kernel, count, terms, placed), in_s...  5.89 us
    ppermute x7, waiting for transfers between devices, swap(): return lax.ppermute(value, 'c', [(0, 1), (1, 0)])  5.57 us
  transfers between devices with their start and end apart: 28, of which 16 were waited for; matrix products, arithmetic and copies ran while one was open for 4% of the time, Pallas kernels for 17%

profile of v3, /device:TPU:1, one launch (start us, length us, event | category | flops | bytes accessed | tf_op | source)
XLA Modules:
  0.0 158.7 jit_solution(6486894548953933715)
XLA Ops:
  0.6 1.5 collective-permute-start.1
  2.1 2.2 %exchange_order.1 = bf16[8,64,1024]{2,1,0:T(8,128)(2,1)} custom-call(s32[1]{0:T(128)} %bitcast.12.y_ref, bf16[64,8192]{1,0:T(8,128)(2,1)} %bitcast.34), custom_call_target="tpu_custom_call" | custom-call | tf_op jit(solution)/shard_map/exchange_order/pallas_call | solution.py:108
  4.4 4.5 %all-to-all-start = ((bf16[8,64,1024]{2,1,0:T(8,128)(2,1)}), bf16[8,64,1024]{2,1,0:T(8,128)(2,1)}, u32[]{:S(2)}, u32[]{:S(2)}) async-start(bf16[8,64,1024]{2,1,0:T(8,128)(2,1)} %exchange_order.1), calls=%async_computation | async-start | bytes 2097152 | tf_op jit(solution)/shard_map/all_to_all | solution.py:373
  8.9 1.3 copy-done.6
  10.2 9.8 %project.1 = (f32[16,64,256]{2,1,0:T(8,128)S(1)}, bf16[16,64,256]{2,1,0:T(8,128)(2,1)}) custom-call(s32[1]{0:T(128)} %bitcast.14.core_ref, bf16[256,8192]{1,0:T(8,128)(2,1)} %grad_ref.1, f32[8192,256]{1,0:T(8,128)} %basis_ref.3, bf16[256,2048]{1,0:T(8,128)(2,1)S(1)} %copy-done.6), custom_call_target="tpu_custom_call" | custom-call | tf_op jit(solution)/shard_map/project/pallas_call | solution.py:67
  20.0 2.7 %dynamic-slice_convert_fusion.refs_4_ = bf16[2048,256]{1,0:T(8,128)(2,1)} fusion(f32[8192,256]{1,0:T(8,128)} %basis_ref.3, s32[]{:T(128)S(6)} %select_n.46), kind=kLoop, calls=%fused_computation | loop fusion | bytes 2097156 | tf_op jit(solution)/shard_map/convert_element_type | solution.py:375
  22.7 1.4 all-to-all-done
  24.1 3.8 %collective-permute-start.3 = (bf16[512,1024]{1,0:T(8,128)(2,1)}, bf16[512,1024]{1,0:T(8,128)(2,1)S(1)}, u32[]{:S(2)}, u32[]{:S(2)}) collective-permute-start(bf16[512,1024]{1,0:T(8,128)(2,1)} %bitcast.15.refs_0_), channel_id=1, source_target_pairs={{0,96},{32,0},{64,32},{96,64},{1,97},{33,1},{65,33},{97,65},{2,98}... | collective-permute-start | bytes 3145736 | tf_op jit(solution)/shard_map/ppermute | solution.py:365
  27.8 2.4 %collective-permute-start.5 = (bf16[256,2048]{1,0:T(8,128)(2,1)S(1)}, bf16[256,2048]{1,0:T(8,128)(2,1)}, u32[]{:S(2)}, u32[]{:S(2)}) collective-permute-start(bf16[256,2048]{1,0:T(8,128)(2,1)S(1)} %copy-done.1), channel_id=1, source_target_pairs={{0,24},{8,0},{16,8},{24,16},{1,25},{9,1},{17,9},{25,17},{2,26},{10... | collective-permute-start | bytes 3145736 | tf_op jit(solution)/shard_map/ppermute | solution.py:365
  30.3 19.5 %collective-permute-done.3.last_ref.refs_2_ = bf16[512,1024]{1,0:T(8,128)(2,1)S(1)} collective-permute-done((bf16[512,1024]{1,0:T(8,128)(2,1)}, bf16[512,1024]{1,0:T(8,128)(2,1)S(1)}, u32[]{:S(2)}, u32[]{:S(2)}) %collective-permute-start.3) | collective-permute-done | bytes 1048608 | tf_op jit(solution)/shard_map/ppermute | solution.py:365
  49.8 3.1 %collective-permute-done.2.first_ref.refs_1_ = bf16[512,1024]{1,0:T(8,128)(2,1)S(1)} collective-permute-done((bf16[512,1024]{1,0:T(8,128)(2,1)}, bf16[512,1024]{1,0:T(8,128)(2,1)S(1)}, u32[]{:S(2)}, u32[]{:S(2)}) %collective-permute-start.2) | collective-permute-done | bytes 1048608 | tf_op jit(solution)/shard_map/ppermute | solution.py:365
  52.9 2.7 %collective-permute-done.4.first_ref.refs_6_ = bf16[256,2048]{1,0:T(8,128)(2,1)} collective-permute-done((bf16[256,2048]{1,0:T(8,128)(2,1)S(1)}, bf16[256,2048]{1,0:T(8,128)(2,1)}, u32[]{:S(2)}, u32[]{:S(2)}) %collective-permute-start.4) | collective-permute-done | bytes 1048608 | tf_op jit(solution)/shard_map/ppermute | solution.py:365
  55.6 1.3 halves.2
  56.9 2.7 %collective-permute-start.7 = (bf16[128,2048]{1,0:T(8,128)(2,1)S(1)}, bf16[128,2048]{1,0:T(8,128)(2,1)}, u32[]{:S(2)}, u32[]{:S(2)}) collective-permute-start(bf16[128,2048]{1,0:T(8,128)(2,1)S(1)} %get-tuple-element.61), channel_id=1, source_target_pairs={{0,24},{8,0},{16,8},{24,16},{1,25},{9,1},{17,9},{25,17},{2,26},{10... | collective-permute-start | bytes 1572872 | tf_op jit(solution)/shard_map/ppermute | solution.py:365
  59.7 2.7 %collective-permute-start.9 = (bf16[256,1024]{1,0:T(8,128)(2,1)S(1)}, bf16[256,1024]{1,0:T(8,128)(2,1)S(1)}, u32[]{:S(2)}, u32[]{:S(2)}) collective-permute-start(bf16[256,1024]{1,0:T(8,128)(2,1)S(1)} %get-tuple-element.63), channel_id=1, source_target_pairs={{0,96},{32,0},{64,32},{96,64},{1,97},{33,1},{65,33},{97,65},{2,98}... | collective-permute-start | bytes 1572872 | tf_op jit(solution)/shard_map/ppermute | solution.py:365
  62.4 7.6 %collective-permute-done.6.refs_8_ = bf16[128,2048]{1,0:T(8,128)(2,1)} collective-permute-done((bf16[128,2048]{1,0:T(8,128)(2,1)S(1)}, bf16[128,2048]{1,0:T(8,128)(2,1)}, u32[]{:S(2)}, u32[]{:S(2)}) %collective-permute-start.6) | collective-permute-done | bytes 524320 | tf_op jit(solution)/shard_map/ppermute | solution.py:365
  70.0 2.2 %collective-permute-done.8.refs_3_ = bf16[256,1024]{1,0:T(8,128)(2,1)S(1)} collective-permute-done((bf16[256,1024]{1,0:T(8,128)(2,1)S(1)}, bf16[256,1024]{1,0:T(8,128)(2,1)S(1)}, u32[]{:S(2)}, u32[]{:S(2)}) %collective-permute-start.8) | collective-permute-done | bytes 524320 | tf_op jit(solution)/shard_map/ppermute | solution.py:365
  72.2 0.8 copy-done.7
  73.0 3.1 %collective-permute-start.10 = (bf16[256,2048]{1,0:T(8,128)(2,1)}, bf16[256,2048]{1,0:T(8,128)(2,1)}, u32[]{:S(2)}, u32[]{:S(2)}) collective-permute-start(bf16[256,2048]{1,0:T(8,128)(2,1)} %collective-permute-done.4.first_ref.refs_6_), channel_id=1, source_target_pairs={{0,4},{4,0},{1,5},{5,1},{2,6},{6,2},{3,7},{7,3},{8,12},{12,8},{9,1... | collective-permute-start | bytes 3145736 | tf_op jit(solution)/shard_map/ppermute | solution.py:361
  76.1 0.8 collective-permute-start.11
  78.1 2.9 %collective-permute-done.12.refs_13_ = bf16[128,2048]{1,0:T(8,128)(2,1)} collective-permute-done((bf16[128,2048]{1,0:T(8,128)(2,1)}, bf16[128,2048]{1,0:T(8,128)(2,1)}, u32[]{:S(2)}, u32[]{:S(2)}) %collective-permute-start.12) | collective-permute-done | bytes 524320 | tf_op jit(solution)/shard_map/ppermute | solution.py:361
  81.0 0.7 collective-permute-done.13.refs_14_
  81.8 15.0 %parts.1 = (bf16[4,256,256]{2,1,0:T(8,128)(2,1)}, bf16[4,256,256]{2,1,0:T(8,128)(2,1)}, bf16[4,256,256]{2,1,0:T(8,128)(2,1)}, bf16[4,256,256]{2,1,0:T(8,128)(2,1...) custom-call(s32[12]{0:T(128)} %stack.51.place_ref.refs_0_, ...), custom_call_target="tpu_custom_call" | custom-call | tf_op jit(solution)/shard_map/parts/pallas_call | solution.py:205
  96.7 1.4 collective-permute-start.14
  98.1 1.5 collective-permute-start.15
  99.6 0.9 add_convert_fusion
  100.6 3.6 %all-to-all-start.1 = ((bf16[16,64,256]{2,1,0:T(8,128)(2,1)}), bf16[16,64,256]{2,1,0:T(8,128)(2,1)S(1)}, u32[]{:S(2)}, u32[]{:S(2)}) async-start(bf16[16,64,256]{2,1,0:T(8,128)(2,1)} %add_convert_fusion), calls=%async_computation.1 | async-start | bytes 1048576 | tf_op jit(solution)/shard_map/all_to_all | solution.py:395
  104.2 1.5 collective-permute-start.17
  105.7 5.6 %collective-permute-done.15.refs_3_ = bf16[4,256,256]{2,1,0:T(8,128)(2,1)} collective-permute-done((bf16[4,256,256]{2,1,0:T(8,128)(2,1)}, bf16[4,256,256]{2,1,0:T(8,128)(2,1)}, u32[]{:S(2)}, u32[]{:S(2)}) %collective-permute-start.15) | collective-permute-done | bytes 524320 | tf_op jit(solution)/shard_map/ppermute | solution.py:365
  111.5 0.8 copy-done.11
  112.3 2.4 %sums.2 = (bf16[4,256,256]{2,1,0:T(8,128)(2,1)}, bf16[4,256,256]{2,1,0:T(8,128)(2,1)}) custom-call(bf16[4,256,256]{2,1,0:T(8,128)(2,1)} %get-tuple-element.78.refs_0_, bf16[4,256,256]{2,1,0:T(8,128)(2,1)} %copy-done.11, bf16[4,256,256]{2,1,0:T(8,128)(2,1)} %get-tuple-element.79.refs_2_, bf16[4,256,256]{2,1,0:T(8,128)(2,1)} %collective-permute-done.15.refs_3_), custom_call_target="tpu_custom_call" | custom-call | tf_op jit(solution)/shard_map/sums/pallas_call | solution.py:251
  114.7 1.1 collective-permute-start.16
  115.9 1.7 %collective-permute-start.19 = (bf16[4,256,256]{2,1,0:T(8,128)(2,1)}, bf16[4,256,256]{2,1,0:T(8,128)(2,1)}, u32[]{:S(2)}, u32[]{:S(2)}) collective-permute-start(bf16[4,256,256]{2,1,0:T(8,128)(2,1)} %get-tuple-element.87), channel_id=1, source_target_pairs={{0,3},{1,0},{2,1},{3,2},{4,7},{5,4},{6,5},{7,6},{8,11},{9,8},{10,9... | collective-permute-start | bytes 1572872 | tf_op jit(solution)/shard_map/ppermute | solution.py:365
  118.3 0.8 broadcast_in_dim.22
  119.2 4.2 %all-to-all-start.2 = ((bf16[16,64,256]{2,1,0:T(8,128)(2,1)}), bf16[16,64,256]{2,1,0:T(8,128)(2,1)}, u32[]{:S(2)}, u32[]{:S(2)}) async-start(bf16[16,64,256]{2,1,0:T(8,128)(2,1)} %broadcast_in_dim.22), calls=%async_computation.2 | async-start | bytes 1048576 | tf_op jit(solution)/shard_map/all_to_all | solution.py:409
  123.5 5.9 %fresh_rows.1 = bf16[64,8192]{1,0:T(8,128)(2,1)} custom-call(f32[64,256]{1,0:T(8,128)S(1)} %fusion.4.direction_ref, f32[8192,256]{1,0:T(8,128)} %basis_ref.3, bf16[64,8192]{1,0:T(8,128)(2,1)S(1)} %bitcast.35), custom_call_target="tpu_custom_call" | custom-call | tf_op jit(solution)/shard_map/fresh_rows/pallas_call | solution.py:128
  129.5 4.3 %collective-permute-done.19.refs_6_ = bf16[4,256,256]{2,1,0:T(8,128)(2,1)} collective-permute-done((bf16[4,256,256]{2,1,0:T(8,128)(2,1)}, bf16[4,256,256]{2,1,0:T(8,128)(2,1)}, u32[]{:S(2)}, u32[]{:S(2)}) %collective-permute-start.19) | collective-permute-done | bytes 524320 | tf_op jit(solution)/shard_map/ppermute | solution.py:365
  134.1 3.5 %sums.3 = bf16[8,256,256]{2,1,0:T(8,128)(2,1)} custom-call(s32[12]{0:T(128)} %stack.51.place_ref.refs_0_, bf16[4,256,256]{2,1,0:T(8,128)(2,1)} %get-tuple-element.83.refs_1_, bf16[4,256,256]{2,1,0:T(8,128)(2,1)} %collective-permute-done.16.refs_2_, bf16[4,256,256]{2,1,0:T(8,128)(2,1)} %collective-permute-done.17.refs_3_, ...), custom_call_target="tpu_custom_call" | custom-call | tf_op jit(solution)/shard_map/sums/pallas_call | solution.py:251
  137.5 4.9 %all-to-all-start.3 = ((bf16[8,256,256]{2,1,0:T(8,128)(2,1)}), bf16[8,256,256]{2,1,0:T(8,128)(2,1)S(1)}, u32[]{:S(2)}, u32[]{:S(2)}) async-start(bf16[8,256,256]{2,1,0:T(8,128)(2,1)} %sums.3), calls=%async_computation.3 | async-start | bytes 2097152 | tf_op jit(solution)/shard_map/all_to_all | solution.py:417
  142.6 1.9 %collective-permute-done.20.other_ref = bf16[16,64,256]{2,1,0:T(8,128)(2,1)S(1)} collective-permute-done((bf16[16,64,256]{2,1,0:T(8,128)(2,1)}, bf16[16,64,256]{2,1,0:T(8,128)(2,1)S(1)}, u32[]{:S(2)}, u32[]{:S(2)}) %collective-permute-start.20) | collective-permute-done | bytes 524320 | tf_op jit(solution)/shard_map/ppermute | solution.py:361
  144.5 1.5 inner.1
  146.1 2.7 %collective-permute-start.23 = (bf16[256,256]{1,0:T(8,128)(2,1)S(1)}, bf16[256,256]{1,0:T(8,128)(2,1)S(1)}, u32[]{:S(2)}, u32[]{:S(2)}) collective-permute-start(bf16[256,256]{1,0:T(8,128)(2,1)S(1)} %convert_element_type.24.refs_0_), channel_id=1, source_target_pairs={{0,2},{1,3},{2,0},{3,1},{4,6},{5,7},{6,4},{7,5},{8,10},{9,11},{10,... | collective-permute-start | bytes 393224 | tf_op jit(solution)/shard_map/ppermute | solution.py:365
  148.8 1.1 collective-permute-start.22
  150.2 2.4 %collective-permute-done.23.refs_3_ = bf16[256,256]{1,0:T(8,128)(2,1)S(1)} collective-permute-done((bf16[256,256]{1,0:T(8,128)(2,1)S(1)}, bf16[256,256]{1,0:T(8,128)(2,1)S(1)}, u32[]{:S(2)}, u32[]{:S(2)}) %collective-permute-start.23) | collective-permute-done | bytes 131104 | tf_op jit(solution)/shard_map/ppermute | solution.py:365
  152.6 3.1 %collective-permute-done.22.refs_2_ = bf16[256,256]{1,0:T(8,128)(2,1)S(1)} collective-permute-done((bf16[256,256]{1,0:T(8,128)(2,1)S(1)}, bf16[256,256]{1,0:T(8,128)(2,1)S(1)}, u32[]{:S(2)}, u32[]{:S(2)}) %collective-permute-start.22) | collective-permute-done | bytes 131104 | tf_op jit(solution)/shard_map/ppermute | solution.py:365
  155.7 1.0 change.1.change_ref
  156.8 0.7 all-to-all-done.3.part_ref
  157.5 1.2 output_rows.1
  (55 shorter events, 3.5 us)
Async XLA Ops:
  0.6 23.4 %collective-permute-start.1 = (bf16[256,2048]{1,0:T(8,128)(2,1)}, bf16[256,2048]{1,0:T(8,128)(2,1)}, u32[]{:S(2)}, u32[]{:S(2)}) collective-permute-start(bf16[256,2048]{1,0:T(8,128)(2,1)} %acts_ref.3), channel_id=1, source_target_pairs={{0,4},{4,0},{1,5},{5,1},{2,6},{6,2},{3,7},{7,3},{8,12},{12,8},{9,1... | collective-permute-start | bytes 3145736 | tf_op jit(solution)/shard_map/ppermute | solution.py:361
  4.4 19.7 %all-to-all-start = ((bf16[8,64,1024]{2,1,0:T(8,128)(2,1)}), bf16[8,64,1024]{2,1,0:T(8,128)(2,1)}, u32[]{:S(2)}, u32[]{:S(2)}) async-start(bf16[8,64,1024]{2,1,0:T(8,128)(2,1)} %exchange_order.1), calls=%async_computation | async-start | bytes 2097152 | tf_op jit(solution)/shard_map/all_to_all | solution.py:373
  8.9 19.0 %copy-start.1 = (bf16[256,2048]{1,0:T(8,128)(2,1)S(1)}, bf16[256,2048]{1,0:T(8,128)(2,1)}, u32[]{:S(2)}) copy-start(bf16[256,2048]{1,0:T(8,128)(2,1)} %acts_ref.3) | copy-start | bytes 3145732
  8.9 1.3 copy-start.6
  20.0 2.7 %collective-permute-start = (bf16[16,64,256]{2,1,0:T(8,128)(2,1)}, bf16[16,64,256]{2,1,0:T(8,128)(2,1)S(1)}, u32[]{:S(2)}, u32[]{:S(2)}) collective-permute-start(bf16[16,64,256]{2,1,0:T(8,128)(2,1)} %get-tuple-element.49), channel_id=1, source_target_pairs={{0,4},{4,0},{1,5},{5,1},{2,6},{6,2},{3,7},{7,3},{8,12},{12,8},{9,1... | collective-permute-start | bytes 1572872 | tf_op jit(solution)/shard_map/ppermute | solution.py:361
  22.7 1.4 copy-start.9
  24.1 25.7 %collective-permute-start.3 = (bf16[512,1024]{1,0:T(8,128)(2,1)}, bf16[512,1024]{1,0:T(8,128)(2,1)S(1)}, u32[]{:S(2)}, u32[]{:S(2)}) collective-permute-start(bf16[512,1024]{1,0:T(8,128)(2,1)} %bitcast.15.refs_0_), channel_id=1, source_target_pairs={{0,96},{32,0},{64,32},{96,64},{1,97},{33,1},{65,33},{97,65},{2,98}... | collective-permute-start | bytes 3145736 | tf_op jit(solution)/shard_map/ppermute | solution.py:365
  27.8 25.0 %collective-permute-start.2 = (bf16[512,1024]{1,0:T(8,128)(2,1)}, bf16[512,1024]{1,0:T(8,128)(2,1)S(1)}, u32[]{:S(2)}, u32[]{:S(2)}) collective-permute-start(bf16[512,1024]{1,0:T(8,128)(2,1)} %bitcast.15.refs_0_), channel_id=1, source_target_pairs={{0,32},{32,64},{64,96},{96,0},{1,33},{33,65},{65,97},{97,1},{2,34}... | collective-permute-start | bytes 3145736 | tf_op jit(solution)/shard_map/ppermute | solution.py:365
  27.8 25.0 %collective-permute-start.5 = (bf16[256,2048]{1,0:T(8,128)(2,1)S(1)}, bf16[256,2048]{1,0:T(8,128)(2,1)}, u32[]{:S(2)}, u32[]{:S(2)}) collective-permute-start(bf16[256,2048]{1,0:T(8,128)(2,1)S(1)} %copy-done.1), channel_id=1, source_target_pairs={{0,24},{8,0},{16,8},{24,16},{1,25},{9,1},{17,9},{25,17},{2,26},{10... | collective-permute-start | bytes 3145736 | tf_op jit(solution)/shard_map/ppermute | solution.py:365
  30.3 25.3 %collective-permute-start.4 = (bf16[256,2048]{1,0:T(8,128)(2,1)S(1)}, bf16[256,2048]{1,0:T(8,128)(2,1)}, u32[]{:S(2)}, u32[]{:S(2)}) collective-permute-start(bf16[256,2048]{1,0:T(8,128)(2,1)S(1)} %copy-done.1), channel_id=1, source_target_pairs={{0,8},{8,16},{16,24},{24,0},{1,9},{9,17},{17,25},{25,1},{2,10},{10... | collective-permute-start | bytes 3145736 | tf_op jit(solution)/shard_map/ppermute | solution.py:365
  49.8 32.0 %copy-start.3 = (bf16[512,1024]{1,0:T(8,128)(2,1)}, bf16[512,1024]{1,0:T(8,128)(2,1)S(1)}, u32[]{:S(2)}) copy-start(bf16[512,1024]{1,0:T(8,128)(2,1)S(1)} %collective-permute-done.3.last_ref.refs_2_) | copy-start | bytes 3145732
  52.9 6.7 %copy-start.4 = (bf16[512,1024]{1,0:T(8,128)(2,1)}, bf16[512,1024]{1,0:T(8,128)(2,1)S(1)}, u32[]{:S(2)}) copy-start(bf16[512,1024]{1,0:T(8,128)(2,1)S(1)} %collective-permute-done.2.first_ref.refs_1_) | copy-start | bytes 3145732
  56.8 13.2 %collective-permute-start.6 = (bf16[128,2048]{1,0:T(8,128)(2,1)S(1)}, bf16[128,2048]{1,0:T(8,128)(2,1)}, u32[]{:S(2)}, u32[]{:S(2)}) collective-permute-start(bf16[128,2048]{1,0:T(8,128)(2,1)S(1)} %get-tuple-element.60), channel_id=1, source_target_pairs={{0,8},{8,16},{16,24},{24,0},{1,9},{9,17},{17,25},{25,1},{2,10},{10... | collective-permute-start | bytes 1572872 | tf_op jit(solution)/shard_map/ppermute | solution.py:365
  56.9 13.1 %collective-permute-start.7 = (bf16[128,2048]{1,0:T(8,128)(2,1)S(1)}, bf16[128,2048]{1,0:T(8,128)(2,1)}, u32[]{:S(2)}, u32[]{:S(2)}) collective-permute-start(bf16[128,2048]{1,0:T(8,128)(2,1)S(1)} %get-tuple-element.61), channel_id=1, source_target_pairs={{0,24},{8,0},{16,8},{24,16},{1,25},{9,1},{17,9},{25,17},{2,26},{10... | collective-permute-start | bytes 1572872 | tf_op jit(solution)/shard_map/ppermute | solution.py:365
  59.7 12.5 %collective-permute-start.8 = (bf16[256,1024]{1,0:T(8,128)(2,1)S(1)}, bf16[256,1024]{1,0:T(8,128)(2,1)S(1)}, u32[]{:S(2)}, u32[]{:S(2)}) collective-permute-start(bf16[256,1024]{1,0:T(8,128)(2,1)S(1)} %get-tuple-element.62), channel_id=1, source_target_pairs={{0,32},{32,64},{64,96},{96,0},{1,33},{33,65},{65,97},{97,1},{2,34}... | collective-permute-start | bytes 1572872 | tf_op jit(solution)/shard_map/ppermute | solution.py:365
  59.7 12.5 %collective-permute-start.9 = (bf16[256,1024]{1,0:T(8,128)(2,1)S(1)}, bf16[256,1024]{1,0:T(8,128)(2,1)S(1)}, u32[]{:S(2)}, u32[]{:S(2)}) collective-permute-start(bf16[256,1024]{1,0:T(8,128)(2,1)S(1)} %get-tuple-element.63), channel_id=1, source_target_pairs={{0,96},{32,0},{64,32},{96,64},{1,97},{33,1},{65,33},{97,65},{2,98}... | collective-permute-start | bytes 1572872 | tf_op jit(solution)/shard_map/ppermute | solution.py:365
  72.2 0.8 copy-start.7
  73.0 3.1 %copy-start.8 = (bf16[256,1024]{1,0:T(8,128)(2,1)}, bf16[256,1024]{1,0:T(8,128)(2,1)S(1)}, u32[]{:S(2)}) copy-start(bf16[256,1024]{1,0:T(8,128)(2,1)S(1)} %collective-permute-done.9.refs_4_) | copy-start | bytes 1572868
  73.0 8.7 %collective-permute-start.10 = (bf16[256,2048]{1,0:T(8,128)(2,1)}, bf16[256,2048]{1,0:T(8,128)(2,1)}, u32[]{:S(2)}, u32[]{:S(2)}) collective-permute-start(bf16[256,2048]{1,0:T(8,128)(2,1)} %collective-permute-done.4.first_ref.refs_6_), channel_id=1, source_target_pairs={{0,4},{4,0},{1,5},{5,1},{2,6},{6,2},{3,7},{7,3},{8,12},{12,8},{9,1... | collective-permute-start | bytes 3145736 | tf_op jit(solution)/shard_map/ppermute | solution.py:361
  76.1 5.6 %collective-permute-start.11 = (bf16[256,2048]{1,0:T(8,128)(2,1)}, bf16[256,2048]{1,0:T(8,128)(2,1)}, u32[]{:S(2)}, u32[]{:S(2)}) collective-permute-start(bf16[256,2048]{1,0:T(8,128)(2,1)} %collective-permute-done.5.last_ref.refs_7_), channel_id=1, source_target_pairs={{0,4},{4,0},{1,5},{5,1},{2,6},{6,2},{3,7},{7,3},{8,12},{12,8},{9,1... | collective-permute-start | bytes 3145736 | tf_op jit(solution)/shard_map/ppermute | solution.py:361
  76.9 4.1 %collective-permute-start.12 = (bf16[128,2048]{1,0:T(8,128)(2,1)}, bf16[128,2048]{1,0:T(8,128)(2,1)}, u32[]{:S(2)}, u32[]{:S(2)}) collective-permute-start(bf16[128,2048]{1,0:T(8,128)(2,1)} %collective-permute-done.6.refs_8_), channel_id=1, source_target_pairs={{0,4},{4,0},{1,5},{5,1},{2,6},{6,2},{3,7},{7,3},{8,12},{12,8},{9,1... | collective-permute-start | bytes 1572872 | tf_op jit(solution)/shard_map/ppermute | solution.py:361
  76.9 4.8 %collective-permute-start.13 = (bf16[128,2048]{1,0:T(8,128)(2,1)}, bf16[128,2048]{1,0:T(8,128)(2,1)}, u32[]{:S(2)}, u32[]{:S(2)}) collective-permute-start(bf16[128,2048]{1,0:T(8,128)(2,1)} %collective-permute-done.7.refs_9_), channel_id=1, source_target_pairs={{0,4},{4,0},{1,5},{5,1},{2,6},{6,2},{3,7},{7,3},{8,12},{12,8},{9,1... | collective-permute-start | bytes 1572872 | tf_op jit(solution)/shard_map/ppermute | solution.py:361
  78.1 21.5 %copy-start.10 = (bf16[16,64,256]{2,1,0:T(8,128)(2,1)S(1)}, bf16[16,64,256]{2,1,0:T(8,128)(2,1)}, u32[]{:S(2)}) copy-start(bf16[16,64,256]{2,1,0:T(8,128)(2,1)} %copy-done.9) | copy-start | bytes 1572868
  78.1 39.5 %copy-start.12 = (f32[1,64,256]{2,1,0:T(8,128)S(1)}, f32[1,64,256]{2,1,0:T(8,128)}, u32[]{:S(2)}) copy-start(f32[1,64,256]{2,1,0:T(8,128)} %param.10) | copy-start | bytes 196612
  78.1 39.5 %copy-start.13 = (f32[1,64,256]{2,1,0:T(8,128)S(1)}, f32[1,64,256]{2,1,0:T(8,128)}, u32[]{:S(2)}) copy-start(f32[1,64,256]{2,1,0:T(8,128)} %param.11) | copy-start | bytes 196612
  78.1 45.3 %copy-start = (bf16[1,64,8192]{2,1,0:T(8,128)(2,1)S(1)}, bf16[1,64,8192]{2,1,0:T(8,128)(2,1)}, u32[]{:S(2)}) copy-start(bf16[1,64,8192]{2,1,0:T(8,128)(2,1)} %param.12) | copy-start | bytes 3145732
  96.7 14.7 %collective-permute-start.14 = (bf16[4,256,256]{2,1,0:T(8,128)(2,1)}, bf16[4,256,256]{2,1,0:T(8,128)(2,1)S(1)}, u32[]{:S(2)}, u32[]{:S(2)}) collective-permute-start(bf16[4,256,256]{2,1,0:T(8,128)(2,1)} %get-tuple-element.75), channel_id=1, source_target_pairs={{0,1},{1,2},{2,3},{3,0},{4,5},{5,6},{6,7},{7,4},{8,9},{9,10},{10,1... | collective-permute-start | bytes 1572872 | tf_op jit(solution)/shard_map/ppermute | solution.py:365
  98.1 13.1 %collective-permute-start.15 = (bf16[4,256,256]{2,1,0:T(8,128)(2,1)}, bf16[4,256,256]{2,1,0:T(8,128)(2,1)}, u32[]{:S(2)}, u32[]{:S(2)}) collective-permute-start(bf16[4,256,256]{2,1,0:T(8,128)(2,1)} %get-tuple-element.80), channel_id=1, source_target_pairs={{0,3},{1,0},{2,1},{3,2},{4,7},{5,4},{6,5},{7,6},{8,11},{9,8},{10,9... | collective-permute-start | bytes 1572872 | tf_op jit(solution)/shard_map/ppermute | solution.py:365
  100.6 15.3 %all-to-all-start.1 = ((bf16[16,64,256]{2,1,0:T(8,128)(2,1)}), bf16[16,64,256]{2,1,0:T(8,128)(2,1)S(1)}, u32[]{:S(2)}, u32[]{:S(2)}) async-start(bf16[16,64,256]{2,1,0:T(8,128)(2,1)} %add_convert_fusion), calls=%async_computation.1 | async-start | bytes 1048576 | tf_op jit(solution)/shard_map/all_to_all | solution.py:395
  104.2 25.3 %collective-permute-start.17 = (bf16[4,256,256]{2,1,0:T(8,128)(2,1)}, bf16[4,256,256]{2,1,0:T(8,128)(2,1)}, u32[]{:S(2)}, u32[]{:S(2)}) collective-permute-start(bf16[4,256,256]{2,1,0:T(8,128)(2,1)} %get-tuple-element.84), channel_id=1, source_target_pairs={{0,3},{1,0},{2,1},{3,2},{4,7},{5,4},{6,5},{7,6},{8,11},{9,8},{10,9... | collective-permute-start | bytes 1572872 | tf_op jit(solution)/shard_map/ppermute | solution.py:365
  105.6 23.8 %collective-permute-start.18 = (bf16[4,256,256]{2,1,0:T(8,128)(2,1)}, bf16[4,256,256]{2,1,0:T(8,128)(2,1)}, u32[]{:S(2)}, u32[]{:S(2)}) collective-permute-start(bf16[4,256,256]{2,1,0:T(8,128)(2,1)} %get-tuple-element.86), channel_id=1, source_target_pairs={{0,1},{1,2},{2,3},{3,0},{4,5},{5,6},{6,7},{7,4},{8,9},{9,10},{10,1... | collective-permute-start | bytes 1572872 | tf_op jit(solution)/shard_map/ppermute | solution.py:365
  111.5 0.8 copy-start.11
  114.7 19.3 %collective-permute-start.16 = (bf16[4,256,256]{2,1,0:T(8,128)(2,1)}, bf16[4,256,256]{2,1,0:T(8,128)(2,1)}, u32[]{:S(2)}, u32[]{:S(2)}) collective-permute-start(bf16[4,256,256]{2,1,0:T(8,128)(2,1)} %get-tuple-element.81), channel_id=1, source_target_pairs={{0,1},{1,2},{2,3},{3,0},{4,5},{5,6},{6,7},{7,4},{8,9},{9,10},{10,1... | collective-permute-start | bytes 1572872 | tf_op jit(solution)/shard_map/ppermute | solution.py:365
  115.9 17.8 %collective-permute-start.19 = (bf16[4,256,256]{2,1,0:T(8,128)(2,1)}, bf16[4,256,256]{2,1,0:T(8,128)(2,1)}, u32[]{:S(2)}, u32[]{:S(2)}) collective-permute-start(bf16[4,256,256]{2,1,0:T(8,128)(2,1)} %get-tuple-element.87), channel_id=1, source_target_pairs={{0,3},{1,0},{2,1},{3,2},{4,7},{5,4},{6,5},{7,6},{8,11},{9,8},{10,9... | collective-permute-start | bytes 1572872 | tf_op jit(solution)/shard_map/ppermute | solution.py:365
  119.2 18.4 %all-to-all-start.2 = ((bf16[16,64,256]{2,1,0:T(8,128)(2,1)}), bf16[16,64,256]{2,1,0:T(8,128)(2,1)}, u32[]{:S(2)}, u32[]{:S(2)}) async-start(bf16[16,64,256]{2,1,0:T(8,128)(2,1)} %broadcast_in_dim.22), calls=%async_computation.2 | async-start | bytes 1048576 | tf_op jit(solution)/shard_map/all_to_all | solution.py:409
  123.5 21.1 %copy-start.2 = (bf16[256,2048]{1,0:T(8,128)(2,1)S(1)}, bf16[256,2048]{1,0:T(8,128)(2,1)}, u32[]{:S(2)}) copy-start(bf16[256,2048]{1,0:T(8,128)(2,1)} %acts_ref.3) | copy-start | bytes 3145732
  123.5 32.2 %copy-start.5 = (bf16[2048,256]{1,0:T(8,128)(2,1)S(1)}, bf16[2048,256]{1,0:T(8,128)(2,1)}, u32[]{:S(2)}) copy-start(bf16[2048,256]{1,0:T(8,128)(2,1)} %dynamic-slice_convert_fusion.refs_4_) | copy-start | bytes 3145732
  137.5 20.0 %all-to-all-start.3 = ((bf16[8,256,256]{2,1,0:T(8,128)(2,1)}), bf16[8,256,256]{2,1,0:T(8,128)(2,1)S(1)}, u32[]{:S(2)}, u32[]{:S(2)}) async-start(bf16[8,256,256]{2,1,0:T(8,128)(2,1)} %sums.3), calls=%async_computation.3 | async-start | bytes 2097152 | tf_op jit(solution)/shard_map/all_to_all | solution.py:417
  142.4 2.1 %collective-permute-start.20 = (bf16[16,64,256]{2,1,0:T(8,128)(2,1)}, bf16[16,64,256]{2,1,0:T(8,128)(2,1)S(1)}, u32[]{:S(2)}, u32[]{:S(2)}) collective-permute-start(bf16[16,64,256]{2,1,0:T(8,128)(2,1)} %all-to-all-done.2.mine_ref), channel_id=1, source_target_pairs={{0,4},{4,0},{1,5},{5,1},{2,6},{6,2},{3,7},{7,3},{8,12},{12,8},{9,1... | collective-permute-start | bytes 1572872 | tf_op jit(solution)/shard_map/ppermute | solution.py:361
  146.1 6.5 %collective-permute-start.23 = (bf16[256,256]{1,0:T(8,128)(2,1)S(1)}, bf16[256,256]{1,0:T(8,128)(2,1)S(1)}, u32[]{:S(2)}, u32[]{:S(2)}) collective-permute-start(bf16[256,256]{1,0:T(8,128)(2,1)S(1)} %convert_element_type.24.refs_0_), channel_id=1, source_target_pairs={{0,2},{1,3},{2,0},{3,1},{4,6},{5,7},{6,4},{7,5},{8,10},{9,11},{10,... | collective-permute-start | bytes 393224 | tf_op jit(solution)/shard_map/ppermute | solution.py:365
  148.8 7.0 %collective-permute-start.22 = (bf16[256,256]{1,0:T(8,128)(2,1)S(1)}, bf16[256,256]{1,0:T(8,128)(2,1)S(1)}, u32[]{:S(2)}, u32[]{:S(2)}) collective-permute-start(bf16[256,256]{1,0:T(8,128)(2,1)S(1)} %convert_element_type.24.refs_0_), channel_id=1, source_target_pairs={{0,3},{1,0},{2,1},{3,2},{4,7},{5,4},{6,5},{7,6},{8,11},{9,8},{10,9... | collective-permute-start | bytes 393224 | tf_op jit(solution)/shard_map/ppermute | solution.py:365
  149.8 5.9 %collective-permute-start.21 = (bf16[256,256]{1,0:T(8,128)(2,1)S(1)}, bf16[256,256]{1,0:T(8,128)(2,1)S(1)}, u32[]{:S(2)}, u32[]{:S(2)}) collective-permute-start(bf16[256,256]{1,0:T(8,128)(2,1)S(1)} %convert_element_type.24.refs_0_), channel_id=1, source_target_pairs={{0,1},{1,2},{2,3},{3,0},{4,5},{5,6},{6,7},{7,4},{8,9},{9,10},{10,1... | collective-permute-start | bytes 393224 | tf_op jit(solution)/shard_map/ppermute | solution.py:365

commit v4 on v3

--- a/solution.py
+++ b/solution.py
@@ -141,8 +141,8 @@
 
 
 def parts_kernel(place_ref, *refs):
-    pieces, acts, outs = refs[:5], refs[5:15], refs[15:23]
-    rows, tokens, made, row_sems, token_sems, made_sems = refs[23:]
+    pieces, acts, outs = refs[:5], refs[5:10], refs[10:14]
+    rows, tokens, made, row_sems, token_sems, made_sems = refs[14:]
     depth, size = pieces[0].shape[0], tokens.shape[1]
     half = size // 2
 
@@ -151,70 +151,49 @@
         count = pieces[n].shape[0]
         at = pl.ds(pl.multiple_of(place_ref[index] * depth + shift, count), count)
         loads.append(pltpu.make_async_copy(pieces[n], rows.at[at, :], row_sems.at[n]))
-    token_loads = []
-    for n in range(8):
-        h, k = n // 4, n % 4
-        copies = []
-        for m in range(2):
-            source = acts[5 * h + k].at[m * half : (m + 1) * half, :] if k < 3 else acts[5 * h + 3 + m]
-            target = tokens.at[n, m * half : (m + 1) * half, :]
-            copies.append(pltpu.make_async_copy(source, target, token_sems.at[n, m]))
-        token_loads.append(copies)
-
+    token_loads = [[pltpu.make_async_copy(acts[n], tokens.at[n], token_sems.at[n])] for n in range(3)]
+    token_loads.append(
+        [
+            pltpu.make_async_copy(acts[3 + m], tokens.at[3, m * half : (m + 1) * half, :], token_sems.at[3 + m])
+            for m in range(2)
+        ]
+    )
     for copy in loads + token_loads[0]:
         copy.start()
     for copy in loads:
         copy.wait()
-
-    def store(n, i, h):
-        return pltpu.make_async_copy(made.at[n, i], outs[2 * i + h].at[lax.rem(n, 4)], made_sems.at[n, i])
-
-    def body(n, carry):
-        for k in range(1, 8):
-
-            @pl.when(n == k - 1)
-            def _(k=k):
-                for copy in token_loads[k]:
-                    copy.start()
-
-        for m in range(2):
-            held = tokens.at[n, m * half : (m + 1) * half, :]
-            pltpu.make_async_copy(held, held, token_sems.at[n, m]).wait()
+    stores = []
+    for n in range(4):
+        if n < 3:
+            for copy in token_loads[n + 1]:
+                copy.start()
+        for copy in token_loads[n]:
+            copy.wait()
         part = dot(tokens[n], rows[...]).astype(BF16)
         for i in range(4):
             made[n, i] = part[:, i * 256 : (i + 1) * 256]
-        for h in range(2):
-
-            @pl.when(n // 4 == h)
-            def _(h=h):
-                for i in range(4):
-                    store(n, i, h).start()
-
-        return carry
-
-    lax.fori_loop(0, 8, body, 0)
-    for n in range(8):
-        for i in range(4):
-            store(n, i, n // 4).wait()
+            stores.append(pltpu.make_async_copy(made.at[n, i], outs[i].at[n], made_sems.at[n, i]))
+            stores[-1].start()
+    for copy in stores:
+        copy.wait()
 
 
 def parts(place, pieces, acts):
     tokens, depth = acts[0].shape
-    columns = pieces[0].shape[1]
     whole = pl.BlockSpec(memory_space=pl.ANY)
     return pl.pallas_call(
         parts_kernel,
-        in_specs=[pl.BlockSpec(memory_space=pltpu.SMEM)] + [whole] * 15,
-        out_specs=[whole] * 8,
+        in_specs=[pl.BlockSpec(memory_space=pltpu.SMEM)] + [whole] * 10,
+        out_specs=[whole] * 4,
         scratch_shapes=[
-            pltpu.VMEM((depth, columns), BF16),
-            pltpu.VMEM((8, tokens, depth), BF16),
-            pltpu.VMEM((8, 4, tokens, columns // 4), BF16),
+            pltpu.VMEM((depth, pieces[0].shape[1]), BF16),
+            pltpu.VMEM((4, tokens, depth), BF16),
+            pltpu.VMEM((4, 4, tokens, 256), BF16),
             pltpu.SemaphoreType.DMA((5,)),
-            pltpu.SemaphoreType.DMA((8, 2)),
-            pltpu.SemaphoreType.DMA((8, 4)),
+            pltpu.SemaphoreType.DMA((5,)),
+            pltpu.SemaphoreType.DMA((4, 4)),
         ],
-        out_shape=[jax.ShapeDtypeStruct((4, tokens, columns // 4), BF16)] * 8,
+        out_shape=[jax.ShapeDtypeStruct((4, tokens, 256), BF16)] * 4,
         compiler_params=pltpu.CompilerParams(vmem_limit_bytes=58 * MIB),
         name="parts",
     )(place, *pieces, *acts)
@@ -264,6 +243,31 @@
     )(*[place] * placed, *[v for g in groups for v in g])
 
 
+def step_kernel(terms_ref, one_ref, two_ref, first_ref, second_ref, direction_ref, sent_ref):
+    projected = jnp.sum(terms_ref[...].astype(F32), axis=0)
+    first = beta_one * one_ref[...] + (1.0 - beta_one) * projected
+    second = beta_two * two_ref[...] + (1.0 - beta_two) * projected * projected
+    direction = (
+        first
+        / (1.0 - beta_one**adam_step)
+        / (jnp.sqrt(second / (1.0 - beta_two**adam_step)) + epsilon)
+    )
+    first_ref[...] = first
+    second_ref[...] = second
+    direction_ref[...] = direction
+    sent_ref[...] = jnp.broadcast_to(direction.astype(BF16)[None], sent_ref.shape)
+
+
+def optimizer_step(terms, one, two):
+    shape = jax.ShapeDtypeStruct(one.shape, F32)
+    return pl.pallas_call(
+        step_kernel,
+        out_shape=[shape] * 3 + [jax.ShapeDtypeStruct(terms.shape, BF16)],
+        compiler_params=pltpu.CompilerParams(vmem_limit_bytes=16 * MIB),
+        name="optimizer_step",
+    )(terms, one, two)
+
+
 def inner_kernel(core_ref, acts_ref, mine_ref, other_ref, out_ref, rows):
     for k in range(16):
         for ref, core in ((mine_ref, core_ref[0]), (other_ref, 1 - core_ref[0])):
@@ -373,7 +377,11 @@
     own = lax.all_to_all(exchange_order(ORDER, tensor, old), ("x", "c"), 0, 0)
     got, beside = swap(give), swap(next_acts)
     rows = lax.dynamic_slice_in_dim(basis, y * 2048, 2048, axis=0).astype(BF16)
-    own, keep, got, tokens, beside, rows = lax.optimization_barrier((own, keep, got, next_acts, beside, rows))
+    place = [(v + d) % 4 for v in (z, x) for d in (0, 3, 1, 2)]
+    place = jnp.stack(place[:4] + [2 * v + c for v in place[4:]] + [2 * v + 1 - c for v in place[4:]])
+    own, keep, got, tokens, beside, rows, place = lax.optimization_barrier(
+        (own, keep, got, next_acts, beside, rows, place)
+    )
     own = own.reshape(512, 1024)
     near = (shift(own, "z", 1), shift(own, "z", -1), shift(tokens, "x", 1), shift(tokens, "x", -1))
     right, left, tr, tl = lax.optimization_barrier(near)
@@ -386,26 +394,18 @@
     pieces = (own, right, left, far_a, far_b)
     blocks = (tokens, tr, tl, ta, tb)
     others = (beside, *(swap(v) for v in blocks[1:]))
-    place = [(v + d) % 4 for v in (z, x) for d in (0, 3, 1, 2)]
-    place = jnp.stack(place[:4] + [2 * v + c for v in place[4:]] + [2 * v + 1 - c for v in place[4:]])
-    up2, down2, up1, down1, up3, down3, up0, down0 = parts(place, pieces, blocks + others)
-    got_up2, got_down2 = shift(up2, "y", 1), shift(down2, "y", -1)
-    keep, got, up2 = lax.optimization_barrier((keep, got, up2))
+    up2, up1, up3, up0 = parts(place, pieces, blocks)
+    got_up2, got_up3 = shift(up2, "y", 1), shift(up3, "y", -1)
+    down2, down1, down3, down0 = parts(place, pieces, others)
+    got_down1, got_down2 = shift(down1, "y", 1), shift(down2, "y", -1)
+    keep, got, down2 = lax.optimization_barrier((keep, got, down2))
     projected = (keep + got.astype(F32)).astype(BF16)
     projected = lax.all_to_all(projected, ("z", "x"), 0, 0)
-    got_down1, got_up3 = shift(down1, "y", 1), shift(up3, "y", -1)
+    up1, got_up3 = lax.optimization_barrier((up1, got_up3))
     up1, down3 = sums(((up1, got_up2), (down3, got_down2)))
     got_up1, got_down3 = shift(up1, "y", 1), shift(down3, "y", -1)
     projected, up1 = lax.optimization_barrier((projected, up1))
-    projected = jnp.sum(projected.astype(F32), axis=0)
-    first = beta_one * moment1[0] + (1.0 - beta_one) * projected
-    second = beta_two * moment2[0] + (1.0 - beta_two) * projected * projected
-    direction = (
-        first
-        / (1.0 - beta_one**adam_step)
-        / (jnp.sqrt(second / (1.0 - beta_two**adam_step)) + epsilon)
-    )
-    sent = jnp.broadcast_to(direction.astype(BF16)[None], (16, 64, 256))
+    first, second, direction, sent = optimizer_step(projected, moment1[0], moment2[0])
     mine = lax.all_to_all(sent, ("z", "x"), 0, 0)
     fresh = fresh_rows(direction, basis, old)
     up0, down0, fresh = lax.optimization_barrier((up0, down0, fresh))

time: 160 us -> 156 us (0.975)
  waiting for transfers between devices: 58.7 us -> 49.2 us
  starting transfers between devices: 46.3 us -> 49.8 us
  Pallas kernels: 44 us -> 47.2 us
    ppermute x17, waiting for transfers between devices: 51 us -> 44.8 us  [shift(): return lax.ppermute(value, axis, [(i, (i + by) % 4) for i in range(4)])]
    ppermute x7, waiting for transfers between devices: 5.57 us -> 2.13 us  [swap(): return lax.ppermute(value, 'c', [(0, 1), (1, 0)])]
    pallas_call x1 -> x2, Pallas kernels: 15 us -> 18.2 us  [parts(): pl.pallas_call(parts_kernel, in_specs=[pl.BlockSpec(memory_space=pltpu.SM...]
    all_to_all x1, starting transfers between devices: 4.86 us -> 6.96 us  [on_device(): part = lax.all_to_all(part, ('x', 'c'), 0, 0)]
    unnamed x28 -> x38, local copies, waits for them, and re-layouts: 2.99 us -> 3.92 us
  transfers between devices with their start and end apart: 28 -> 28, of which waited for: 16 -> 13; matrix products, arithmetic and copies ran while one was open for 4% -> 3% of each run, Pallas kernels for 17% -> 29%
where the time goes in v4:
time: 156 us; the launch traced here: 155 us
  starting transfers between devices  49.8 us (32%)
  waiting for transfers between devices  49.2 us (32%)
  Pallas kernels  47.2 us (30%)
  local copies, waits for them, and re-layouts  7.26 us (5%)
    ppermute x17, waiting for transfers between devices, shift(): return lax.ppermute(value, axis, [(i, (i + by) % 4) for i in range(4)])  44.8 us
    ppermute x17, starting transfers between devices, shift(): return lax.ppermute(value, axis, [(i, (i + by) % 4) for i in range(4)])  23.4 us
    pallas_call x2, Pallas kernels, parts(): pl.pallas_call(parts_kernel, in_specs=[pl.BlockSpec(memory_space=pltpu.SM...  18.2 us
    pallas_call x1, Pallas kernels, project(): pl.pallas_call(project_kernel, grid_spec=pltpu.PrefetchScalarGridSpec(num...  9.05 us
    all_to_all x1, starting transfers between devices, on_device(): part = lax.all_to_all(part, ('x', 'c'), 0, 0)  6.96 us
    pallas_call x1, Pallas kernels, fresh_rows(): pl.pallas_call(fresh_kernel, grid=(width // block,), in_specs=[pl.BlockSp...  5.95 us
    pallas_call x2, Pallas kernels, sums(): pl.pallas_call(functools.partial(sums_kernel, count, terms, placed), in_s...  5.88 us
    ppermute x7, starting transfers between devices, swap(): return lax.ppermute(value, 'c', [(0, 1), (1, 0)])  5.38 us
  transfers between devices with their start and end apart: 28, of which 13 were waited for; matrix products, arithmetic and copies ran while one was open for 3% of the time, Pallas kernels for 29%

profile of v4, /device:TPU:1, one launch (start us, length us, event | category | flops | bytes accessed | tf_op | source)
XLA Modules:
  0.0 155.4 jit_solution(17386621967111010646)
XLA Ops:
  0.6 1.5 collective-permute-start.1
  2.1 2.2 %exchange_order.1 = bf16[8,64,1024]{2,1,0:T(8,128)(2,1)} custom-call(s32[1]{0:T(128)} %bitcast.y_ref, bf16[64,8192]{1,0:T(8,128)(2,1)} %bitcast.21), custom_call_target="tpu_custom_call" | custom-call | tf_op jit(solution)/shard_map/exchange_order/pallas_call | solution.py:108
  4.4 4.5 %all-to-all-start = ((bf16[8,64,1024]{2,1,0:T(8,128)(2,1)}), bf16[8,64,1024]{2,1,0:T(8,128)(2,1)}, u32[]{:S(2)}, u32[]{:S(2)}) async-start(bf16[8,64,1024]{2,1,0:T(8,128)(2,1)} %exchange_order.1), calls=%async_computation | async-start | bytes 2097152 | tf_op jit(solution)/shard_map/all_to_all | solution.py:377
  8.9 1.3 copy-done.9
  10.2 9.1 %project.1 = (f32[16,64,256]{2,1,0:T(8,128)S(1)}, bf16[16,64,256]{2,1,0:T(8,128)(2,1)S(1)}) custom-call(s32[1]{0:T(128)} %bitcast.2.core_ref, bf16[256,8192]{1,0:T(8,128)(2,1)} %grad_ref.1, f32[8192,256]{1,0:T(8,128)} %basis_ref.3, bf16[256,2048]{1,0:T(8,128)(2,1)S(1)} %copy-done.9), custom_call_target="tpu_custom_call" | custom-call | tf_op jit(solution)/shard_map/project/pallas_call | solution.py:67
  19.3 1.0 copy-done.7
  20.2 0.6 stack.51.place_ref.refs_0_
  20.9 2.7 %dynamic-slice_convert_fusion.refs_4_ = bf16[2048,256]{1,0:T(8,128)(2,1)} fusion(f32[8192,256]{1,0:T(8,128)} %basis_ref.3, s32[]{:T(128)S(6)} %select_n.38), kind=kLoop, calls=%fused_computation | loop fusion | bytes 2097156 | tf_op jit(solution)/shard_map/convert_element_type | solution.py:379
  24.1 1.6 %collective-permute-start.2 = (bf16[512,1024]{1,0:T(8,128)(2,1)}, bf16[512,1024]{1,0:T(8,128)(2,1)S(1)}, u32[]{:S(2)}, u32[]{:S(2)}) collective-permute-start(bf16[512,1024]{1,0:T(8,128)(2,1)} %bitcast.15.refs_0_), channel_id=1, source_target_pairs={{0,32},{32,64},{64,96},{96,0},{1,33},{33,65},{65,97},{97,1},{2,34}... | collective-permute-start | bytes 3145736 | tf_op jit(solution)/shard_map/ppermute | solution.py:369
  25.7 3.1 %collective-permute-start.3 = (bf16[512,1024]{1,0:T(8,128)(2,1)}, bf16[512,1024]{1,0:T(8,128)(2,1)S(1)}, u32[]{:S(2)}, u32[]{:S(2)}) collective-permute-start(bf16[512,1024]{1,0:T(8,128)(2,1)} %bitcast.15.refs_0_), channel_id=1, source_target_pairs={{0,96},{32,0},{64,32},{96,64},{1,97},{33,1},{65,33},{97,65},{2,98}... | collective-permute-start | bytes 3145736 | tf_op jit(solution)/shard_map/ppermute | solution.py:369
  28.8 1.3 collective-permute-start.4
  30.1 1.4 collective-permute-start.5
  31.5 19.2 %collective-permute-done.2.first_ref.refs_1_ = bf16[512,1024]{1,0:T(8,128)(2,1)S(1)} collective-permute-done((bf16[512,1024]{1,0:T(8,128)(2,1)}, bf16[512,1024]{1,0:T(8,128)(2,1)S(1)}, u32[]{:S(2)}, u32[]{:S(2)}) %collective-permute-start.2) | collective-permute-done | bytes 1048608 | tf_op jit(solution)/shard_map/ppermute | solution.py:369
  50.7 2.8 %collective-permute-done.4.first_ref.refs_6_ = bf16[256,2048]{1,0:T(8,128)(2,1)S(1)} collective-permute-done((bf16[256,2048]{1,0:T(8,128)(2,1)S(1)}, bf16[256,2048]{1,0:T(8,128)(2,1)S(1)}, u32[]{:S(2)}, u32[]{:S(2)}) %collective-permute-start.4) | collective-permute-done | bytes 1048608 | tf_op jit(solution)/shard_map/ppermute | solution.py:369
  53.5 0.7 collective-permute-done.5.last_ref.refs_7_
  54.2 1.1 halves.2
  55.3 1.3 collective-permute-start.6
  56.5 1.5 collective-permute-start.7
  58.2 2.6 %collective-permute-start.9 = (bf16[256,1024]{1,0:T(8,128)(2,1)S(1)}, bf16[256,1024]{1,0:T(8,128)(2,1)S(1)}, u32[]{:S(2)}, u32[]{:S(2)}) collective-permute-start(bf16[256,1024]{1,0:T(8,128)(2,1)S(1)} %get-tuple-element.71), channel_id=1, source_target_pairs={{0,96},{32,0},{64,32},{96,64},{1,97},{33,1},{65,33},{97,65},{2,98}... | collective-permute-start | bytes 1572872 | tf_op jit(solution)/shard_map/ppermute | solution.py:369
  60.9 7.4 %collective-permute-done.6.refs_8_ = bf16[128,2048]{1,0:T(8,128)(2,1)} collective-permute-done((bf16[128,2048]{1,0:T(8,128)(2,1)S(1)}, bf16[128,2048]{1,0:T(8,128)(2,1)}, u32[]{:S(2)}, u32[]{:S(2)}) %collective-permute-start.6) | collective-permute-done | bytes 524320 | tf_op jit(solution)/shard_map/ppermute | solution.py:369
  68.3 2.3 %collective-permute-done.8.refs_3_ = bf16[256,1024]{1,0:T(8,128)(2,1)S(1)} collective-permute-done((bf16[256,1024]{1,0:T(8,128)(2,1)S(1)}, bf16[256,1024]{1,0:T(8,128)(2,1)S(1)}, u32[]{:S(2)}, u32[]{:S(2)}) %collective-permute-start.8) | collective-permute-done | bytes 524320 | tf_op jit(solution)/shard_map/ppermute | solution.py:369
  70.6 3.3 %collective-permute-start.10 = (bf16[256,2048]{1,0:T(8,128)(2,1)S(1)}, bf16[256,2048]{1,0:T(8,128)(2,1)}, u32[]{:S(2)}, u32[]{:S(2)}) collective-permute-start(bf16[256,2048]{1,0:T(8,128)(2,1)S(1)} %collective-permute-done.4.first_ref.refs_6_), channel_id=1, source_target_pairs={{0,4},{4,0},{1,5},{5,1},{2,6},{6,2},{3,7},{7,3},{8,12},{12,8},{9,1... | collective-permute-start | bytes 3145736 | tf_op jit(solution)/shard_map/ppermute | solution.py:365
  74.4 9.1 %parts.2 = (bf16[4,256,256]{2,1,0:T(8,128)(2,1)}, bf16[4,256,256]{2,1,0:T(8,128)(2,1)}, bf16[4,256,256]{2,1,0:T(8,128)(2,1)}, bf16[4,256,256]{2,1,0:T(8,128)(2,1)}) custom-call(s32[12]{0:T(128)} %stack.51.place_ref.refs_0_, bf16[512,1024]{1,0:T(8,128)(2,1)} %bitcast.15.refs_0_, bf16[512,1024]{1,0:T(8,128)(2,1)} %copy-done, bf16[512,1024]{1,0:T(8,128)(2,1)} %copy-done.1, ...), custom_call_target="tpu_custom_call" | custom-call | tf_op jit(solution)/shard_map/parts/pallas_call | solution.py:184
  83.6 2.8 %collective-permute-start.14 = (bf16[4,256,256]{2,1,0:T(8,128)(2,1)}, bf16[4,256,256]{2,1,0:T(8,128)(2,1)}, u32[]{:S(2)}, u32[]{:S(2)}) collective-permute-start(bf16[4,256,256]{2,1,0:T(8,128)(2,1)} %get-tuple-element.87), channel_id=1, source_target_pairs={{0,3},{1,0},{2,1},{3,2},{4,7},{5,4},{6,5},{7,6},{8,11},{9,8},{10,9... | collective-permute-start | bytes 1572872 | tf_op jit(solution)/shard_map/ppermute | solution.py:369
  86.4 0.8 copy-done.15
  87.2 9.1 %parts.3 = (bf16[4,256,256]{2,1,0:T(8,128)(2,1)}, bf16[4,256,256]{2,1,0:T(8,128)(2,1)}, bf16[4,256,256]{2,1,0:T(8,128)(2,1)}, bf16[4,256,256]{2,1,0:T(8,128)(2,1)}) custom-call(s32[12]{0:T(128)} %stack.51.place_ref.refs_0_, bf16[512,1024]{1,0:T(8,128)(2,1)} %bitcast.15.refs_0_, bf16[512,1024]{1,0:T(8,128)(2,1)} %copy-done, bf16[512,1024]{1,0:T(8,128)(2,1)} %copy-done.1, ...), custom_call_target="tpu_custom_call" | custom-call | tf_op jit(solution)/shard_map/parts/pallas_call | solution.py:184
  96.3 2.0 %collective-permute-start.16 = (bf16[4,256,256]{2,1,0:T(8,128)(2,1)}, bf16[4,256,256]{2,1,0:T(8,128)(2,1)S(1)}, u32[]{:S(2)}, u32[]{:S(2)}) collective-permute-start(bf16[4,256,256]{2,1,0:T(8,128)(2,1)} %get-tuple-element.83), channel_id=1, source_target_pairs={{0,3},{1,0},{2,1},{3,2},{4,7},{5,4},{6,5},{7,6},{8,11},{9,8},{10,9... | collective-permute-start | bytes 1572872 | tf_op jit(solution)/shard_map/ppermute | solution.py:369
  98.3 1.0 add_convert_fusion
  99.2 4.8 %all-to-all-start.1 = ((bf16[16,64,256]{2,1,0:T(8,128)(2,1)}), bf16[16,64,256]{2,1,0:T(8,128)(2,1)S(1)}, u32[]{:S(2)}, u32[]{:S(2)}) async-start(bf16[16,64,256]{2,1,0:T(8,128)(2,1)} %add_convert_fusion), calls=%async_computation.1 | async-start | bytes 1048576 | tf_op jit(solution)/shard_map/all_to_all | solution.py:403
  104.2 5.2 %collective-permute-done.16.refs_3_ = bf16[4,256,256]{2,1,0:T(8,128)(2,1)S(1)} collective-permute-done((bf16[4,256,256]{2,1,0:T(8,128)(2,1)}, bf16[4,256,256]{2,1,0:T(8,128)(2,1)S(1)}, u32[]{:S(2)}, u32[]{:S(2)}) %collective-permute-start.16) | collective-permute-done | bytes 524320 | tf_op jit(solution)/shard_map/ppermute | solution.py:369
  109.4 0.8 copy-done.18
  110.1 2.4 %sums.2 = (bf16[4,256,256]{2,1,0:T(8,128)(2,1)}, bf16[4,256,256]{2,1,0:T(8,128)(2,1)}) custom-call(bf16[4,256,256]{2,1,0:T(8,128)(2,1)} %get-tuple-element.88.refs_0_, bf16[4,256,256]{2,1,0:T(8,128)(2,1)} %collective-permute-done.15.refs_1_, bf16[4,256,256]{2,1,0:T(8,128)(2,1)} %get-tuple-element.90.refs_2_, bf16[4,256,256]{2,1,0:T(8,128)(2,1)} %copy-done.18), custom_call_target="tpu_custom_call" | custom-call | tf_op jit(solution)/shard_map/sums/pallas_call | solution.py:230
  112.8 2.7 %collective-permute-start.19 = (bf16[4,256,256]{2,1,0:T(8,128)(2,1)}, bf16[4,256,256]{2,1,0:T(8,128)(2,1)}, u32[]{:S(2)}, u32[]{:S(2)}) collective-permute-start(bf16[4,256,256]{2,1,0:T(8,128)(2,1)} %get-tuple-element.98), channel_id=1, source_target_pairs={{0,3},{1,0},{2,1},{3,2},{4,7},{5,4},{6,5},{7,6},{8,11},{9,8},{10,9... | collective-permute-start | bytes 1572872 | tf_op jit(solution)/shard_map/ppermute | solution.py:369
  115.5 1.0 optimizer_step.1
  116.5 4.8 %all-to-all-start.2 = ((bf16[16,64,256]{2,1,0:T(8,128)(2,1)}), bf16[16,64,256]{2,1,0:T(8,128)(2,1)}, u32[]{:S(2)}, u32[]{:S(2)}) async-start(bf16[16,64,256]{2,1,0:T(8,128)(2,1)} %get-tuple-element.99), calls=%async_computation.2 | async-start | bytes 1048576 | tf_op jit(solution)/shard_map/all_to_all | solution.py:409
  121.3 5.9 %fresh_rows.1 = bf16[64,8192]{1,0:T(8,128)(2,1)} custom-call(f32[64,256]{1,0:T(8,128)S(1)} %get-tuple-element.93.direction_ref, f32[8192,256]{1,0:T(8,128)} %basis_ref.3, bf16[64,8192]{1,0:T(8,128)(2,1)S(1)} %bitcast.22), custom_call_target="tpu_custom_call" | custom-call | tf_op jit(solution)/shard_map/fresh_rows/pallas_call | solution.py:128
  127.3 1.4 collective-permute-done.17.refs_2_
  128.7 3.5 %sums.3 = bf16[8,256,256]{2,1,0:T(8,128)(2,1)} custom-call(s32[12]{0:T(128)} %stack.51.place_ref.refs_0_, bf16[4,256,256]{2,1,0:T(8,128)(2,1)} %get-tuple-element.94.refs_1_, bf16[4,256,256]{2,1,0:T(8,128)(2,1)} %collective-permute-done.17.refs_2_, bf16[4,256,256]{2,1,0:T(8,128)(2,1)} %collective-permute-done.14.refs_3_, ...), custom_call_target="tpu_custom_call" | custom-call | tf_op jit(solution)/shard_map/sums/pallas_call | solution.py:230
  132.2 7.0 %all-to-all-start.3 = ((bf16[8,256,256]{2,1,0:T(8,128)(2,1)}), bf16[8,256,256]{2,1,0:T(8,128)(2,1)S(1)}, u32[]{:S(2)}, u32[]{:S(2)}) async-start(bf16[8,256,256]{2,1,0:T(8,128)(2,1)} %sums.3), calls=%async_computation.3 | async-start | bytes 2097152 | tf_op jit(solution)/shard_map/all_to_all | solution.py:417
  139.1 2.1 %collective-permute-done.20.other_ref = bf16[16,64,256]{2,1,0:T(8,128)(2,1)S(1)} collective-permute-done((bf16[16,64,256]{2,1,0:T(8,128)(2,1)}, bf16[16,64,256]{2,1,0:T(8,128)(2,1)S(1)}, u32[]{:S(2)}, u32[]{:S(2)}) %collective-permute-start.20) | collective-permute-done | bytes 524320 | tf_op jit(solution)/shard_map/ppermute | solution.py:365
  141.3 1.5 inner.1
  142.9 2.7 %collective-permute-start.22 = (bf16[256,256]{1,0:T(8,128)(2,1)S(1)}, bf16[256,256]{1,0:T(8,128)(2,1)S(1)}, u32[]{:S(2)}, u32[]{:S(2)}) collective-permute-start(bf16[256,256]{1,0:T(8,128)(2,1)S(1)} %convert_element_type.15.refs_0_), channel_id=1, source_target_pairs={{0,3},{1,0},{2,1},{3,2},{4,7},{5,4},{6,5},{7,6},{8,11},{9,8},{10,9... | collective-permute-start | bytes 393224 | tf_op jit(solution)/shard_map/ppermute | solution.py:369
  145.6 3.5 %collective-permute-done.21.refs_1_ = bf16[256,256]{1,0:T(8,128)(2,1)S(1)} collective-permute-done((bf16[256,256]{1,0:T(8,128)(2,1)S(1)}, bf16[256,256]{1,0:T(8,128)(2,1)S(1)}, u32[]{:S(2)}, u32[]{:S(2)}) %collective-permute-start.21) | collective-permute-done | bytes 131104 | tf_op jit(solution)/shard_map/ppermute | solution.py:369
  149.1 1.7 %collective-permute-done.22.refs_2_ = bf16[256,256]{1,0:T(8,128)(2,1)S(1)} collective-permute-done((bf16[256,256]{1,0:T(8,128)(2,1)S(1)}, bf16[256,256]{1,0:T(8,128)(2,1)S(1)}, u32[]{:S(2)}, u32[]{:S(2)}) %collective-permute-start.22) | collective-permute-done | bytes 131104 | tf_op jit(solution)/shard_map/ppermute | solution.py:369
  150.7 0.7 collective-permute-done.23.refs_3_
  151.4 1.0 change.1.change_ref
  152.4 1.8 %all-to-all-done.3.part_ref = bf16[8,256,256]{2,1,0:T(8,128)(2,1)S(1)} async-done(((bf16[8,256,256]{2,1,0:T(8,128)(2,1)}), bf16[8,256,256]{2,1,0:T(8,128)(2,1)S(1)}, u32[]{:S(2)}, u32[]{:S(2)}) %all-to-all-start.3) | async-done | bytes 1048608 | tf_op jit(solution)/shard_map/all_to_all | solution.py:417
  154.2 1.2 output_rows.1
  (63 shorter events, 1.8 us)
Async XLA Ops:
  0.6 23.4 %collective-permute-start.1 = (bf16[256,2048]{1,0:T(8,128)(2,1)}, bf16[256,2048]{1,0:T(8,128)(2,1)S(1)}, u32[]{:S(2)}, u32[]{:S(2)}) collective-permute-start(bf16[256,2048]{1,0:T(8,128)(2,1)} %acts_ref.3), channel_id=1, source_target_pairs={{0,4},{4,0},{1,5},{5,1},{2,6},{6,2},{3,7},{7,3},{8,12},{12,8},{9,1... | collective-permute-start | bytes 3145736 | tf_op jit(solution)/shard_map/ppermute | solution.py:365
  4.4 19.7 %all-to-all-start = ((bf16[8,64,1024]{2,1,0:T(8,128)(2,1)}), bf16[8,64,1024]{2,1,0:T(8,128)(2,1)}, u32[]{:S(2)}, u32[]{:S(2)}) async-start(bf16[8,64,1024]{2,1,0:T(8,128)(2,1)} %exchange_order.1), calls=%async_computation | async-start | bytes 2097152 | tf_op jit(solution)/shard_map/all_to_all | solution.py:377
  8.9 19.9 %copy-start.3 = (bf16[256,2048]{1,0:T(8,128)(2,1)S(1)}, bf16[256,2048]{1,0:T(8,128)(2,1)}, u32[]{:S(2)}) copy-start(bf16[256,2048]{1,0:T(8,128)(2,1)} %acts_ref.3) | copy-start | bytes 3145732
  8.9 1.3 copy-start.9
  19.2 1.0 copy-start.7
  20.2 3.4 %collective-permute-start = (bf16[16,64,256]{2,1,0:T(8,128)(2,1)S(1)}, bf16[16,64,256]{2,1,0:T(8,128)(2,1)S(1)}, u32[]{:S(2)}, u32[]{:S(2)}) collective-permute-start(bf16[16,64,256]{2,1,0:T(8,128)(2,1)S(1)} %get-tuple-element.56), channel_id=1, source_target_pairs={{0,4},{4,0},{1,5},{5,1},{2,6},{6,2},{3,7},{7,3},{8,12},{12,8},{9,1... | collective-permute-start | bytes 1572872 | tf_op jit(solution)/shard_map/ppermute | solution.py:365
  23.6 34.6 %copy-start.16 = (bf16[16,64,256]{2,1,0:T(8,128)(2,1)}, bf16[16,64,256]{2,1,0:T(8,128)(2,1)S(1)}, u32[]{:S(2)}) copy-start(bf16[16,64,256]{2,1,0:T(8,128)(2,1)S(1)} %collective-permute-done) | copy-start | bytes 1572868
  24.1 1.6 %copy-start.14 = (bf16[256,2048]{1,0:T(8,128)(2,1)}, bf16[256,2048]{1,0:T(8,128)(2,1)S(1)}, u32[]{:S(2)}) copy-start(bf16[256,2048]{1,0:T(8,128)(2,1)S(1)} %collective-permute-done.1.refs_5_) | copy-start | bytes 3145732
  24.1 26.6 %collective-permute-start.2 = (bf16[512,1024]{1,0:T(8,128)(2,1)}, bf16[512,1024]{1,0:T(8,128)(2,1)S(1)}, u32[]{:S(2)}, u32[]{:S(2)}) collective-permute-start(bf16[512,1024]{1,0:T(8,128)(2,1)} %bitcast.15.refs_0_), channel_id=1, source_target_pairs={{0,32},{32,64},{64,96},{96,0},{1,33},{33,65},{65,97},{97,1},{2,34}... | collective-permute-start | bytes 3145736 | tf_op jit(solution)/shard_map/ppermute | solution.py:369
  25.7 25.0 %collective-permute-start.3 = (bf16[512,1024]{1,0:T(8,128)(2,1)}, bf16[512,1024]{1,0:T(8,128)(2,1)S(1)}, u32[]{:S(2)}, u32[]{:S(2)}) collective-permute-start(bf16[512,1024]{1,0:T(8,128)(2,1)} %bitcast.15.refs_0_), channel_id=1, source_target_pairs={{0,96},{32,0},{64,32},{96,64},{1,97},{33,1},{65,33},{97,65},{2,98}... | collective-permute-start | bytes 3145736 | tf_op jit(solution)/shard_map/ppermute | solution.py:369
  28.8 24.7 %collective-permute-start.4 = (bf16[256,2048]{1,0:T(8,128)(2,1)S(1)}, bf16[256,2048]{1,0:T(8,128)(2,1)S(1)}, u32[]{:S(2)}, u32[]{:S(2)}) collective-permute-start(bf16[256,2048]{1,0:T(8,128)(2,1)S(1)} %copy-done.3), channel_id=1, source_target_pairs={{0,8},{8,16},{16,24},{24,0},{1,9},{9,17},{17,25},{25,1},{2,10},{10... | collective-permute-start | bytes 3145736 | tf_op jit(solution)/shard_map/ppermute | solution.py:369
  30.1 24.1 %collective-permute-start.5 = (bf16[256,2048]{1,0:T(8,128)(2,1)S(1)}, bf16[256,2048]{1,0:T(8,128)(2,1)}, u32[]{:S(2)}, u32[]{:S(2)}) collective-permute-start(bf16[256,2048]{1,0:T(8,128)(2,1)S(1)} %copy-done.3), channel_id=1, source_target_pairs={{0,24},{8,0},{16,8},{24,16},{1,25},{9,1},{17,9},{25,17},{2,26},{10... | collective-permute-start | bytes 3145736 | tf_op jit(solution)/shard_map/ppermute | solution.py:369
  50.7 23.7 %copy-start = (bf16[512,1024]{1,0:T(8,128)(2,1)}, bf16[512,1024]{1,0:T(8,128)(2,1)S(1)}, u32[]{:S(2)}) copy-start(bf16[512,1024]{1,0:T(8,128)(2,1)S(1)} %collective-permute-done.2.first_ref.refs_1_) | copy-start | bytes 3145732
  50.7 23.7 %copy-start.1 = (bf16[512,1024]{1,0:T(8,128)(2,1)}, bf16[512,1024]{1,0:T(8,128)(2,1)S(1)}, u32[]{:S(2)}) copy-start(bf16[512,1024]{1,0:T(8,128)(2,1)S(1)} %collective-permute-done.3.last_ref.refs_2_) | copy-start | bytes 3145732
  53.5 20.9 %copy-start.5 = (bf16[256,2048]{1,0:T(8,128)(2,1)}, bf16[256,2048]{1,0:T(8,128)(2,1)S(1)}, u32[]{:S(2)}) copy-start(bf16[256,2048]{1,0:T(8,128)(2,1)S(1)} %collective-permute-done.4.first_ref.refs_6_) | copy-start | bytes 3145732
  55.3 13.0 %collective-permute-start.6 = (bf16[128,2048]{1,0:T(8,128)(2,1)S(1)}, bf16[128,2048]{1,0:T(8,128)(2,1)}, u32[]{:S(2)}, u32[]{:S(2)}) collective-permute-start(bf16[128,2048]{1,0:T(8,128)(2,1)S(1)} %get-tuple-element.68), channel_id=1, source_target_pairs={{0,8},{8,16},{16,24},{24,0},{1,9},{9,17},{17,25},{25,1},{2,10},{10... | collective-permute-start | bytes 1572872 | tf_op jit(solution)/shard_map/ppermute | solution.py:369
  56.5 11.7 %collective-permute-start.7 = (bf16[128,2048]{1,0:T(8,128)(2,1)S(1)}, bf16[128,2048]{1,0:T(8,128)(2,1)}, u32[]{:S(2)}, u32[]{:S(2)}) collective-permute-start(bf16[128,2048]{1,0:T(8,128)(2,1)S(1)} %get-tuple-element.69), channel_id=1, source_target_pairs={{0,24},{8,0},{16,8},{24,16},{1,25},{9,1},{17,9},{25,17},{2,26},{10... | collective-permute-start | bytes 1572872 | tf_op jit(solution)/shard_map/ppermute | solution.py:369
  58.1 12.4 %collective-permute-start.8 = (bf16[256,1024]{1,0:T(8,128)(2,1)S(1)}, bf16[256,1024]{1,0:T(8,128)(2,1)S(1)}, u32[]{:S(2)}, u32[]{:S(2)}) collective-permute-start(bf16[256,1024]{1,0:T(8,128)(2,1)S(1)} %get-tuple-element.70), channel_id=1, source_target_pairs={{0,32},{32,64},{64,96},{96,0},{1,33},{33,65},{65,97},{97,1},{2,34}... | collective-permute-start | bytes 1572872 | tf_op jit(solution)/shard_map/ppermute | solution.py:369
  58.2 40.1 %copy-start.8 = (f32[16,64,256]{2,1,0:T(8,128)S(1)}, f32[16,64,256]{2,1,0:T(8,128)}, u32[]{:S(2)}) copy-start(f32[16,64,256]{2,1,0:T(8,128)} %copy-done.7) | copy-start | bytes 3145732
  58.2 12.3 %collective-permute-start.9 = (bf16[256,1024]{1,0:T(8,128)(2,1)S(1)}, bf16[256,1024]{1,0:T(8,128)(2,1)S(1)}, u32[]{:S(2)}, u32[]{:S(2)}) collective-permute-start(bf16[256,1024]{1,0:T(8,128)(2,1)S(1)} %get-tuple-element.71), channel_id=1, source_target_pairs={{0,96},{32,0},{64,32},{96,64},{1,97},{33,1},{65,33},{97,65},{2,98}... | collective-permute-start | bytes 1572872 | tf_op jit(solution)/shard_map/ppermute | solution.py:369
  70.5 3.9 %copy-start.12 = (bf16[256,1024]{1,0:T(8,128)(2,1)}, bf16[256,1024]{1,0:T(8,128)(2,1)S(1)}, u32[]{:S(2)}) copy-start(bf16[256,1024]{1,0:T(8,128)(2,1)S(1)} %collective-permute-done.8.refs_3_) | copy-start | bytes 1572868
  70.5 3.9 %copy-start.13 = (bf16[256,1024]{1,0:T(8,128)(2,1)}, bf16[256,1024]{1,0:T(8,128)(2,1)S(1)}, u32[]{:S(2)}) copy-start(bf16[256,1024]{1,0:T(8,128)(2,1)S(1)} %collective-permute-done.9.refs_4_) | copy-start | bytes 1572868
  70.6 15.9 %collective-permute-start.10 = (bf16[256,2048]{1,0:T(8,128)(2,1)S(1)}, bf16[256,2048]{1,0:T(8,128)(2,1)}, u32[]{:S(2)}, u32[]{:S(2)}) collective-permute-start(bf16[256,2048]{1,0:T(8,128)(2,1)S(1)} %collective-permute-done.4.first_ref.refs_6_), channel_id=1, source_target_pairs={{0,4},{4,0},{1,5},{5,1},{2,6},{6,2},{3,7},{7,3},{8,12},{12,8},{9,1... | collective-permute-start | bytes 3145736 | tf_op jit(solution)/shard_map/ppermute | solution.py:365
  73.8 12.6 %collective-permute-start.11 = (bf16[256,2048]{1,0:T(8,128)(2,1)}, bf16[256,2048]{1,0:T(8,128)(2,1)}, u32[]{:S(2)}, u32[]{:S(2)}) collective-permute-start(bf16[256,2048]{1,0:T(8,128)(2,1)} %collective-permute-done.5.last_ref.refs_7_), channel_id=1, source_target_pairs={{0,4},{4,0},{1,5},{5,1},{2,6},{6,2},{3,7},{7,3},{8,12},{12,8},{9,1... | collective-permute-start | bytes 3145736 | tf_op jit(solution)/shard_map/ppermute | solution.py:365
  73.9 12.5 %collective-permute-start.12 = (bf16[128,2048]{1,0:T(8,128)(2,1)}, bf16[128,2048]{1,0:T(8,128)(2,1)S(1)}, u32[]{:S(2)}, u32[]{:S(2)}) collective-permute-start(bf16[128,2048]{1,0:T(8,128)(2,1)} %collective-permute-done.6.refs_8_), channel_id=1, source_target_pairs={{0,4},{4,0},{1,5},{5,1},{2,6},{6,2},{3,7},{7,3},{8,12},{12,8},{9,1... | collective-permute-start | bytes 1572872 | tf_op jit(solution)/shard_map/ppermute | solution.py:365
  74.3 12.1 %collective-permute-start.13 = (bf16[128,2048]{1,0:T(8,128)(2,1)}, bf16[128,2048]{1,0:T(8,128)(2,1)}, u32[]{:S(2)}, u32[]{:S(2)}) collective-permute-start(bf16[128,2048]{1,0:T(8,128)(2,1)} %collective-permute-done.7.refs_9_), channel_id=1, source_target_pairs={{0,4},{4,0},{1,5},{5,1},{2,6},{6,2},{3,7},{7,3},{8,12},{12,8},{9,1... | collective-permute-start | bytes 1572872 | tf_op jit(solution)/shard_map/ppermute | solution.py:365
  83.5 14.7 %copy-start.17 = (bf16[16,64,256]{2,1,0:T(8,128)(2,1)S(1)}, bf16[16,64,256]{2,1,0:T(8,128)(2,1)}, u32[]{:S(2)}) copy-start(bf16[16,64,256]{2,1,0:T(8,128)(2,1)} %copy-done.16) | copy-start | bytes 1572868
  83.6 32.0 %copy-start.10 = (f32[1,64,256]{2,1,0:T(8,128)S(1)}, f32[1,64,256]{2,1,0:T(8,128)}, u32[]{:S(2)}) copy-start(f32[1,64,256]{2,1,0:T(8,128)} %param.10) | copy-start | bytes 196612
  83.6 32.0 %copy-start.11 = (f32[1,64,256]{2,1,0:T(8,128)S(1)}, f32[1,64,256]{2,1,0:T(8,128)}, u32[]{:S(2)}) copy-start(f32[1,64,256]{2,1,0:T(8,128)} %param.11) | copy-start | bytes 196612
  83.6 37.7 %copy-start.2 = (bf16[1,64,8192]{2,1,0:T(8,128)(2,1)S(1)}, bf16[1,64,8192]{2,1,0:T(8,128)(2,1)}, u32[]{:S(2)}) copy-start(bf16[1,64,8192]{2,1,0:T(8,128)(2,1)} %param.12) | copy-start | bytes 3145732
  83.6 20.5 %collective-permute-start.14 = (bf16[4,256,256]{2,1,0:T(8,128)(2,1)}, bf16[4,256,256]{2,1,0:T(8,128)(2,1)}, u32[]{:S(2)}, u32[]{:S(2)}) collective-permute-start(bf16[4,256,256]{2,1,0:T(8,128)(2,1)} %get-tuple-element.87), channel_id=1, source_target_pairs={{0,3},{1,0},{2,1},{3,2},{4,7},{5,4},{6,5},{7,6},{8,11},{9,8},{10,9... | collective-permute-start | bytes 1572872 | tf_op jit(solution)/shard_map/ppermute | solution.py:369
  86.4 0.8 copy-start.15
  86.4 17.8 %collective-permute-start.15 = (bf16[4,256,256]{2,1,0:T(8,128)(2,1)}, bf16[4,256,256]{2,1,0:T(8,128)(2,1)}, u32[]{:S(2)}, u32[]{:S(2)}) collective-permute-start(bf16[4,256,256]{2,1,0:T(8,128)(2,1)} %get-tuple-element.89), channel_id=1, source_target_pairs={{0,1},{1,2},{2,3},{3,0},{4,5},{5,6},{6,7},{7,4},{8,9},{9,10},{10,1... | collective-permute-start | bytes 1572872 | tf_op jit(solution)/shard_map/ppermute | solution.py:369
  96.3 13.0 %collective-permute-start.16 = (bf16[4,256,256]{2,1,0:T(8,128)(2,1)}, bf16[4,256,256]{2,1,0:T(8,128)(2,1)S(1)}, u32[]{:S(2)}, u32[]{:S(2)}) collective-permute-start(bf16[4,256,256]{2,1,0:T(8,128)(2,1)} %get-tuple-element.83), channel_id=1, source_target_pairs={{0,3},{1,0},{2,1},{3,2},{4,7},{5,4},{6,5},{7,6},{8,11},{9,8},{10,9... | collective-permute-start | bytes 1572872 | tf_op jit(solution)/shard_map/ppermute | solution.py:369
  99.2 16.3 %all-to-all-start.1 = ((bf16[16,64,256]{2,1,0:T(8,128)(2,1)}), bf16[16,64,256]{2,1,0:T(8,128)(2,1)S(1)}, u32[]{:S(2)}, u32[]{:S(2)}) async-start(bf16[16,64,256]{2,1,0:T(8,128)(2,1)} %add_convert_fusion), calls=%async_computation.1 | async-start | bytes 1048576 | tf_op jit(solution)/shard_map/all_to_all | solution.py:403
  104.1 23.2 %collective-permute-start.18 = (bf16[4,256,256]{2,1,0:T(8,128)(2,1)}, bf16[4,256,256]{2,1,0:T(8,128)(2,1)}, u32[]{:S(2)}, u32[]{:S(2)}) collective-permute-start(bf16[4,256,256]{2,1,0:T(8,128)(2,1)} %get-tuple-element.97), channel_id=1, source_target_pairs={{0,1},{1,2},{2,3},{3,0},{4,5},{5,6},{6,7},{7,4},{8,9},{9,10},{10,1... | collective-permute-start | bytes 1572872 | tf_op jit(solution)/shard_map/ppermute | solution.py:369
  109.3 0.8 copy-start.18
  112.6 16.1 %collective-permute-start.17 = (bf16[4,256,256]{2,1,0:T(8,128)(2,1)}, bf16[4,256,256]{2,1,0:T(8,128)(2,1)}, u32[]{:S(2)}, u32[]{:S(2)}) collective-permute-start(bf16[4,256,256]{2,1,0:T(8,128)(2,1)} %get-tuple-element.91), channel_id=1, source_target_pairs={{0,1},{1,2},{2,3},{3,0},{4,5},{5,6},{6,7},{7,4},{8,9},{9,10},{10,1... | collective-permute-start | bytes 1572872 | tf_op jit(solution)/shard_map/ppermute | solution.py:369
  112.8 15.9 %collective-permute-start.19 = (bf16[4,256,256]{2,1,0:T(8,128)(2,1)}, bf16[4,256,256]{2,1,0:T(8,128)(2,1)}, u32[]{:S(2)}, u32[]{:S(2)}) collective-permute-start(bf16[4,256,256]{2,1,0:T(8,128)(2,1)} %get-tuple-element.98), channel_id=1, source_target_pairs={{0,3},{1,0},{2,1},{3,2},{4,7},{5,4},{6,5},{7,6},{8,11},{9,8},{10,9... | collective-permute-start | bytes 1572872 | tf_op jit(solution)/shard_map/ppermute | solution.py:369
  116.5 15.7 %all-to-all-start.2 = ((bf16[16,64,256]{2,1,0:T(8,128)(2,1)}), bf16[16,64,256]{2,1,0:T(8,128)(2,1)}, u32[]{:S(2)}, u32[]{:S(2)}) async-start(bf16[16,64,256]{2,1,0:T(8,128)(2,1)} %get-tuple-element.99), calls=%async_computation.2 | async-start | bytes 1048576 | tf_op jit(solution)/shard_map/all_to_all | solution.py:409
  121.3 20.0 %copy-start.4 = (bf16[256,2048]{1,0:T(8,128)(2,1)S(1)}, bf16[256,2048]{1,0:T(8,128)(2,1)}, u32[]{:S(2)}) copy-start(bf16[256,2048]{1,0:T(8,128)(2,1)} %acts_ref.3) | copy-start | bytes 3145732
  121.3 30.1 %copy-start.6 = (bf16[2048,256]{1,0:T(8,128)(2,1)S(1)}, bf16[2048,256]{1,0:T(8,128)(2,1)}, u32[]{:S(2)}) copy-start(bf16[2048,256]{1,0:T(8,128)(2,1)} %dynamic-slice_convert_fusion.refs_4_) | copy-start | bytes 3145732
  132.2 22.1 %all-to-all-start.3 = ((bf16[8,256,256]{2,1,0:T(8,128)(2,1)}), bf16[8,256,256]{2,1,0:T(8,128)(2,1)S(1)}, u32[]{:S(2)}, u32[]{:S(2)}) async-start(bf16[8,256,256]{2,1,0:T(8,128)(2,1)} %sums.3), calls=%async_computation.3 | async-start | bytes 2097152 | tf_op jit(solution)/shard_map/all_to_all | solution.py:417
  139.1 2.1 %collective-permute-start.20 = (bf16[16,64,256]{2,1,0:T(8,128)(2,1)}, bf16[16,64,256]{2,1,0:T(8,128)(2,1)S(1)}, u32[]{:S(2)}, u32[]{:S(2)}) collective-permute-start(bf16[16,64,256]{2,1,0:T(8,128)(2,1)} %all-to-all-done.2.mine_ref), channel_id=1, source_target_pairs={{0,4},{4,0},{1,5},{5,1},{2,6},{6,2},{3,7},{7,3},{8,12},{12,8},{9,1... | collective-permute-start | bytes 1572872 | tf_op jit(solution)/shard_map/ppermute | solution.py:365
  142.8 6.2 %collective-permute-start.21 = (bf16[256,256]{1,0:T(8,128)(2,1)S(1)}, bf16[256,256]{1,0:T(8,128)(2,1)S(1)}, u32[]{:S(2)}, u32[]{:S(2)}) collective-permute-start(bf16[256,256]{1,0:T(8,128)(2,1)S(1)} %convert_element_type.15.refs_0_), channel_id=1, source_target_pairs={{0,1},{1,2},{2,3},{3,0},{4,5},{5,6},{6,7},{7,4},{8,9},{9,10},{10,1... | collective-permute-start | bytes 393224 | tf_op jit(solution)/shard_map/ppermute | solution.py:369
  142.9 7.8 %collective-permute-start.22 = (bf16[256,256]{1,0:T(8,128)(2,1)S(1)}, bf16[256,256]{1,0:T(8,128)(2,1)S(1)}, u32[]{:S(2)}, u32[]{:S(2)}) collective-permute-start(bf16[256,256]{1,0:T(8,128)(2,1)S(1)} %convert_element_type.15.refs_0_), channel_id=1, source_target_pairs={{0,3},{1,0},{2,1},{3,2},{4,7},{5,4},{6,5},{7,6},{8,11},{9,8},{10,9... | collective-permute-start | bytes 393224 | tf_op jit(solution)/shard_map/ppermute | solution.py:369
  145.6 5.8 %collective-permute-start.23 = (bf16[256,256]{1,0:T(8,128)(2,1)S(1)}, bf16[256,256]{1,0:T(8,128)(2,1)S(1)}, u32[]{:S(2)}, u32[]{:S(2)}) collective-permute-start(bf16[256,256]{1,0:T(8,128)(2,1)S(1)} %convert_element_type.15.refs_0_), channel_id=1, source_target_pairs={{0,2},{1,3},{2,0},{3,1},{4,6},{5,7},{6,4},{7,5},{8,10},{9,11},{10,... | collective-permute-start | bytes 393224 | tf_op jit(solution)/shard_map/ppermute | solution.py:369

commit v5 on v4

--- a/solution.py
+++ b/solution.py
@@ -376,15 +376,16 @@
     keep, give = project(core, acts, out_grad, basis)
     own = lax.all_to_all(exchange_order(ORDER, tensor, old), ("x", "c"), 0, 0)
     got, beside = swap(give), swap(next_acts)
-    rows = lax.dynamic_slice_in_dim(basis, y * 2048, 2048, axis=0).astype(BF16)
     place = [(v + d) % 4 for v in (z, x) for d in (0, 3, 1, 2)]
     place = jnp.stack(place[:4] + [2 * v + c for v in place[4:]] + [2 * v + 1 - c for v in place[4:]])
-    own, keep, got, tokens, beside, rows, place = lax.optimization_barrier(
-        (own, keep, got, next_acts, beside, rows, place)
+    keep, got, tokens, beside, place, rows = lax.optimization_barrier(
+        (keep, got, next_acts, beside, place, basis)
     )
     own = own.reshape(512, 1024)
     near = (shift(own, "z", 1), shift(own, "z", -1), shift(tokens, "x", 1), shift(tokens, "x", -1))
-    right, left, tr, tl = lax.optimization_barrier(near)
+    rows = lax.dynamic_slice_in_dim(rows, y * 2048, 2048, axis=0).astype(BF16)
+    projected = (keep + got.astype(F32)).astype(BF16)
+    right, left, tr, tl, rows, projected = lax.optimization_barrier((*near, rows, projected))
     ta, tb = halves(tr, tl)
     ta, tb, right, left = lax.optimization_barrier((ta, tb, right, left))
     near_a, near_b = halves(right, left)
@@ -398,8 +399,7 @@
     got_up2, got_up3 = shift(up2, "y", 1), shift(up3, "y", -1)
     down2, down1, down3, down0 = parts(place, pieces, others)
     got_down1, got_down2 = shift(down1, "y", 1), shift(down2, "y", -1)
-    keep, got, down2 = lax.optimization_barrier((keep, got, down2))
-    projected = (keep + got.astype(F32)).astype(BF16)
+    projected, down2 = lax.optimization_barrier((projected, down2))
     projected = lax.all_to_all(projected, ("z", "x"), 0, 0)
     up1, got_up3 = lax.optimization_barrier((up1, got_up3))
     up1, down3 = sums(((up1, got_up2), (down3, got_down2)))

time: 156 us -> 155 us (level)
  waiting for transfers between devices: 49.2 us -> 45.7 us
    ppermute x17, waiting for transfers between devices: 44.8 us -> 39.2 us  [shift(): return lax.ppermute(value, axis, [(i, (i + by) % 4) for i in range(4)])]
    all_to_all x1, waiting for transfers between devices: 0.49 us -> 2.55 us  [on_device(): own = lax.all_to_all(exchange_order(ORDER, tensor, old), ('x', 'c'), 0, 0)]
    unnamed x38 -> x34, local copies, waits for them, and re-layouts: 3.92 us -> 3.44 us
  transfers between devices with their start and end apart: 28 -> 28, of which waited for: 13 -> 12; matrix products, arithmetic and copies ran while one was open for 3% -> 4% of each run, Pallas kernels for 29% -> 30%
where the time goes in v5:
time: 155 us; the launch traced here: 154 us
  starting transfers between devices  50.4 us (33%)
  Pallas kernels  48.1 us (31%)
  waiting for transfers between devices  45.7 us (29%)
  local copies, waits for them, and re-layouts  6.78 us (4%)
  other arithmetic  2.31 us (1%)
    ppermute x17, waiting for transfers between devices, shift(): return lax.ppermute(value, axis, [(i, (i + by) % 4) for i in range(4)])  39.2 us
    ppermute x17, starting transfers between devices, shift(): return lax.ppermute(value, axis, [(i, (i + by) % 4) for i in range(4)])  23.6 us
    pallas_call x2, Pallas kernels, parts(): pl.pallas_call(parts_kernel, in_specs=[pl.BlockSpec(memory_space=pltpu.SM...  18.2 us
    pallas_call x1, Pallas kernels, project(): pl.pallas_call(project_kernel, grid_spec=pltpu.PrefetchScalarGridSpec(num...  9.82 us
    all_to_all x1, starting transfers between devices, on_device(): part = lax.all_to_all(part, ('x', 'c'), 0, 0)  6.96 us
    pallas_call x1, Pallas kernels, fresh_rows(): pl.pallas_call(fresh_kernel, grid=(width // block,), in_specs=[pl.BlockSp...  5.95 us
    pallas_call x2, Pallas kernels, sums(): pl.pallas_call(functools.partial(sums_kernel, count, terms, placed), in_s...  5.89 us
    ppermute x7, starting transfers between devices, swap(): return lax.ppermute(value, 'c', [(0, 1), (1, 0)])  5.63 us
  transfers between devices with their start and end apart: 28, of which 12 were waited for; matrix products, arithmetic and copies ran while one was open for 4% of the time, Pallas kernels for 30%

profile of v5, /device:TPU:1, one launch (start us, length us, event | category | flops | bytes accessed | tf_op | source)
XLA Modules:
  0.0 154.2 jit_solution(6879598664334235838)
XLA Ops:
  0.6 1.5 collective-permute-start.1
  2.1 2.2 %exchange_order.1 = bf16[8,64,1024]{2,1,0:T(8,128)(2,1)} custom-call(s32[1]{0:T(128)} %bitcast.13.y_ref, bf16[64,8192]{1,0:T(8,128)(2,1)} %bitcast.21), custom_call_target="tpu_custom_call" | custom-call | tf_op jit(solution)/shard_map/exchange_order/pallas_call | solution.py:108
  4.4 4.6 %all-to-all-start = ((bf16[8,64,1024]{2,1,0:T(8,128)(2,1)}), bf16[8,64,1024]{2,1,0:T(8,128)(2,1)}, u32[]{:S(2)}, u32[]{:S(2)}) async-start(bf16[8,64,1024]{2,1,0:T(8,128)(2,1)} %exchange_order.1), calls=%async_computation | async-start | bytes 2097152 | tf_op jit(solution)/shard_map/all_to_all | solution.py:377
  9.0 1.2 copy-done.7
  10.2 9.8 %project.1 = (f32[16,64,256]{2,1,0:T(8,128)S(1)}, bf16[16,64,256]{2,1,0:T(8,128)(2,1)}) custom-call(s32[1]{0:T(128)} %bitcast.core_ref, bf16[256,8192]{1,0:T(8,128)(2,1)} %grad_ref.1, f32[8192,256]{1,0:T(8,128)} %basis_ref.3, bf16[256,2048]{1,0:T(8,128)(2,1)S(1)} %copy-done.7), custom_call_target="tpu_custom_call" | custom-call | tf_op jit(solution)/shard_map/project/pallas_call | solution.py:67
  20.1 1.0 copy-done.6
  21.0 0.6 stack.51.place_ref.refs_0_
  21.7 2.5 %all-to-all-done = bf16[8,64,1024]{2,1,0:T(8,128)(2,1)} async-done(((bf16[8,64,1024]{2,1,0:T(8,128)(2,1)}), bf16[8,64,1024]{2,1,0:T(8,128)(2,1)}, u32[]{:S(2)}, u32[]{:S(2)}) %all-to-all-start) | async-done | bytes 1048608 | tf_op jit(solution)/shard_map/all_to_all | solution.py:377
  24.2 1.6 %collective-permute-start.2 = (bf16[512,1024]{1,0:T(8,128)(2,1)}, bf16[512,1024]{1,0:T(8,128)(2,1)S(1)}, u32[]{:S(2)}, u32[]{:S(2)}) collective-permute-start(bf16[512,1024]{1,0:T(8,128)(2,1)} %bitcast.15.refs_0_), channel_id=1, source_target_pairs={{0,32},{32,64},{64,96},{96,0},{1,33},{33,65},{65,97},{97,1},{2,34}... | collective-permute-start | bytes 3145736 | tf_op jit(solution)/shard_map/ppermute | solution.py:369
  25.9 2.1 %collective-permute-start.3 = (bf16[512,1024]{1,0:T(8,128)(2,1)}, bf16[512,1024]{1,0:T(8,128)(2,1)S(1)}, u32[]{:S(2)}, u32[]{:S(2)}) collective-permute-start(bf16[512,1024]{1,0:T(8,128)(2,1)} %bitcast.15.refs_0_), channel_id=1, source_target_pairs={{0,96},{32,0},{64,32},{96,64},{1,97},{33,1},{65,33},{97,65},{2,98}... | collective-permute-start | bytes 3145736 | tf_op jit(solution)/shard_map/ppermute | solution.py:369
  28.0 0.4 collective-permute-start.4
  28.3 2.4 %collective-permute-start.5 = (bf16[256,2048]{1,0:T(8,128)(2,1)S(1)}, bf16[256,2048]{1,0:T(8,128)(2,1)}, u32[]{:S(2)}, u32[]{:S(2)}) collective-permute-start(bf16[256,2048]{1,0:T(8,128)(2,1)S(1)} %copy-done.3), channel_id=1, source_target_pairs={{0,24},{8,0},{16,8},{24,16},{1,25},{9,1},{17,9},{25,17},{2,26},{10... | collective-permute-start | bytes 3145736 | tf_op jit(solution)/shard_map/ppermute | solution.py:369
  30.7 2.7 %dynamic-slice_convert_fusion.refs_4_ = bf16[2048,256]{1,0:T(8,128)(2,1)} fusion(f32[8192,256]{1,0:T(8,128)} %basis_ref.3, s32[]{:T(128)S(6)} %select_n.46), kind=kLoop, calls=%fused_computation | loop fusion | bytes 2097156 | tf_op jit(solution)/shard_map/convert_element_type | solution.py:386
  33.4 2.3 %add_convert_fusion = bf16[16,64,256]{2,1,0:T(8,128)(2,1)} fusion(f32[16,64,256]{2,1,0:T(8,128)} %copy-done.6, bf16[16,64,256]{2,1,0:T(8,128)(2,1)} %collective-permute-done), kind=kLoop, calls=%fused_computation.1 | loop fusion | flops 786432 | bytes 2097152 | tf_op jit(solution)/shard_map/convert_element_type | solution.py:387
  35.7 15.2 %collective-permute-done.2.first_ref.refs_1_ = bf16[512,1024]{1,0:T(8,128)(2,1)S(1)} collective-permute-done((bf16[512,1024]{1,0:T(8,128)(2,1)}, bf16[512,1024]{1,0:T(8,128)(2,1)S(1)}, u32[]{:S(2)}, u32[]{:S(2)}) %collective-permute-start.2) | collective-permute-done | bytes 1048608 | tf_op jit(solution)/shard_map/ppermute | solution.py:369
  51.0 1.9 %collective-permute-done.4.first_ref.refs_6_ = bf16[256,2048]{1,0:T(8,128)(2,1)} collective-permute-done((bf16[256,2048]{1,0:T(8,128)(2,1)S(1)}, bf16[256,2048]{1,0:T(8,128)(2,1)}, u32[]{:S(2)}, u32[]{:S(2)}) %collective-permute-start.4) | collective-permute-done | bytes 1048608 | tf_op jit(solution)/shard_map/ppermute | solution.py:369
  52.9 1.3 halves.2
  54.2 2.7 %collective-permute-start.7 = (bf16[128,2048]{1,0:T(8,128)(2,1)S(1)}, bf16[128,2048]{1,0:T(8,128)(2,1)S(1)}, u32[]{:S(2)}, u32[]{:S(2)}) collective-permute-start(bf16[128,2048]{1,0:T(8,128)(2,1)S(1)} %get-tuple-element.71), channel_id=1, source_target_pairs={{0,24},{8,0},{16,8},{24,16},{1,25},{9,1},{17,9},{25,17},{2,26},{10... | collective-permute-start | bytes 1572872 | tf_op jit(solution)/shard_map/ppermute | solution.py:369
  57.1 2.6 %collective-permute-start.9 = (bf16[256,1024]{1,0:T(8,128)(2,1)S(1)}, bf16[256,1024]{1,0:T(8,128)(2,1)S(1)}, u32[]{:S(2)}, u32[]{:S(2)}) collective-permute-start(bf16[256,1024]{1,0:T(8,128)(2,1)S(1)} %get-tuple-element.73), channel_id=1, source_target_pairs={{0,96},{32,0},{64,32},{96,64},{1,97},{33,1},{65,33},{97,65},{2,98}... | collective-permute-start | bytes 1572872 | tf_op jit(solution)/shard_map/ppermute | solution.py:369
  59.7 7.2 %collective-permute-done.6.refs_8_ = bf16[128,2048]{1,0:T(8,128)(2,1)} collective-permute-done((bf16[128,2048]{1,0:T(8,128)(2,1)S(1)}, bf16[128,2048]{1,0:T(8,128)(2,1)}, u32[]{:S(2)}, u32[]{:S(2)}) %collective-permute-start.6) | collective-permute-done | bytes 524320 | tf_op jit(solution)/shard_map/ppermute | solution.py:369
  66.9 2.3 %collective-permute-done.8.refs_3_ = bf16[256,1024]{1,0:T(8,128)(2,1)S(1)} collective-permute-done((bf16[256,1024]{1,0:T(8,128)(2,1)S(1)}, bf16[256,1024]{1,0:T(8,128)(2,1)S(1)}, u32[]{:S(2)}, u32[]{:S(2)}) %collective-permute-start.8) | collective-permute-done | bytes 524320 | tf_op jit(solution)/shard_map/ppermute | solution.py:369
  69.2 3.5 %collective-permute-start.10 = (bf16[256,2048]{1,0:T(8,128)(2,1)}, bf16[256,2048]{1,0:T(8,128)(2,1)S(1)}, u32[]{:S(2)}, u32[]{:S(2)}) collective-permute-start(bf16[256,2048]{1,0:T(8,128)(2,1)} %collective-permute-done.4.first_ref.refs_6_), channel_id=1, source_target_pairs={{0,4},{4,0},{1,5},{5,1},{2,6},{6,2},{3,7},{7,3},{8,12},{12,8},{9,1... | collective-permute-start | bytes 3145736 | tf_op jit(solution)/shard_map/ppermute | solution.py:365
  72.8 0.4 collective-permute-start.12
  73.3 9.1 %parts.2 = (bf16[4,256,256]{2,1,0:T(8,128)(2,1)}, bf16[4,256,256]{2,1,0:T(8,128)(2,1)}, bf16[4,256,256]{2,1,0:T(8,128)(2,1)}, bf16[4,256,256]{2,1,0:T(8,128)(2,1)}) custom-call(s32[12]{0:T(128)} %stack.51.place_ref.refs_0_, bf16[512,1024]{1,0:T(8,128)(2,1)} %bitcast.15.refs_0_, bf16[512,1024]{1,0:T(8,128)(2,1)} %copy-done, bf16[512,1024]{1,0:T(8,128)(2,1)} %copy-done.1, ...), custom_call_target="tpu_custom_call" | custom-call | tf_op jit(solution)/shard_map/parts/pallas_call | solution.py:184
  82.4 2.8 %collective-permute-start.14 = (bf16[4,256,256]{2,1,0:T(8,128)(2,1)}, bf16[4,256,256]{2,1,0:T(8,128)(2,1)S(1)}, u32[]{:S(2)}, u32[]{:S(2)}) collective-permute-start(bf16[4,256,256]{2,1,0:T(8,128)(2,1)} %get-tuple-element.87), channel_id=1, source_target_pairs={{0,3},{1,0},{2,1},{3,2},{4,7},{5,4},{6,5},{7,6},{8,11},{9,8},{10,9... | collective-permute-start | bytes 1572872 | tf_op jit(solution)/shard_map/ppermute | solution.py:369
  85.3 0.8 copy-done.15
  86.0 0.4 copy-done.12
  86.5 9.1 %parts.3 = (bf16[4,256,256]{2,1,0:T(8,128)(2,1)}, bf16[4,256,256]{2,1,0:T(8,128)(2,1)}, bf16[4,256,256]{2,1,0:T(8,128)(2,1)}, bf16[4,256,256]{2,1,0:T(8,128)(2,1)}) custom-call(s32[12]{0:T(128)} %stack.51.place_ref.refs_0_, bf16[512,1024]{1,0:T(8,128)(2,1)} %bitcast.15.refs_0_, bf16[512,1024]{1,0:T(8,128)(2,1)} %copy-done, bf16[512,1024]{1,0:T(8,128)(2,1)} %copy-done.1, ...), custom_call_target="tpu_custom_call" | custom-call | tf_op jit(solution)/shard_map/parts/pallas_call | solution.py:184
  95.5 2.5 %collective-permute-start.16 = (bf16[4,256,256]{2,1,0:T(8,128)(2,1)}, bf16[4,256,256]{2,1,0:T(8,128)(2,1)}, u32[]{:S(2)}, u32[]{:S(2)}) collective-permute-start(bf16[4,256,256]{2,1,0:T(8,128)(2,1)} %get-tuple-element.84), channel_id=1, source_target_pairs={{0,3},{1,0},{2,1},{3,2},{4,7},{5,4},{6,5},{7,6},{8,11},{9,8},{10,9... | collective-permute-start | bytes 1572872 | tf_op jit(solution)/shard_map/ppermute | solution.py:369
  98.1 4.8 %all-to-all-start.1 = ((bf16[16,64,256]{2,1,0:T(8,128)(2,1)}), bf16[16,64,256]{2,1,0:T(8,128)(2,1)S(1)}, u32[]{:S(2)}, u32[]{:S(2)}) async-start(bf16[16,64,256]{2,1,0:T(8,128)(2,1)} %add_convert_fusion), calls=%async_computation.1 | async-start | bytes 1048576 | tf_op jit(solution)/shard_map/all_to_all | solution.py:403
  103.0 5.7 %collective-permute-done.16.refs_3_ = bf16[4,256,256]{2,1,0:T(8,128)(2,1)} collective-permute-done((bf16[4,256,256]{2,1,0:T(8,128)(2,1)}, bf16[4,256,256]{2,1,0:T(8,128)(2,1)}, u32[]{:S(2)}, u32[]{:S(2)}) %collective-permute-start.16) | collective-permute-done | bytes 524320 | tf_op jit(solution)/shard_map/ppermute | solution.py:369
  108.7 2.4 %sums.2 = (bf16[4,256,256]{2,1,0:T(8,128)(2,1)}, bf16[4,256,256]{2,1,0:T(8,128)(2,1)}) custom-call(bf16[4,256,256]{2,1,0:T(8,128)(2,1)} %get-tuple-element.88.refs_0_, bf16[4,256,256]{2,1,0:T(8,128)(2,1)} %copy-done.16, bf16[4,256,256]{2,1,0:T(8,128)(2,1)} %get-tuple-element.90.refs_2_, bf16[4,256,256]{2,1,0:T(8,128)(2,1)} %collective-permute-done.16.refs_3_), custom_call_target="tpu_custom_call" | custom-call | tf_op jit(solution)/shard_map/sums/pallas_call | solution.py:230
  111.2 3.4 %collective-permute-start.19 = (bf16[4,256,256]{2,1,0:T(8,128)(2,1)}, bf16[4,256,256]{2,1,0:T(8,128)(2,1)}, u32[]{:S(2)}, u32[]{:S(2)}) collective-permute-start(bf16[4,256,256]{2,1,0:T(8,128)(2,1)} %get-tuple-element.98), channel_id=1, source_target_pairs={{0,3},{1,0},{2,1},{3,2},{4,7},{5,4},{6,5},{7,6},{8,11},{9,8},{10,9... | collective-permute-start | bytes 1572872 | tf_op jit(solution)/shard_map/ppermute | solution.py:369
  114.6 1.0 optimizer_step.1
  115.6 4.8 %all-to-all-start.2 = ((bf16[16,64,256]{2,1,0:T(8,128)(2,1)}), bf16[16,64,256]{2,1,0:T(8,128)(2,1)}, u32[]{:S(2)}, u32[]{:S(2)}) async-start(bf16[16,64,256]{2,1,0:T(8,128)(2,1)} %get-tuple-element.99), calls=%async_computation.2 | async-start | bytes 1048576 | tf_op jit(solution)/shard_map/all_to_all | solution.py:409
  120.4 5.9 %fresh_rows.1 = bf16[64,8192]{1,0:T(8,128)(2,1)} custom-call(f32[64,256]{1,0:T(8,128)S(1)} %get-tuple-element.93.direction_ref, f32[8192,256]{1,0:T(8,128)} %basis_ref.3, bf16[64,8192]{1,0:T(8,128)(2,1)S(1)} %bitcast.22), custom_call_target="tpu_custom_call" | custom-call | tf_op jit(solution)/shard_map/fresh_rows/pallas_call | solution.py:128
  126.4 1.2 collective-permute-done.17.refs_2_
  127.5 3.5 %sums.3 = bf16[8,256,256]{2,1,0:T(8,128)(2,1)} custom-call(s32[12]{0:T(128)} %stack.51.place_ref.refs_0_, bf16[4,256,256]{2,1,0:T(8,128)(2,1)} %get-tuple-element.94.refs_1_, bf16[4,256,256]{2,1,0:T(8,128)(2,1)} %collective-permute-done.17.refs_2_, bf16[4,256,256]{2,1,0:T(8,128)(2,1)} %copy-done.13, bf16[4,256,256]{2,1,0:T(8,128)(2,1)} %get-tuple-element.96.refs_4_, ...), custom_call_target="tpu_custom_call" | custom-call | tf_op jit(solution)/shard_map/sums/pallas_call | solution.py:230
  131.0 7.0 %all-to-all-start.3 = ((bf16[8,256,256]{2,1,0:T(8,128)(2,1)}), bf16[8,256,256]{2,1,0:T(8,128)(2,1)S(1)}, u32[]{:S(2)}, u32[]{:S(2)}) async-start(bf16[8,256,256]{2,1,0:T(8,128)(2,1)} %sums.3), calls=%async_computation.3 | async-start | bytes 2097152 | tf_op jit(solution)/shard_map/all_to_all | solution.py:417
  138.0 2.1 %collective-permute-done.20.other_ref = bf16[16,64,256]{2,1,0:T(8,128)(2,1)S(1)} collective-permute-done((bf16[16,64,256]{2,1,0:T(8,128)(2,1)}, bf16[16,64,256]{2,1,0:T(8,128)(2,1)S(1)}, u32[]{:S(2)}, u32[]{:S(2)}) %collective-permute-start.20) | collective-permute-done | bytes 524320 | tf_op jit(solution)/shard_map/ppermute | solution.py:365
  140.1 1.5 %inner.1 = f32[256,256]{1,0:T(8,128)S(1)} custom-call(s32[1]{0:T(128)} %bitcast.core_ref, bf16[256,2048]{1,0:T(8,128)(2,1)S(1)} %copy-done.4, bf16[16,64,256]{2,1,0:T(8,128)(2,1)} %all-to-all-done.2.mine_ref, bf16[16,64,256]{2,1,0:T(8,128)(2,1)S(1)} %collective-permute-done.20.other_ref), custom_call_target="tpu_custom_call" | custom-call | tf_op jit(solution)/shard_map/inner/pallas_call | solution.py:282
  141.7 2.7 %collective-permute-start.22 = (bf16[256,256]{1,0:T(8,128)(2,1)S(1)}, bf16[256,256]{1,0:T(8,128)(2,1)S(1)}, u32[]{:S(2)}, u32[]{:S(2)}) collective-permute-start(bf16[256,256]{1,0:T(8,128)(2,1)S(1)} %convert_element_type.15.refs_0_), channel_id=1, source_target_pairs={{0,3},{1,0},{2,1},{3,2},{4,7},{5,4},{6,5},{7,6},{8,11},{9,8},{10,9... | collective-permute-start | bytes 393224 | tf_op jit(solution)/shard_map/ppermute | solution.py:369
  144.4 3.5 %collective-permute-done.21.refs_1_ = bf16[256,256]{1,0:T(8,128)(2,1)S(1)} collective-permute-done((bf16[256,256]{1,0:T(8,128)(2,1)S(1)}, bf16[256,256]{1,0:T(8,128)(2,1)S(1)}, u32[]{:S(2)}, u32[]{:S(2)}) %collective-permute-start.21) | collective-permute-done | bytes 131104 | tf_op jit(solution)/shard_map/ppermute | solution.py:369
  147.9 1.7 %collective-permute-done.22.refs_2_ = bf16[256,256]{1,0:T(8,128)(2,1)S(1)} collective-permute-done((bf16[256,256]{1,0:T(8,128)(2,1)S(1)}, bf16[256,256]{1,0:T(8,128)(2,1)S(1)}, u32[]{:S(2)}, u32[]{:S(2)}) %collective-permute-start.22) | collective-permute-done | bytes 131104 | tf_op jit(solution)/shard_map/ppermute | solution.py:369
  149.5 0.7 collective-permute-done.23.refs_3_
  150.2 1.0 change.1.change_ref
  151.3 1.8 %all-to-all-done.3.part_ref = bf16[8,256,256]{2,1,0:T(8,128)(2,1)S(1)} async-done(((bf16[8,256,256]{2,1,0:T(8,128)(2,1)}), bf16[8,256,256]{2,1,0:T(8,128)(2,1)S(1)}, u32[]{:S(2)}, u32[]{:S(2)}) %all-to-all-start.3) | async-done | bytes 1048608 | tf_op jit(solution)/shard_map/all_to_all | solution.py:417
  153.1 1.2 output_rows.1
  (59 shorter events, 0.8 us)
Async XLA Ops:
  0.6 27.4 %collective-permute-start.1 = (bf16[256,2048]{1,0:T(8,128)(2,1)}, bf16[256,2048]{1,0:T(8,128)(2,1)}, u32[]{:S(2)}, u32[]{:S(2)}) collective-permute-start(bf16[256,2048]{1,0:T(8,128)(2,1)} %acts_ref.3), channel_id=1, source_target_pairs={{0,4},{4,0},{1,5},{5,1},{2,6},{6,2},{3,7},{7,3},{8,12},{12,8},{9,1... | collective-permute-start | bytes 3145736 | tf_op jit(solution)/shard_map/ppermute | solution.py:365
  4.4 23.6 %copy-start.3 = (bf16[256,2048]{1,0:T(8,128)(2,1)S(1)}, bf16[256,2048]{1,0:T(8,128)(2,1)}, u32[]{:S(2)}) copy-start(bf16[256,2048]{1,0:T(8,128)(2,1)} %acts_ref.3) | copy-start | bytes 3145732
  4.4 19.8 %all-to-all-start = ((bf16[8,64,1024]{2,1,0:T(8,128)(2,1)}), bf16[8,64,1024]{2,1,0:T(8,128)(2,1)}, u32[]{:S(2)}, u32[]{:S(2)}) async-start(bf16[8,64,1024]{2,1,0:T(8,128)(2,1)} %exchange_order.1), calls=%async_computation | async-start | bytes 2097152 | tf_op jit(solution)/shard_map/all_to_all | solution.py:377
  9.0 1.2 copy-start.7
  20.1 1.0 copy-start.6
  21.0 7.0 %collective-permute-start = (bf16[16,64,256]{2,1,0:T(8,128)(2,1)}, bf16[16,64,256]{2,1,0:T(8,128)(2,1)}, u32[]{:S(2)}, u32[]{:S(2)}) collective-permute-start(bf16[16,64,256]{2,1,0:T(8,128)(2,1)} %get-tuple-element.56), channel_id=1, source_target_pairs={{0,4},{4,0},{1,5},{5,1},{2,6},{6,2},{3,7},{7,3},{8,12},{12,8},{9,1... | collective-permute-start | bytes 1572872 | tf_op jit(solution)/shard_map/ppermute | solution.py:365
  24.2 26.7 %collective-permute-start.2 = (bf16[512,1024]{1,0:T(8,128)(2,1)}, bf16[512,1024]{1,0:T(8,128)(2,1)S(1)}, u32[]{:S(2)}, u32[]{:S(2)}) collective-permute-start(bf16[512,1024]{1,0:T(8,128)(2,1)} %bitcast.15.refs_0_), channel_id=1, source_target_pairs={{0,32},{32,64},{64,96},{96,0},{1,33},{33,65},{65,97},{97,1},{2,34}... | collective-permute-start | bytes 3145736 | tf_op jit(solution)/shard_map/ppermute | solution.py:369
  25.9 25.1 %collective-permute-start.3 = (bf16[512,1024]{1,0:T(8,128)(2,1)}, bf16[512,1024]{1,0:T(8,128)(2,1)S(1)}, u32[]{:S(2)}, u32[]{:S(2)}) collective-permute-start(bf16[512,1024]{1,0:T(8,128)(2,1)} %bitcast.15.refs_0_), channel_id=1, source_target_pairs={{0,96},{32,0},{64,32},{96,64},{1,97},{33,1},{65,33},{97,65},{2,98}... | collective-permute-start | bytes 3145736 | tf_op jit(solution)/shard_map/ppermute | solution.py:369
  28.0 24.9 %collective-permute-start.4 = (bf16[256,2048]{1,0:T(8,128)(2,1)S(1)}, bf16[256,2048]{1,0:T(8,128)(2,1)}, u32[]{:S(2)}, u32[]{:S(2)}) collective-permute-start(bf16[256,2048]{1,0:T(8,128)(2,1)S(1)} %copy-done.3), channel_id=1, source_target_pairs={{0,8},{8,16},{16,24},{24,0},{1,9},{9,17},{17,25},{25,1},{2,10},{10... | collective-permute-start | bytes 3145736 | tf_op jit(solution)/shard_map/ppermute | solution.py:369
  28.3 24.5 %collective-permute-start.5 = (bf16[256,2048]{1,0:T(8,128)(2,1)S(1)}, bf16[256,2048]{1,0:T(8,128)(2,1)}, u32[]{:S(2)}, u32[]{:S(2)}) collective-permute-start(bf16[256,2048]{1,0:T(8,128)(2,1)S(1)} %copy-done.3), channel_id=1, source_target_pairs={{0,24},{8,0},{16,8},{24,16},{1,25},{9,1},{17,9},{25,17},{2,26},{10... | collective-permute-start | bytes 3145736 | tf_op jit(solution)/shard_map/ppermute | solution.py:369
  51.0 22.3 %copy-start = (bf16[512,1024]{1,0:T(8,128)(2,1)}, bf16[512,1024]{1,0:T(8,128)(2,1)S(1)}, u32[]{:S(2)}) copy-start(bf16[512,1024]{1,0:T(8,128)(2,1)S(1)} %collective-permute-done.2.first_ref.refs_1_) | copy-start | bytes 3145732
  51.0 22.3 %copy-start.1 = (bf16[512,1024]{1,0:T(8,128)(2,1)}, bf16[512,1024]{1,0:T(8,128)(2,1)S(1)}, u32[]{:S(2)}) copy-start(bf16[512,1024]{1,0:T(8,128)(2,1)S(1)} %collective-permute-done.3.last_ref.refs_2_) | copy-start | bytes 3145732
  54.2 12.7 %collective-permute-start.6 = (bf16[128,2048]{1,0:T(8,128)(2,1)S(1)}, bf16[128,2048]{1,0:T(8,128)(2,1)}, u32[]{:S(2)}, u32[]{:S(2)}) collective-permute-start(bf16[128,2048]{1,0:T(8,128)(2,1)S(1)} %get-tuple-element.70), channel_id=1, source_target_pairs={{0,8},{8,16},{16,24},{24,0},{1,9},{9,17},{17,25},{25,1},{2,10},{10... | collective-permute-start | bytes 1572872 | tf_op jit(solution)/shard_map/ppermute | solution.py:369
  54.2 12.6 %collective-permute-start.7 = (bf16[128,2048]{1,0:T(8,128)(2,1)S(1)}, bf16[128,2048]{1,0:T(8,128)(2,1)S(1)}, u32[]{:S(2)}, u32[]{:S(2)}) collective-permute-start(bf16[128,2048]{1,0:T(8,128)(2,1)S(1)} %get-tuple-element.71), channel_id=1, source_target_pairs={{0,24},{8,0},{16,8},{24,16},{1,25},{9,1},{17,9},{25,17},{2,26},{10... | collective-permute-start | bytes 1572872 | tf_op jit(solution)/shard_map/ppermute | solution.py:369
  57.0 12.2 %collective-permute-start.8 = (bf16[256,1024]{1,0:T(8,128)(2,1)S(1)}, bf16[256,1024]{1,0:T(8,128)(2,1)S(1)}, u32[]{:S(2)}, u32[]{:S(2)}) collective-permute-start(bf16[256,1024]{1,0:T(8,128)(2,1)S(1)} %get-tuple-element.72), channel_id=1, source_target_pairs={{0,32},{32,64},{64,96},{96,0},{1,33},{33,65},{65,97},{97,1},{2,34}... | collective-permute-start | bytes 1572872 | tf_op jit(solution)/shard_map/ppermute | solution.py:369
  57.1 57.6 %copy-start.8 = (f32[1,64,256]{2,1,0:T(8,128)S(1)}, f32[1,64,256]{2,1,0:T(8,128)}, u32[]{:S(2)}) copy-start(f32[1,64,256]{2,1,0:T(8,128)} %param.10) | copy-start | bytes 196612
  57.1 57.6 %copy-start.9 = (f32[1,64,256]{2,1,0:T(8,128)S(1)}, f32[1,64,256]{2,1,0:T(8,128)}, u32[]{:S(2)}) copy-start(f32[1,64,256]{2,1,0:T(8,128)} %param.11) | copy-start | bytes 196612
  57.1 12.1 %collective-permute-start.9 = (bf16[256,1024]{1,0:T(8,128)(2,1)S(1)}, bf16[256,1024]{1,0:T(8,128)(2,1)S(1)}, u32[]{:S(2)}, u32[]{:S(2)}) collective-permute-start(bf16[256,1024]{1,0:T(8,128)(2,1)S(1)} %get-tuple-element.73), channel_id=1, source_target_pairs={{0,96},{32,0},{64,32},{96,64},{1,97},{33,1},{65,33},{97,65},{2,98}... | collective-permute-start | bytes 1572872 | tf_op jit(solution)/shard_map/ppermute | solution.py:369
  66.9 6.4 %copy-start.14 = (bf16[128,2048]{1,0:T(8,128)(2,1)}, bf16[128,2048]{1,0:T(8,128)(2,1)S(1)}, u32[]{:S(2)}) copy-start(bf16[128,2048]{1,0:T(8,128)(2,1)S(1)} %collective-permute-done.7.refs_9_) | copy-start | bytes 1572868
  69.1 4.1 %copy-start.10 = (bf16[256,1024]{1,0:T(8,128)(2,1)}, bf16[256,1024]{1,0:T(8,128)(2,1)S(1)}, u32[]{:S(2)}) copy-start(bf16[256,1024]{1,0:T(8,128)(2,1)S(1)} %collective-permute-done.8.refs_3_) | copy-start | bytes 1572868
  69.1 4.1 %copy-start.11 = (bf16[256,1024]{1,0:T(8,128)(2,1)}, bf16[256,1024]{1,0:T(8,128)(2,1)S(1)}, u32[]{:S(2)}) copy-start(bf16[256,1024]{1,0:T(8,128)(2,1)S(1)} %collective-permute-done.9.refs_4_) | copy-start | bytes 1572868
  69.2 16.1 %collective-permute-start.10 = (bf16[256,2048]{1,0:T(8,128)(2,1)}, bf16[256,2048]{1,0:T(8,128)(2,1)S(1)}, u32[]{:S(2)}, u32[]{:S(2)}) collective-permute-start(bf16[256,2048]{1,0:T(8,128)(2,1)} %collective-permute-done.4.first_ref.refs_6_), channel_id=1, source_target_pairs={{0,4},{4,0},{1,5},{5,1},{2,6},{6,2},{3,7},{7,3},{8,12},{12,8},{9,1... | collective-permute-start | bytes 3145736 | tf_op jit(solution)/shard_map/ppermute | solution.py:365
  72.7 12.6 %collective-permute-start.11 = (bf16[256,2048]{1,0:T(8,128)(2,1)}, bf16[256,2048]{1,0:T(8,128)(2,1)}, u32[]{:S(2)}, u32[]{:S(2)}) collective-permute-start(bf16[256,2048]{1,0:T(8,128)(2,1)} %collective-permute-done.5.last_ref.refs_7_), channel_id=1, source_target_pairs={{0,4},{4,0},{1,5},{5,1},{2,6},{6,2},{3,7},{7,3},{8,12},{12,8},{9,1... | collective-permute-start | bytes 3145736 | tf_op jit(solution)/shard_map/ppermute | solution.py:365
  72.8 12.5 %collective-permute-start.12 = (bf16[128,2048]{1,0:T(8,128)(2,1)}, bf16[128,2048]{1,0:T(8,128)(2,1)S(1)}, u32[]{:S(2)}, u32[]{:S(2)}) collective-permute-start(bf16[128,2048]{1,0:T(8,128)(2,1)} %collective-permute-done.6.refs_8_), channel_id=1, source_target_pairs={{0,4},{4,0},{1,5},{5,1},{2,6},{6,2},{3,7},{7,3},{8,12},{12,8},{9,1... | collective-permute-start | bytes 1572872 | tf_op jit(solution)/shard_map/ppermute | solution.py:365
  73.2 12.0 %collective-permute-start.13 = (bf16[128,2048]{1,0:T(8,128)(2,1)S(1)}, bf16[128,2048]{1,0:T(8,128)(2,1)}, u32[]{:S(2)}, u32[]{:S(2)}) collective-permute-start(bf16[128,2048]{1,0:T(8,128)(2,1)S(1)} %collective-permute-done.7.refs_9_), channel_id=1, source_target_pairs={{0,4},{4,0},{1,5},{5,1},{2,6},{6,2},{3,7},{7,3},{8,12},{12,8},{9,1... | collective-permute-start | bytes 1572872 | tf_op jit(solution)/shard_map/ppermute | solution.py:365
  82.4 38.0 %copy-start.2 = (bf16[1,64,8192]{2,1,0:T(8,128)(2,1)S(1)}, bf16[1,64,8192]{2,1,0:T(8,128)(2,1)}, u32[]{:S(2)}) copy-start(bf16[1,64,8192]{2,1,0:T(8,128)(2,1)} %param.12) | copy-start | bytes 3145732
  82.4 20.5 %collective-permute-start.14 = (bf16[4,256,256]{2,1,0:T(8,128)(2,1)}, bf16[4,256,256]{2,1,0:T(8,128)(2,1)S(1)}, u32[]{:S(2)}, u32[]{:S(2)}) collective-permute-start(bf16[4,256,256]{2,1,0:T(8,128)(2,1)} %get-tuple-element.87), channel_id=1, source_target_pairs={{0,3},{1,0},{2,1},{3,2},{4,7},{5,4},{6,5},{7,6},{8,11},{9,8},{10,9... | collective-permute-start | bytes 1572872 | tf_op jit(solution)/shard_map/ppermute | solution.py:369
  85.2 0.8 copy-start.15
  85.2 17.7 %collective-permute-start.15 = (bf16[4,256,256]{2,1,0:T(8,128)(2,1)}, bf16[4,256,256]{2,1,0:T(8,128)(2,1)S(1)}, u32[]{:S(2)}, u32[]{:S(2)}) collective-permute-start(bf16[4,256,256]{2,1,0:T(8,128)(2,1)} %get-tuple-element.89), channel_id=1, source_target_pairs={{0,1},{1,2},{2,3},{3,0},{4,5},{5,6},{6,7},{7,4},{8,9},{9,10},{10,1... | collective-permute-start | bytes 1572872 | tf_op jit(solution)/shard_map/ppermute | solution.py:369
  85.2 1.2 copy-start.12
  95.5 13.1 %collective-permute-start.16 = (bf16[4,256,256]{2,1,0:T(8,128)(2,1)}, bf16[4,256,256]{2,1,0:T(8,128)(2,1)}, u32[]{:S(2)}, u32[]{:S(2)}) collective-permute-start(bf16[4,256,256]{2,1,0:T(8,128)(2,1)} %get-tuple-element.84), channel_id=1, source_target_pairs={{0,3},{1,0},{2,1},{3,2},{4,7},{5,4},{6,5},{7,6},{8,11},{9,8},{10,9... | collective-permute-start | bytes 1572872 | tf_op jit(solution)/shard_map/ppermute | solution.py:369
  98.1 16.6 %all-to-all-start.1 = ((bf16[16,64,256]{2,1,0:T(8,128)(2,1)}), bf16[16,64,256]{2,1,0:T(8,128)(2,1)S(1)}, u32[]{:S(2)}, u32[]{:S(2)}) async-start(bf16[16,64,256]{2,1,0:T(8,128)(2,1)} %add_convert_fusion), calls=%async_computation.1 | async-start | bytes 1048576 | tf_op jit(solution)/shard_map/all_to_all | solution.py:403
  102.9 11.7 %copy-start.13 = (bf16[4,256,256]{2,1,0:T(8,128)(2,1)}, bf16[4,256,256]{2,1,0:T(8,128)(2,1)S(1)}, u32[]{:S(2)}) copy-start(bf16[4,256,256]{2,1,0:T(8,128)(2,1)S(1)} %collective-permute-done.14.refs_3_) | copy-start | bytes 1572868
  102.9 23.5 %collective-permute-start.18 = (bf16[4,256,256]{2,1,0:T(8,128)(2,1)}, bf16[4,256,256]{2,1,0:T(8,128)(2,1)}, u32[]{:S(2)}, u32[]{:S(2)}) collective-permute-start(bf16[4,256,256]{2,1,0:T(8,128)(2,1)} %get-tuple-element.97), channel_id=1, source_target_pairs={{0,1},{1,2},{2,3},{3,0},{4,5},{5,6},{6,7},{7,4},{8,9},{9,10},{10,1... | collective-permute-start | bytes 1572872 | tf_op jit(solution)/shard_map/ppermute | solution.py:369
  103.0 5.7 %copy-start.16 = (bf16[4,256,256]{2,1,0:T(8,128)(2,1)}, bf16[4,256,256]{2,1,0:T(8,128)(2,1)S(1)}, u32[]{:S(2)}) copy-start(bf16[4,256,256]{2,1,0:T(8,128)(2,1)S(1)} %collective-permute-done.15.refs_1_) | copy-start | bytes 1572868
  111.1 16.4 %collective-permute-start.17 = (bf16[4,256,256]{2,1,0:T(8,128)(2,1)}, bf16[4,256,256]{2,1,0:T(8,128)(2,1)}, u32[]{:S(2)}, u32[]{:S(2)}) collective-permute-start(bf16[4,256,256]{2,1,0:T(8,128)(2,1)} %get-tuple-element.91), channel_id=1, source_target_pairs={{0,1},{1,2},{2,3},{3,0},{4,5},{5,6},{6,7},{7,4},{8,9},{9,10},{10,1... | collective-permute-start | bytes 1572872 | tf_op jit(solution)/shard_map/ppermute | solution.py:369
  111.2 16.3 %collective-permute-start.19 = (bf16[4,256,256]{2,1,0:T(8,128)(2,1)}, bf16[4,256,256]{2,1,0:T(8,128)(2,1)}, u32[]{:S(2)}, u32[]{:S(2)}) collective-permute-start(bf16[4,256,256]{2,1,0:T(8,128)(2,1)} %get-tuple-element.98), channel_id=1, source_target_pairs={{0,3},{1,0},{2,1},{3,2},{4,7},{5,4},{6,5},{7,6},{8,11},{9,8},{10,9... | collective-permute-start | bytes 1572872 | tf_op jit(solution)/shard_map/ppermute | solution.py:369
  115.6 15.4 %all-to-all-start.2 = ((bf16[16,64,256]{2,1,0:T(8,128)(2,1)}), bf16[16,64,256]{2,1,0:T(8,128)(2,1)}, u32[]{:S(2)}, u32[]{:S(2)}) async-start(bf16[16,64,256]{2,1,0:T(8,128)(2,1)} %get-tuple-element.99), calls=%async_computation.2 | async-start | bytes 1048576 | tf_op jit(solution)/shard_map/all_to_all | solution.py:409
  120.4 19.7 %copy-start.4 = (bf16[256,2048]{1,0:T(8,128)(2,1)S(1)}, bf16[256,2048]{1,0:T(8,128)(2,1)}, u32[]{:S(2)}) copy-start(bf16[256,2048]{1,0:T(8,128)(2,1)} %acts_ref.3) | copy-start | bytes 3145732
  120.4 29.8 %copy-start.5 = (bf16[2048,256]{1,0:T(8,128)(2,1)S(1)}, bf16[2048,256]{1,0:T(8,128)(2,1)}, u32[]{:S(2)}) copy-start(bf16[2048,256]{1,0:T(8,128)(2,1)} %dynamic-slice_convert_fusion.refs_4_) | copy-start | bytes 3145732
  131.0 22.1 %all-to-all-start.3 = ((bf16[8,256,256]{2,1,0:T(8,128)(2,1)}), bf16[8,256,256]{2,1,0:T(8,128)(2,1)S(1)}, u32[]{:S(2)}, u32[]{:S(2)}) async-start(bf16[8,256,256]{2,1,0:T(8,128)(2,1)} %sums.3), calls=%async_computation.3 | async-start | bytes 2097152 | tf_op jit(solution)/shard_map/all_to_all | solution.py:417
  138.0 2.1 %collective-permute-start.20 = (bf16[16,64,256]{2,1,0:T(8,128)(2,1)}, bf16[16,64,256]{2,1,0:T(8,128)(2,1)S(1)}, u32[]{:S(2)}, u32[]{:S(2)}) collective-permute-start(bf16[16,64,256]{2,1,0:T(8,128)(2,1)} %all-to-all-done.2.mine_ref), channel_id=1, source_target_pairs={{0,4},{4,0},{1,5},{5,1},{2,6},{6,2},{3,7},{7,3},{8,12},{12,8},{9,1... | collective-permute-start | bytes 1572872 | tf_op jit(solution)/shard_map/ppermute | solution.py:365
  141.7 6.2 %collective-permute-start.21 = (bf16[256,256]{1,0:T(8,128)(2,1)S(1)}, bf16[256,256]{1,0:T(8,128)(2,1)S(1)}, u32[]{:S(2)}, u32[]{:S(2)}) collective-permute-start(bf16[256,256]{1,0:T(8,128)(2,1)S(1)} %convert_element_type.15.refs_0_), channel_id=1, source_target_pairs={{0,1},{1,2},{2,3},{3,0},{4,5},{5,6},{6,7},{7,4},{8,9},{9,10},{10,1... | collective-permute-start | bytes 393224 | tf_op jit(solution)/shard_map/ppermute | solution.py:369
  141.7 7.8 %collective-permute-start.22 = (bf16[256,256]{1,0:T(8,128)(2,1)S(1)}, bf16[256,256]{1,0:T(8,128)(2,1)S(1)}, u32[]{:S(2)}, u32[]{:S(2)}) collective-permute-start(bf16[256,256]{1,0:T(8,128)(2,1)S(1)} %convert_element_type.15.refs_0_), channel_id=1, source_target_pairs={{0,3},{1,0},{2,1},{3,2},{4,7},{5,4},{6,5},{7,6},{8,11},{9,8},{10,9... | collective-permute-start | bytes 393224 | tf_op jit(solution)/shard_map/ppermute | solution.py:369
  144.4 5.8 %collective-permute-start.23 = (bf16[256,256]{1,0:T(8,128)(2,1)S(1)}, bf16[256,256]{1,0:T(8,128)(2,1)S(1)}, u32[]{:S(2)}, u32[]{:S(2)}) collective-permute-start(bf16[256,256]{1,0:T(8,128)(2,1)S(1)} %convert_element_type.15.refs_0_), channel_id=1, source_target_pairs={{0,2},{1,3},{2,0},{3,1},{4,6},{5,7},{6,4},{7,5},{8,10},{9,11},{10,... | collective-permute-start | bytes 393224 | tf_op jit(solution)/shard_map/ppermute | solution.py:369

commit v6 on v5

--- a/solution.py
+++ b/solution.py
@@ -407,13 +407,15 @@
     projected, up1 = lax.optimization_barrier((projected, up1))
     first, second, direction, sent = optimizer_step(projected, moment1[0], moment2[0])
     mine = lax.all_to_all(sent, ("z", "x"), 0, 0)
-    fresh = fresh_rows(direction, basis, old)
-    up0, down0, fresh = lax.optimization_barrier((up0, down0, fresh))
-    part = sums(((up0, got_up1, got_up3), (down0, got_down1, got_down3)), place)
+    up0, down0, direction = lax.optimization_barrier((up0, down0, direction))
+    up0, down0 = sums(((up0, got_up3), (down0, got_down1)))
+    part = sums(((up0, got_up1), (down0, got_down3)), place)
     part, mine = lax.optimization_barrier((part, mine))
     share = inner(core, next_acts, mine, swap(mine)).astype(BF16)
     shares = [share] + [shift(share, "y", d) for d in (1, -1, 2)]
     change = change_of(shares, rows)
+    direction, mine = lax.optimization_barrier((direction, mine))
+    fresh = fresh_rows(direction, basis, old)
     part = lax.all_to_all(part, ("x", "c"), 0, 0)
     output = output_rows(part, change)
     return (output, fresh[None], first[None], second[None])

time: 155 us -> 156 us (level)
  local copies, waits for them, and re-layouts: 6.78 us -> 9.2 us
  waiting for transfers between devices: 45.7 us -> 43.3 us
    unnamed x34 -> x36, local copies, waits for them, and re-layouts: 3.44 us -> 5.91 us
    ppermute x17, waiting for transfers between devices: 39.2 us -> 36.9 us  [shift(): return lax.ppermute(value, axis, [(i, (i + by) % 4) for i in range(4)])]
    pallas_call x2 -> x3, Pallas kernels: 5.89 us -> 7.97 us  [sums(): pl.pallas_call(functools.partial(sums_kernel, count, terms, placed), in_s...]
  transfers between devices with their start and end apart: 28 -> 28, of which waited for: 12 -> 9; matrix products, arithmetic and copies ran while one was open for 4% -> 4% of each run, Pallas kernels for 30% -> 30%
where the time goes in v6:
time: 156 us
  starting transfers between devices  50.7 us (32%)
  Pallas kernels  49.1 us (31%)
  waiting for transfers between devices  43.3 us (28%)
  local copies, waits for them, and re-layouts  9.2 us (6%)
  other arithmetic  2.32 us (1%)
    ppermute x17, waiting for transfers between devices, shift(): return lax.ppermute(value, axis, [(i, (i + by) % 4) for i in range(4)])  36.9 us
    ppermute x17, starting transfers between devices, shift(): return lax.ppermute(value, axis, [(i, (i + by) % 4) for i in range(4)])  23.9 us
    pallas_call x2, Pallas kernels, parts(): pl.pallas_call(parts_kernel, in_specs=[pl.BlockSpec(memory_space=pltpu.SM...  18.2 us
    pallas_call x1, Pallas kernels, project(): pl.pallas_call(project_kernel, grid_spec=pltpu.PrefetchScalarGridSpec(num...  9.83 us
    pallas_call x3, Pallas kernels, sums(): pl.pallas_call(functools.partial(sums_kernel, count, terms, placed), in_s...  7.97 us
    all_to_all x1, starting transfers between devices, on_device(): part = lax.all_to_all(part, ('x', 'c'), 0, 0)  6.95 us
    unnamed x36, local copies, waits for them, and re-layouts  5.91 us
    pallas_call x1, Pallas kernels, fresh_rows(): pl.pallas_call(fresh_kernel, grid=(width // block,), in_specs=[pl.BlockSp...  5.8 us
  transfers between devices with their start and end apart: 28, of which 9 were waited for; matrix products, arithmetic and copies ran while one was open for 4% of the time, Pallas kernels for 30%

profile of v6, /device:TPU:1, one launch (start us, length us, event | category | flops | bytes accessed | tf_op | source)
XLA Modules:
  0.0 155.5 jit_solution(10135757144739317250)
XLA Ops:
  0.6 1.5 collective-permute-start.1
  2.1 2.2 %exchange_order.1 = bf16[8,64,1024]{2,1,0:T(8,128)(2,1)} custom-call(s32[1]{0:T(128)} %bitcast.13.y_ref, bf16[64,8192]{1,0:T(8,128)(2,1)} %bitcast.21), custom_call_target="tpu_custom_call" | custom-call | tf_op jit(solution)/shard_map/exchange_order/pallas_call | solution.py:108
  4.4 4.6 %all-to-all-start = ((bf16[8,64,1024]{2,1,0:T(8,128)(2,1)}), bf16[8,64,1024]{2,1,0:T(8,128)(2,1)}, u32[]{:S(2)}, u32[]{:S(2)}) async-start(bf16[8,64,1024]{2,1,0:T(8,128)(2,1)} %exchange_order.1), calls=%async_computation | async-start | bytes 2097152 | tf_op jit(solution)/shard_map/all_to_all | solution.py:377
  9.0 1.2 copy-done.9
  10.2 9.8 %project.1 = (f32[16,64,256]{2,1,0:T(8,128)S(1)}, bf16[16,64,256]{2,1,0:T(8,128)(2,1)}) custom-call(s32[1]{0:T(128)} %bitcast.core_ref, bf16[256,8192]{1,0:T(8,128)(2,1)} %grad_ref.1, f32[8192,256]{1,0:T(8,128)} %basis_ref.3, bf16[256,2048]{1,0:T(8,128)(2,1)S(1)} %copy-done.9), custom_call_target="tpu_custom_call" | custom-call | tf_op jit(solution)/shard_map/project/pallas_call | solution.py:67
  20.1 1.0 copy-done.8
  21.0 0.6 stack.51.place_ref.refs_0_
  21.6 2.6 %all-to-all-done = bf16[8,64,1024]{2,1,0:T(8,128)(2,1)} async-done(((bf16[8,64,1024]{2,1,0:T(8,128)(2,1)}), bf16[8,64,1024]{2,1,0:T(8,128)(2,1)}, u32[]{:S(2)}, u32[]{:S(2)}) %all-to-all-start) | async-done | bytes 1048608 | tf_op jit(solution)/shard_map/all_to_all | solution.py:377
  24.2 1.6 %collective-permute-start.2 = (bf16[512,1024]{1,0:T(8,128)(2,1)}, bf16[512,1024]{1,0:T(8,128)(2,1)S(1)}, u32[]{:S(2)}, u32[]{:S(2)}) collective-permute-start(bf16[512,1024]{1,0:T(8,128)(2,1)} %bitcast.15.refs_0_), channel_id=1, source_target_pairs={{0,32},{32,64},{64,96},{96,0},{1,33},{33,65},{65,97},{97,1},{2,34}... | collective-permute-start | bytes 3145736 | tf_op jit(solution)/shard_map/ppermute | solution.py:369
  25.9 2.1 %collective-permute-start.3 = (bf16[512,1024]{1,0:T(8,128)(2,1)}, bf16[512,1024]{1,0:T(8,128)(2,1)S(1)}, u32[]{:S(2)}, u32[]{:S(2)}) collective-permute-start(bf16[512,1024]{1,0:T(8,128)(2,1)} %bitcast.15.refs_0_), channel_id=1, source_target_pairs={{0,96},{32,0},{64,32},{96,64},{1,97},{33,1},{65,33},{97,65},{2,98}... | collective-permute-start | bytes 3145736 | tf_op jit(solution)/shard_map/ppermute | solution.py:369
  28.0 0.4 collective-permute-start.4
  28.3 2.4 %collective-permute-start.5 = (bf16[256,2048]{1,0:T(8,128)(2,1)S(1)}, bf16[256,2048]{1,0:T(8,128)(2,1)}, u32[]{:S(2)}, u32[]{:S(2)}) collective-permute-start(bf16[256,2048]{1,0:T(8,128)(2,1)S(1)} %copy-done.2), channel_id=1, source_target_pairs={{0,24},{8,0},{16,8},{24,16},{1,25},{9,1},{17,9},{25,17},{2,26},{10... | collective-permute-start | bytes 3145736 | tf_op jit(solution)/shard_map/ppermute | solution.py:369
  30.7 2.7 %dynamic-slice_convert_fusion.refs_4_ = bf16[2048,256]{1,0:T(8,128)(2,1)} fusion(f32[8192,256]{1,0:T(8,128)} %basis_ref.3, s32[]{:T(128)S(6)} %select_n.46), kind=kLoop, calls=%fused_computation | loop fusion | bytes 2097156 | tf_op jit(solution)/shard_map/convert_element_type | solution.py:386
  33.4 2.3 %add_convert_fusion = bf16[16,64,256]{2,1,0:T(8,128)(2,1)} fusion(f32[16,64,256]{2,1,0:T(8,128)} %copy-done.8, bf16[16,64,256]{2,1,0:T(8,128)(2,1)} %collective-permute-done), kind=kLoop, calls=%fused_computation.1 | loop fusion | flops 786432 | bytes 2097152 | tf_op jit(solution)/shard_map/convert_element_type | solution.py:387
  35.7 15.2 %collective-permute-done.2.first_ref.refs_1_ = bf16[512,1024]{1,0:T(8,128)(2,1)S(1)} collective-permute-done((bf16[512,1024]{1,0:T(8,128)(2,1)}, bf16[512,1024]{1,0:T(8,128)(2,1)S(1)}, u32[]{:S(2)}, u32[]{:S(2)}) %collective-permute-start.2) | collective-permute-done | bytes 1048608 | tf_op jit(solution)/shard_map/ppermute | solution.py:369
  51.0 1.9 %collective-permute-done.4.first_ref.refs_6_ = bf16[256,2048]{1,0:T(8,128)(2,1)} collective-permute-done((bf16[256,2048]{1,0:T(8,128)(2,1)S(1)}, bf16[256,2048]{1,0:T(8,128)(2,1)}, u32[]{:S(2)}, u32[]{:S(2)}) %collective-permute-start.4) | collective-permute-done | bytes 1048608 | tf_op jit(solution)/shard_map/ppermute | solution.py:369
  52.9 1.3 halves.2
  54.2 2.7 %collective-permute-start.7 = (bf16[128,2048]{1,0:T(8,128)(2,1)S(1)}, bf16[128,2048]{1,0:T(8,128)(2,1)S(1)}, u32[]{:S(2)}, u32[]{:S(2)}) collective-permute-start(bf16[128,2048]{1,0:T(8,128)(2,1)S(1)} %get-tuple-element.74), channel_id=1, source_target_pairs={{0,24},{8,0},{16,8},{24,16},{1,25},{9,1},{17,9},{25,17},{2,26},{10... | collective-permute-start | bytes 1572872 | tf_op jit(solution)/shard_map/ppermute | solution.py:369
  57.1 2.6 %collective-permute-start.9 = (bf16[256,1024]{1,0:T(8,128)(2,1)S(1)}, bf16[256,1024]{1,0:T(8,128)(2,1)S(1)}, u32[]{:S(2)}, u32[]{:S(2)}) collective-permute-start(bf16[256,1024]{1,0:T(8,128)(2,1)S(1)} %get-tuple-element.76), channel_id=1, source_target_pairs={{0,96},{32,0},{64,32},{96,64},{1,97},{33,1},{65,33},{97,65},{2,98}... | collective-permute-start | bytes 1572872 | tf_op jit(solution)/shard_map/ppermute | solution.py:369
  59.7 7.2 %collective-permute-done.6.refs_8_ = bf16[128,2048]{1,0:T(8,128)(2,1)} collective-permute-done((bf16[128,2048]{1,0:T(8,128)(2,1)S(1)}, bf16[128,2048]{1,0:T(8,128)(2,1)}, u32[]{:S(2)}, u32[]{:S(2)}) %collective-permute-start.6) | collective-permute-done | bytes 524320 | tf_op jit(solution)/shard_map/ppermute | solution.py:369
  66.9 2.3 %collective-permute-done.8.refs_3_ = bf16[256,1024]{1,0:T(8,128)(2,1)S(1)} collective-permute-done((bf16[256,1024]{1,0:T(8,128)(2,1)S(1)}, bf16[256,1024]{1,0:T(8,128)(2,1)S(1)}, u32[]{:S(2)}, u32[]{:S(2)}) %collective-permute-start.8) | collective-permute-done | bytes 524320 | tf_op jit(solution)/shard_map/ppermute | solution.py:369
  69.2 3.5 %collective-permute-start.10 = (bf16[256,2048]{1,0:T(8,128)(2,1)}, bf16[256,2048]{1,0:T(8,128)(2,1)S(1)}, u32[]{:S(2)}, u32[]{:S(2)}) collective-permute-start(bf16[256,2048]{1,0:T(8,128)(2,1)} %collective-permute-done.4.first_ref.refs_6_), channel_id=1, source_target_pairs={{0,4},{4,0},{1,5},{5,1},{2,6},{6,2},{3,7},{7,3},{8,12},{12,8},{9,1... | collective-permute-start | bytes 3145736 | tf_op jit(solution)/shard_map/ppermute | solution.py:365
  72.8 0.4 collective-permute-start.12
  73.3 9.1 %parts.2 = (bf16[4,256,256]{2,1,0:T(8,128)(2,1)}, bf16[4,256,256]{2,1,0:T(8,128)(2,1)}, bf16[4,256,256]{2,1,0:T(8,128)(2,1)}, bf16[4,256,256]{2,1,0:T(8,128)(2,1)}) custom-call(s32[12]{0:T(128)} %stack.51.place_ref.refs_0_, bf16[512,1024]{1,0:T(8,128)(2,1)} %bitcast.15.refs_0_, bf16[512,1024]{1,0:T(8,128)(2,1)} %copy-done, bf16[512,1024]{1,0:T(8,128)(2,1)} %copy-done.1, ...), custom_call_target="tpu_custom_call" | custom-call | tf_op jit(solution)/shard_map/parts/pallas_call | solution.py:184
  82.4 2.8 %collective-permute-start.14 = (bf16[4,256,256]{2,1,0:T(8,128)(2,1)}, bf16[4,256,256]{2,1,0:T(8,128)(2,1)S(1)}, u32[]{:S(2)}, u32[]{:S(2)}) collective-permute-start(bf16[4,256,256]{2,1,0:T(8,128)(2,1)} %get-tuple-element.90), channel_id=1, source_target_pairs={{0,3},{1,0},{2,1},{3,2},{4,7},{5,4},{6,5},{7,6},{8,11},{9,8},{10,9... | collective-permute-start | bytes 1572872 | tf_op jit(solution)/shard_map/ppermute | solution.py:369
  85.2 0.9 copy-done.16
  86.1 1.0 copy-done.14
  87.1 9.1 %parts.3 = (bf16[4,256,256]{2,1,0:T(8,128)(2,1)}, bf16[4,256,256]{2,1,0:T(8,128)(2,1)}, bf16[4,256,256]{2,1,0:T(8,128)(2,1)}, bf16[4,256,256]{2,1,0:T(8,128)(2,1)}) custom-call(s32[12]{0:T(128)} %stack.51.place_ref.refs_0_, bf16[512,1024]{1,0:T(8,128)(2,1)} %bitcast.15.refs_0_, bf16[512,1024]{1,0:T(8,128)(2,1)} %copy-done, bf16[512,1024]{1,0:T(8,128)(2,1)} %copy-done.1, ...), custom_call_target="tpu_custom_call" | custom-call | tf_op jit(solution)/shard_map/parts/pallas_call | solution.py:184
  96.2 2.7 %collective-permute-start.16 = (bf16[4,256,256]{2,1,0:T(8,128)(2,1)}, bf16[4,256,256]{2,1,0:T(8,128)(2,1)}, u32[]{:S(2)}, u32[]{:S(2)}) collective-permute-start(bf16[4,256,256]{2,1,0:T(8,128)(2,1)} %get-tuple-element.87), channel_id=1, source_target_pairs={{0,3},{1,0},{2,1},{3,2},{4,7},{5,4},{6,5},{7,6},{8,11},{9,8},{10,9... | collective-permute-start | bytes 1572872 | tf_op jit(solution)/shard_map/ppermute | solution.py:369
  98.9 4.8 %all-to-all-start.1 = ((bf16[16,64,256]{2,1,0:T(8,128)(2,1)}), bf16[16,64,256]{2,1,0:T(8,128)(2,1)S(1)}, u32[]{:S(2)}, u32[]{:S(2)}) async-start(bf16[16,64,256]{2,1,0:T(8,128)(2,1)} %add_convert_fusion), calls=%async_computation.1 | async-start | bytes 1048576 | tf_op jit(solution)/shard_map/all_to_all | solution.py:403
  103.8 5.6 %collective-permute-done.16.refs_3_ = bf16[4,256,256]{2,1,0:T(8,128)(2,1)} collective-permute-done((bf16[4,256,256]{2,1,0:T(8,128)(2,1)}, bf16[4,256,256]{2,1,0:T(8,128)(2,1)}, u32[]{:S(2)}, u32[]{:S(2)}) %collective-permute-start.16) | collective-permute-done | bytes 524320 | tf_op jit(solution)/shard_map/ppermute | solution.py:369
  109.5 2.4 %sums.3 = (bf16[4,256,256]{2,1,0:T(8,128)(2,1)}, bf16[4,256,256]{2,1,0:T(8,128)(2,1)}) custom-call(bf16[4,256,256]{2,1,0:T(8,128)(2,1)} %get-tuple-element.91.refs_0_, bf16[4,256,256]{2,1,0:T(8,128)(2,1)} %collective-permute-done.15.refs_1_, bf16[4,256,256]{2,1,0:T(8,128)(2,1)} %get-tuple-element.93.refs_2_, bf16[4,256,256]{2,1,0:T(8,128)(2,1)} %collective-permute-done.16.refs_3_), custom_call_target="tpu_custom_call" | custom-call | tf_op jit(solution)/shard_map/sums/pallas_call | solution.py:230
  112.0 3.5 %collective-permute-start.19 = (bf16[4,256,256]{2,1,0:T(8,128)(2,1)}, bf16[4,256,256]{2,1,0:T(8,128)(2,1)}, u32[]{:S(2)}, u32[]{:S(2)}) collective-permute-start(bf16[4,256,256]{2,1,0:T(8,128)(2,1)} %get-tuple-element.103), channel_id=1, source_target_pairs={{0,3},{1,0},{2,1},{3,2},{4,7},{5,4},{6,5},{7,6},{8,11},{9,8},{10,9... | collective-permute-start | bytes 1572872 | tf_op jit(solution)/shard_map/ppermute | solution.py:369
  115.5 1.0 optimizer_step.1
  116.5 4.7 %all-to-all-start.2 = ((bf16[16,64,256]{2,1,0:T(8,128)(2,1)}), bf16[16,64,256]{2,1,0:T(8,128)(2,1)S(1)}, u32[]{:S(2)}, u32[]{:S(2)}) async-start(bf16[16,64,256]{2,1,0:T(8,128)(2,1)} %get-tuple-element.104), calls=%async_computation.2 | async-start | bytes 1048576 | tf_op jit(solution)/shard_map/all_to_all | solution.py:409
  121.3 2.4 %sums.4 = (bf16[4,256,256]{2,1,0:T(8,128)(2,1)}, bf16[4,256,256]{2,1,0:T(8,128)(2,1)}) custom-call(bf16[4,256,256]{2,1,0:T(8,128)(2,1)} %get-tuple-element.97.refs_0_, bf16[4,256,256]{2,1,0:T(8,128)(2,1)} %copy-done.17, bf16[4,256,256]{2,1,0:T(8,128)(2,1)} %get-tuple-element.99.refs_2_, bf16[4,256,256]{2,1,0:T(8,128)(2,1)} %collective-permute-done.17.refs_3_), custom_call_target="tpu_custom_call" | custom-call | tf_op jit(solution)/shard_map/sums/pallas_call | solution.py:230
  123.7 4.7 %collective-permute-done.18.refs_2_ = bf16[4,256,256]{2,1,0:T(8,128)(2,1)} collective-permute-done((bf16[4,256,256]{2,1,0:T(8,128)(2,1)}, bf16[4,256,256]{2,1,0:T(8,128)(2,1)}, u32[]{:S(2)}, u32[]{:S(2)}) %collective-permute-start.18) | collective-permute-done | bytes 524320 | tf_op jit(solution)/shard_map/ppermute | solution.py:369
  128.4 3.1 %sums.5 = bf16[8,256,256]{2,1,0:T(8,128)(2,1)} custom-call(s32[12]{0:T(128)} %stack.51.place_ref.refs_0_, bf16[4,256,256]{2,1,0:T(8,128)(2,1)} %get-tuple-element.101.refs_1_, bf16[4,256,256]{2,1,0:T(8,128)(2,1)} %collective-permute-done.18.refs_2_, bf16[4,256,256]{2,1,0:T(8,128)(2,1)} %get-tuple-element.102.refs_3_, ...), custom_call_target="tpu_custom_call" | custom-call | tf_op jit(solution)/shard_map/sums/pallas_call | solution.py:230
  131.5 0.8 copy-done.6
  132.3 7.0 %all-to-all-start.3 = ((bf16[8,256,256]{2,1,0:T(8,128)(2,1)}), bf16[8,256,256]{2,1,0:T(8,128)(2,1)S(1)}, u32[]{:S(2)}, u32[]{:S(2)}) async-start(bf16[8,256,256]{2,1,0:T(8,128)(2,1)} %sums.5), calls=%async_computation.3 | async-start | bytes 2097152 | tf_op jit(solution)/shard_map/all_to_all | solution.py:419
  139.3 2.0 %collective-permute-done.20.other_ref = bf16[16,64,256]{2,1,0:T(8,128)(2,1)S(1)} collective-permute-done((bf16[16,64,256]{2,1,0:T(8,128)(2,1)}, bf16[16,64,256]{2,1,0:T(8,128)(2,1)S(1)}, u32[]{:S(2)}, u32[]{:S(2)}) %collective-permute-start.20) | collective-permute-done | bytes 524320 | tf_op jit(solution)/shard_map/ppermute | solution.py:365
  141.4 1.0 copy-done.7
  142.4 0.5 inner.1
  143.0 2.7 %collective-permute-start.22 = (bf16[256,256]{1,0:T(8,128)(2,1)S(1)}, bf16[256,256]{1,0:T(8,128)(2,1)S(1)}, u32[]{:S(2)}, u32[]{:S(2)}) collective-permute-start(bf16[256,256]{1,0:T(8,128)(2,1)S(1)} %convert_element_type.15.refs_0_), channel_id=1, source_target_pairs={{0,3},{1,0},{2,1},{3,2},{4,7},{5,4},{6,5},{7,6},{8,11},{9,8},{10,9... | collective-permute-start | bytes 393224 | tf_op jit(solution)/shard_map/ppermute | solution.py:369
  145.7 5.8 %fresh_rows.1 = bf16[64,8192]{1,0:T(8,128)(2,1)} custom-call(f32[64,256]{1,0:T(8,128)S(1)} %get-tuple-element.109.direction_ref, f32[8192,256]{1,0:T(8,128)} %basis_ref.3, bf16[64,8192]{1,0:T(8,128)(2,1)S(1)} %bitcast.22), custom_call_target="tpu_custom_call" | custom-call | tf_op jit(solution)/shard_map/fresh_rows/pallas_call | solution.py:128
  151.5 1.1 change.1.change_ref
  152.6 1.8 %all-to-all-done.3.part_ref = bf16[8,256,256]{2,1,0:T(8,128)(2,1)S(1)} async-done(((bf16[8,256,256]{2,1,0:T(8,128)(2,1)}), bf16[8,256,256]{2,1,0:T(8,128)(2,1)S(1)}, u32[]{:S(2)}, u32[]{:S(2)}) %all-to-all-start.3) | async-done | bytes 1048608 | tf_op jit(solution)/shard_map/all_to_all | solution.py:419
  154.4 1.2 output_rows.1
  (62 shorter events, 0.9 us)
Async XLA Ops:
  0.6 27.4 %collective-permute-start.1 = (bf16[256,2048]{1,0:T(8,128)(2,1)}, bf16[256,2048]{1,0:T(8,128)(2,1)}, u32[]{:S(2)}, u32[]{:S(2)}) collective-permute-start(bf16[256,2048]{1,0:T(8,128)(2,1)} %acts_ref.3), channel_id=1, source_target_pairs={{0,4},{4,0},{1,5},{5,1},{2,6},{6,2},{3,7},{7,3},{8,12},{12,8},{9,1... | collective-permute-start | bytes 3145736 | tf_op jit(solution)/shard_map/ppermute | solution.py:365
  4.4 23.6 %copy-start.2 = (bf16[256,2048]{1,0:T(8,128)(2,1)S(1)}, bf16[256,2048]{1,0:T(8,128)(2,1)}, u32[]{:S(2)}) copy-start(bf16[256,2048]{1,0:T(8,128)(2,1)} %acts_ref.3) | copy-start | bytes 3145732
  4.4 19.8 %all-to-all-start = ((bf16[8,64,1024]{2,1,0:T(8,128)(2,1)}), bf16[8,64,1024]{2,1,0:T(8,128)(2,1)}, u32[]{:S(2)}, u32[]{:S(2)}) async-start(bf16[8,64,1024]{2,1,0:T(8,128)(2,1)} %exchange_order.1), calls=%async_computation | async-start | bytes 2097152 | tf_op jit(solution)/shard_map/all_to_all | solution.py:377
  9.0 1.2 copy-start.9
  20.1 1.0 copy-start.8
  21.0 6.9 %collective-permute-start = (bf16[16,64,256]{2,1,0:T(8,128)(2,1)}, bf16[16,64,256]{2,1,0:T(8,128)(2,1)}, u32[]{:S(2)}, u32[]{:S(2)}) collective-permute-start(bf16[16,64,256]{2,1,0:T(8,128)(2,1)} %get-tuple-element.59), channel_id=1, source_target_pairs={{0,4},{4,0},{1,5},{5,1},{2,6},{6,2},{3,7},{7,3},{8,12},{12,8},{9,1... | collective-permute-start | bytes 1572872 | tf_op jit(solution)/shard_map/ppermute | solution.py:365
  24.2 26.7 %collective-permute-start.2 = (bf16[512,1024]{1,0:T(8,128)(2,1)}, bf16[512,1024]{1,0:T(8,128)(2,1)S(1)}, u32[]{:S(2)}, u32[]{:S(2)}) collective-permute-start(bf16[512,1024]{1,0:T(8,128)(2,1)} %bitcast.15.refs_0_), channel_id=1, source_target_pairs={{0,32},{32,64},{64,96},{96,0},{1,33},{33,65},{65,97},{97,1},{2,34}... | collective-permute-start | bytes 3145736 | tf_op jit(solution)/shard_map/ppermute | solution.py:369
  25.9 25.1 %collective-permute-start.3 = (bf16[512,1024]{1,0:T(8,128)(2,1)}, bf16[512,1024]{1,0:T(8,128)(2,1)S(1)}, u32[]{:S(2)}, u32[]{:S(2)}) collective-permute-start(bf16[512,1024]{1,0:T(8,128)(2,1)} %bitcast.15.refs_0_), channel_id=1, source_target_pairs={{0,96},{32,0},{64,32},{96,64},{1,97},{33,1},{65,33},{97,65},{2,98}... | collective-permute-start | bytes 3145736 | tf_op jit(solution)/shard_map/ppermute | solution.py:369
  28.0 24.9 %collective-permute-start.4 = (bf16[256,2048]{1,0:T(8,128)(2,1)S(1)}, bf16[256,2048]{1,0:T(8,128)(2,1)}, u32[]{:S(2)}, u32[]{:S(2)}) collective-permute-start(bf16[256,2048]{1,0:T(8,128)(2,1)S(1)} %copy-done.2), channel_id=1, source_target_pairs={{0,8},{8,16},{16,24},{24,0},{1,9},{9,17},{17,25},{25,1},{2,10},{10... | collective-permute-start | bytes 3145736 | tf_op jit(solution)/shard_map/ppermute | solution.py:369
  28.3 24.5 %collective-permute-start.5 = (bf16[256,2048]{1,0:T(8,128)(2,1)S(1)}, bf16[256,2048]{1,0:T(8,128)(2,1)}, u32[]{:S(2)}, u32[]{:S(2)}) collective-permute-start(bf16[256,2048]{1,0:T(8,128)(2,1)S(1)} %copy-done.2), channel_id=1, source_target_pairs={{0,24},{8,0},{16,8},{24,16},{1,25},{9,1},{17,9},{25,17},{2,26},{10... | collective-permute-start | bytes 3145736 | tf_op jit(solution)/shard_map/ppermute | solution.py:369
  51.0 22.3 %copy-start = (bf16[512,1024]{1,0:T(8,128)(2,1)}, bf16[512,1024]{1,0:T(8,128)(2,1)S(1)}, u32[]{:S(2)}) copy-start(bf16[512,1024]{1,0:T(8,128)(2,1)S(1)} %collective-permute-done.2.first_ref.refs_1_) | copy-start | bytes 3145732
  51.0 22.3 %copy-start.1 = (bf16[512,1024]{1,0:T(8,128)(2,1)}, bf16[512,1024]{1,0:T(8,128)(2,1)S(1)}, u32[]{:S(2)}) copy-start(bf16[512,1024]{1,0:T(8,128)(2,1)S(1)} %collective-permute-done.3.last_ref.refs_2_) | copy-start | bytes 3145732
  54.2 12.7 %collective-permute-start.6 = (bf16[128,2048]{1,0:T(8,128)(2,1)S(1)}, bf16[128,2048]{1,0:T(8,128)(2,1)}, u32[]{:S(2)}, u32[]{:S(2)}) collective-permute-start(bf16[128,2048]{1,0:T(8,128)(2,1)S(1)} %get-tuple-element.73), channel_id=1, source_target_pairs={{0,8},{8,16},{16,24},{24,0},{1,9},{9,17},{17,25},{25,1},{2,10},{10... | collective-permute-start | bytes 1572872 | tf_op jit(solution)/shard_map/ppermute | solution.py:369
  54.2 12.6 %collective-permute-start.7 = (bf16[128,2048]{1,0:T(8,128)(2,1)S(1)}, bf16[128,2048]{1,0:T(8,128)(2,1)S(1)}, u32[]{:S(2)}, u32[]{:S(2)}) collective-permute-start(bf16[128,2048]{1,0:T(8,128)(2,1)S(1)} %get-tuple-element.74), channel_id=1, source_target_pairs={{0,24},{8,0},{16,8},{24,16},{1,25},{9,1},{17,9},{25,17},{2,26},{10... | collective-permute-start | bytes 1572872 | tf_op jit(solution)/shard_map/ppermute | solution.py:369
  57.0 12.2 %collective-permute-start.8 = (bf16[256,1024]{1,0:T(8,128)(2,1)S(1)}, bf16[256,1024]{1,0:T(8,128)(2,1)S(1)}, u32[]{:S(2)}, u32[]{:S(2)}) collective-permute-start(bf16[256,1024]{1,0:T(8,128)(2,1)S(1)} %get-tuple-element.75), channel_id=1, source_target_pairs={{0,32},{32,64},{64,96},{96,0},{1,33},{33,65},{65,97},{97,1},{2,34}... | collective-permute-start | bytes 1572872 | tf_op jit(solution)/shard_map/ppermute | solution.py:369
  57.1 58.4 %copy-start.10 = (f32[1,64,256]{2,1,0:T(8,128)S(1)}, f32[1,64,256]{2,1,0:T(8,128)}, u32[]{:S(2)}) copy-start(f32[1,64,256]{2,1,0:T(8,128)} %param.10) | copy-start | bytes 196612
  57.1 58.4 %copy-start.11 = (f32[1,64,256]{2,1,0:T(8,128)S(1)}, f32[1,64,256]{2,1,0:T(8,128)}, u32[]{:S(2)}) copy-start(f32[1,64,256]{2,1,0:T(8,128)} %param.11) | copy-start | bytes 196612
  57.1 12.1 %collective-permute-start.9 = (bf16[256,1024]{1,0:T(8,128)(2,1)S(1)}, bf16[256,1024]{1,0:T(8,128)(2,1)S(1)}, u32[]{:S(2)}, u32[]{:S(2)}) collective-permute-start(bf16[256,1024]{1,0:T(8,128)(2,1)S(1)} %get-tuple-element.76), channel_id=1, source_target_pairs={{0,96},{32,0},{64,32},{96,64},{1,97},{33,1},{65,33},{97,65},{2,98}... | collective-permute-start | bytes 1572872 | tf_op jit(solution)/shard_map/ppermute | solution.py:369
  66.9 6.4 %copy-start.15 = (bf16[128,2048]{1,0:T(8,128)(2,1)}, bf16[128,2048]{1,0:T(8,128)(2,1)S(1)}, u32[]{:S(2)}) copy-start(bf16[128,2048]{1,0:T(8,128)(2,1)S(1)} %collective-permute-done.7.refs_9_) | copy-start | bytes 1572868
  69.1 4.1 %copy-start.12 = (bf16[256,1024]{1,0:T(8,128)(2,1)}, bf16[256,1024]{1,0:T(8,128)(2,1)S(1)}, u32[]{:S(2)}) copy-start(bf16[256,1024]{1,0:T(8,128)(2,1)S(1)} %collective-permute-done.8.refs_3_) | copy-start | bytes 1572868
  69.1 4.1 %copy-start.13 = (bf16[256,1024]{1,0:T(8,128)(2,1)}, bf16[256,1024]{1,0:T(8,128)(2,1)S(1)}, u32[]{:S(2)}) copy-start(bf16[256,1024]{1,0:T(8,128)(2,1)S(1)} %collective-permute-done.9.refs_4_) | copy-start | bytes 1572868
  69.2 16.9 %collective-permute-start.10 = (bf16[256,2048]{1,0:T(8,128)(2,1)}, bf16[256,2048]{1,0:T(8,128)(2,1)S(1)}, u32[]{:S(2)}, u32[]{:S(2)}) collective-permute-start(bf16[256,2048]{1,0:T(8,128)(2,1)} %collective-permute-done.4.first_ref.refs_6_), channel_id=1, source_target_pairs={{0,4},{4,0},{1,5},{5,1},{2,6},{6,2},{3,7},{7,3},{8,12},{12,8},{9,1... | collective-permute-start | bytes 3145736 | tf_op jit(solution)/shard_map/ppermute | solution.py:365
  72.7 13.4 %collective-permute-start.11 = (bf16[256,2048]{1,0:T(8,128)(2,1)}, bf16[256,2048]{1,0:T(8,128)(2,1)}, u32[]{:S(2)}, u32[]{:S(2)}) collective-permute-start(bf16[256,2048]{1,0:T(8,128)(2,1)} %collective-permute-done.5.last_ref.refs_7_), channel_id=1, source_target_pairs={{0,4},{4,0},{1,5},{5,1},{2,6},{6,2},{3,7},{7,3},{8,12},{12,8},{9,1... | collective-permute-start | bytes 3145736 | tf_op jit(solution)/shard_map/ppermute | solution.py:365
  72.8 12.4 %collective-permute-start.12 = (bf16[128,2048]{1,0:T(8,128)(2,1)}, bf16[128,2048]{1,0:T(8,128)(2,1)S(1)}, u32[]{:S(2)}, u32[]{:S(2)}) collective-permute-start(bf16[128,2048]{1,0:T(8,128)(2,1)} %collective-permute-done.6.refs_8_), channel_id=1, source_target_pairs={{0,4},{4,0},{1,5},{5,1},{2,6},{6,2},{3,7},{7,3},{8,12},{12,8},{9,1... | collective-permute-start | bytes 1572872 | tf_op jit(solution)/shard_map/ppermute | solution.py:365
  73.2 12.9 %collective-permute-start.13 = (bf16[128,2048]{1,0:T(8,128)(2,1)S(1)}, bf16[128,2048]{1,0:T(8,128)(2,1)}, u32[]{:S(2)}, u32[]{:S(2)}) collective-permute-start(bf16[128,2048]{1,0:T(8,128)(2,1)S(1)} %collective-permute-done.7.refs_9_), channel_id=1, source_target_pairs={{0,4},{4,0},{1,5},{5,1},{2,6},{6,2},{3,7},{7,3},{8,12},{12,8},{9,1... | collective-permute-start | bytes 1572872 | tf_op jit(solution)/shard_map/ppermute | solution.py:365
  82.4 21.3 %collective-permute-start.14 = (bf16[4,256,256]{2,1,0:T(8,128)(2,1)}, bf16[4,256,256]{2,1,0:T(8,128)(2,1)S(1)}, u32[]{:S(2)}, u32[]{:S(2)}) collective-permute-start(bf16[4,256,256]{2,1,0:T(8,128)(2,1)} %get-tuple-element.90), channel_id=1, source_target_pairs={{0,3},{1,0},{2,1},{3,2},{4,7},{5,4},{6,5},{7,6},{8,11},{9,8},{10,9... | collective-permute-start | bytes 1572872 | tf_op jit(solution)/shard_map/ppermute | solution.py:369
  85.2 0.9 copy-start.16
  86.1 55.3 %copy-start.3 = (bf16[256,2048]{1,0:T(8,128)(2,1)S(1)}, bf16[256,2048]{1,0:T(8,128)(2,1)}, u32[]{:S(2)}) copy-start(bf16[256,2048]{1,0:T(8,128)(2,1)} %acts_ref.3) | copy-start | bytes 3145732
  86.1 17.8 %collective-permute-start.15 = (bf16[4,256,256]{2,1,0:T(8,128)(2,1)}, bf16[4,256,256]{2,1,0:T(8,128)(2,1)}, u32[]{:S(2)}, u32[]{:S(2)}) collective-permute-start(bf16[4,256,256]{2,1,0:T(8,128)(2,1)} %get-tuple-element.92), channel_id=1, source_target_pairs={{0,1},{1,2},{2,3},{3,0},{4,5},{5,6},{6,7},{7,4},{8,9},{9,10},{10,1... | collective-permute-start | bytes 1572872 | tf_op jit(solution)/shard_map/ppermute | solution.py:369
  86.1 1.0 copy-start.14
  96.2 49.5 %copy-start.4 = (bf16[1,64,8192]{2,1,0:T(8,128)(2,1)S(1)}, bf16[1,64,8192]{2,1,0:T(8,128)(2,1)}, u32[]{:S(2)}) copy-start(bf16[1,64,8192]{2,1,0:T(8,128)(2,1)} %param.12) | copy-start | bytes 3145732
  96.2 13.3 %collective-permute-start.16 = (bf16[4,256,256]{2,1,0:T(8,128)(2,1)}, bf16[4,256,256]{2,1,0:T(8,128)(2,1)}, u32[]{:S(2)}, u32[]{:S(2)}) collective-permute-start(bf16[4,256,256]{2,1,0:T(8,128)(2,1)} %get-tuple-element.87), channel_id=1, source_target_pairs={{0,3},{1,0},{2,1},{3,2},{4,7},{5,4},{6,5},{7,6},{8,11},{9,8},{10,9... | collective-permute-start | bytes 1572872 | tf_op jit(solution)/shard_map/ppermute | solution.py:369
  98.9 16.6 %all-to-all-start.1 = ((bf16[16,64,256]{2,1,0:T(8,128)(2,1)}), bf16[16,64,256]{2,1,0:T(8,128)(2,1)S(1)}, u32[]{:S(2)}, u32[]{:S(2)}) async-start(bf16[16,64,256]{2,1,0:T(8,128)(2,1)} %add_convert_fusion), calls=%async_computation.1 | async-start | bytes 1048576 | tf_op jit(solution)/shard_map/all_to_all | solution.py:403
  103.7 17.5 %copy-start.17 = (bf16[4,256,256]{2,1,0:T(8,128)(2,1)}, bf16[4,256,256]{2,1,0:T(8,128)(2,1)S(1)}, u32[]{:S(2)}) copy-start(bf16[4,256,256]{2,1,0:T(8,128)(2,1)S(1)} %collective-permute-done.14.refs_1_) | copy-start | bytes 1572868
  103.8 17.5 %collective-permute-start.17 = (bf16[4,256,256]{2,1,0:T(8,128)(2,1)}, bf16[4,256,256]{2,1,0:T(8,128)(2,1)}, u32[]{:S(2)}, u32[]{:S(2)}) collective-permute-start(bf16[4,256,256]{2,1,0:T(8,128)(2,1)} %get-tuple-element.100), channel_id=1, source_target_pairs={{0,1},{1,2},{2,3},{3,0},{4,5},{5,6},{6,7},{7,4},{8,9},{9,10},{10,1... | collective-permute-start | bytes 1572872 | tf_op jit(solution)/shard_map/ppermute | solution.py:369
  111.9 16.5 %collective-permute-start.18 = (bf16[4,256,256]{2,1,0:T(8,128)(2,1)}, bf16[4,256,256]{2,1,0:T(8,128)(2,1)}, u32[]{:S(2)}, u32[]{:S(2)}) collective-permute-start(bf16[4,256,256]{2,1,0:T(8,128)(2,1)} %get-tuple-element.94), channel_id=1, source_target_pairs={{0,1},{1,2},{2,3},{3,0},{4,5},{5,6},{6,7},{7,4},{8,9},{9,10},{10,1... | collective-permute-start | bytes 1572872 | tf_op jit(solution)/shard_map/ppermute | solution.py:369
  112.0 16.4 %collective-permute-start.19 = (bf16[4,256,256]{2,1,0:T(8,128)(2,1)}, bf16[4,256,256]{2,1,0:T(8,128)(2,1)}, u32[]{:S(2)}, u32[]{:S(2)}) collective-permute-start(bf16[4,256,256]{2,1,0:T(8,128)(2,1)} %get-tuple-element.103), channel_id=1, source_target_pairs={{0,3},{1,0},{2,1},{3,2},{4,7},{5,4},{6,5},{7,6},{8,11},{9,8},{10,9... | collective-permute-start | bytes 1572872 | tf_op jit(solution)/shard_map/ppermute | solution.py:369
  116.5 15.0 %all-to-all-start.2 = ((bf16[16,64,256]{2,1,0:T(8,128)(2,1)}), bf16[16,64,256]{2,1,0:T(8,128)(2,1)S(1)}, u32[]{:S(2)}, u32[]{:S(2)}) async-start(bf16[16,64,256]{2,1,0:T(8,128)(2,1)} %get-tuple-element.104), calls=%async_computation.2 | async-start | bytes 1048576 | tf_op jit(solution)/shard_map/all_to_all | solution.py:409
  131.5 0.8 copy-start.6
  132.3 22.1 %all-to-all-start.3 = ((bf16[8,256,256]{2,1,0:T(8,128)(2,1)}), bf16[8,256,256]{2,1,0:T(8,128)(2,1)S(1)}, u32[]{:S(2)}, u32[]{:S(2)}) async-start(bf16[8,256,256]{2,1,0:T(8,128)(2,1)} %sums.5), calls=%async_computation.3 | async-start | bytes 2097152 | tf_op jit(solution)/shard_map/all_to_all | solution.py:419
  139.3 12.3 %copy-start.5 = (bf16[2048,256]{1,0:T(8,128)(2,1)S(1)}, bf16[2048,256]{1,0:T(8,128)(2,1)}, u32[]{:S(2)}) copy-start(bf16[2048,256]{1,0:T(8,128)(2,1)} %dynamic-slice_convert_fusion.refs_4_) | copy-start | bytes 3145732
  139.3 2.1 %collective-permute-start.20 = (bf16[16,64,256]{2,1,0:T(8,128)(2,1)}, bf16[16,64,256]{2,1,0:T(8,128)(2,1)S(1)}, u32[]{:S(2)}, u32[]{:S(2)}) collective-permute-start(bf16[16,64,256]{2,1,0:T(8,128)(2,1)} %copy-done.6), channel_id=1, source_target_pairs={{0,4},{4,0},{1,5},{5,1},{2,6},{6,2},{3,7},{7,3},{8,12},{12,8},{9,1... | collective-permute-start | bytes 1572872 | tf_op jit(solution)/shard_map/ppermute | solution.py:365
  141.4 1.0 copy-start.7
  143.0 8.6 %collective-permute-start.21 = (bf16[256,256]{1,0:T(8,128)(2,1)S(1)}, bf16[256,256]{1,0:T(8,128)(2,1)S(1)}, u32[]{:S(2)}, u32[]{:S(2)}) collective-permute-start(bf16[256,256]{1,0:T(8,128)(2,1)S(1)} %convert_element_type.15.refs_0_), channel_id=1, source_target_pairs={{0,1},{1,2},{2,3},{3,0},{4,5},{5,6},{6,7},{7,4},{8,9},{9,10},{10,1... | collective-permute-start | bytes 393224 | tf_op jit(solution)/shard_map/ppermute | solution.py:369
  143.0 8.5 %collective-permute-start.22 = (bf16[256,256]{1,0:T(8,128)(2,1)S(1)}, bf16[256,256]{1,0:T(8,128)(2,1)S(1)}, u32[]{:S(2)}, u32[]{:S(2)}) collective-permute-start(bf16[256,256]{1,0:T(8,128)(2,1)S(1)} %convert_element_type.15.refs_0_), channel_id=1, source_target_pairs={{0,3},{1,0},{2,1},{3,2},{4,7},{5,4},{6,5},{7,6},{8,11},{9,8},{10,9... | collective-permute-start | bytes 393224 | tf_op jit(solution)/shard_map/ppermute | solution.py:369
  145.7 5.8 %collective-permute-start.23 = (bf16[256,256]{1,0:T(8,128)(2,1)S(1)}, bf16[256,256]{1,0:T(8,128)(2,1)S(1)}, u32[]{:S(2)}, u32[]{:S(2)}) collective-permute-start(bf16[256,256]{1,0:T(8,128)(2,1)S(1)} %convert_element_type.15.refs_0_), channel_id=1, source_target_pairs={{0,2},{1,3},{2,0},{3,1},{4,6},{5,7},{6,4},{7,5},{8,10},{9,11},{10,... | collective-permute-start | bytes 393224 | tf_op jit(solution)/shard_map/ppermute | solution.py:369
